TPU v7x, 32 devices: a whole 2x2x4 slice. The times are simulated.
32 devices in a mesh: batch: 4 (over y, core), ctx: 8 (over z, x).
Axes of the slice: x: 2, y: 2, z: 4, core: 2. Of those that a mesh axis runs over, the one named last changes fastest.
Arguments:
- tokens: bfloat16 [4, 1024, 1024], P('batch', 'ctx'), may hold values from -6 to 6
- cotangent: bfloat16 [4, 1024, 1024], P('batch', 'ctx'), may hold values from -6 to 6
- ln1_gain: bfloat16 [1024], P('batch'), may hold values from 0.099609375 to 1.8984375
- ln1_bias: bfloat16 [1024], P('batch'), may hold values from -3 to 3
- qkv_weight: bfloat16 [1024, 3072], P('batch'), may hold values from -0.1875 to 0.1875
- qv_bias: bfloat16 [2048], P('batch'), may hold values from -3 to 3
- proj_weight: bfloat16 [1024, 1024], P('batch'), may hold values from -0.5 to 0.5
- proj_bias: bfloat16 [1024], P('batch'), may hold values from -3 to 3
- ln2_gain: bfloat16 [1024], P('batch'), may hold values from 0.099609375 to 1.8984375
- ln2_bias: bfloat16 [1024], P('batch'), may hold values from -3 to 3
- fc_weight: bfloat16 [1024, 4096], P('batch'), may hold values from -0.1875 to 0.1875
- fc_bias: bfloat16 [4096], P('batch'), may hold values from -3 to 3
- out_weight: bfloat16 [4096, 1024], P('batch'), may hold values from -0.125 to 0.125
- out_bias: bfloat16 [1024], P('batch'), may hold values from -3 to 3
Outputs:
- layer_out: bfloat16 [4, 1024, 1024], P('batch', 'ctx')
- grad_tokens: bfloat16 [4, 1024, 1024], P('batch', 'ctx')
- grad_ln1_gain: float32 [1024], P('batch')
- grad_ln1_bias: float32 [1024], P('batch')
- grad_qkv_weight: float32 [1024, 3072], P('batch')
- grad_qv_bias: float32 [2048], P('batch')
- grad_proj_weight: float32 [1024, 1024], P('batch')
- grad_proj_bias: float32 [1024], P('batch')
- grad_ln2_gain: float32 [1024], P('batch')
- grad_ln2_bias: float32 [1024], P('batch')
- grad_fc_weight: float32 [1024, 4096], P('batch')
- grad_fc_bias: float32 [4096], P('batch')
- grad_out_weight: float32 [4096, 1024], P('batch')
- grad_out_bias: float32 [1024], P('batch')
All inputs are finite; a program needn't handle non-finite values.
Results may differ from a plain program's by a relative error of at most 0.019.
Values may be sent and summed in bfloat16 or wider, within the bound.
A program may use at most 320 MiB of HBM per device.

v0:
```python
from functools import partial

import jax
import jax.numpy as jnp
from jax import lax
from jax.sharding import PartitionSpec as P

HEADS = 16
HEAD_DIM = 64


epsilon = 1e-05
masked_value = -1e30


def shifted(block, axis, distance):
    devices = range(lax.axis_size(axis))
    route = [(i - distance, i) for i in devices if i - distance in devices]
    return lax.ppermute(block, axis, route)


def from_behind(block, axis, distance):
    devices = range(lax.axis_size(axis))
    route = [((i - distance) % len(devices), i) for i in devices]
    return lax.ppermute(block, axis, route)


def layer_norm(inputs, gain_vec, bias_vec):
    centre = inputs - jnp.mean(inputs, -1, keepdims=True)
    spread = jnp.mean(centre * centre, -1, keepdims=True)
    return centre * lax.rsqrt(spread + epsilon) * gain_vec + bias_vec


def keep_same(running):
    return running


def per_device(
    tokens,
    cotangent,
    ln1_gain,
    ln1_bias,
    qkv_weight,
    qv_bias,
    proj_weight,
    proj_bias,
    ln2_gain,
    ln2_bias,
    fc_weight,
    fc_bias,
    out_weight,
    out_bias,
):
    (
        gain_one,
        bias_one,
        weight_qkv,
        bias_qv,
        weight_proj,
        bias_proj,
        gain_two,
        bias_two,
        weight_fc,
        bias_fc,
        weight_out,
        bias_out,
    ) = (
        lax.all_gather(ln1_gain, "batch", axis=0, tiled=True),
        lax.all_gather(ln1_bias, "batch", axis=0, tiled=True),
        lax.all_gather(qkv_weight, "batch", axis=0, tiled=True),
        lax.all_gather(qv_bias, "batch", axis=0, tiled=True),
        lax.all_gather(proj_weight, "batch", axis=0, tiled=True),
        lax.all_gather(proj_bias, "batch", axis=0, tiled=True),
        lax.all_gather(ln2_gain, "batch", axis=0, tiled=True),
        lax.all_gather(ln2_bias, "batch", axis=0, tiled=True),
        lax.all_gather(fc_weight, "batch", axis=0, tiled=True),
        lax.all_gather(fc_bias, "batch", axis=0, tiled=True),
        lax.all_gather(out_weight, "batch", axis=0, tiled=True),
        lax.all_gather(out_bias, "batch", axis=0, tiled=True),
    )
    seq_count, ctx_rows, model_width = tokens.shape
    row_count = seq_count * ctx_rows
    inputs = tokens.astype(jnp.float32).reshape(row_count, model_width)
    norm_one, norm_one_pull = jax.vjp(
        layer_norm, inputs, gain_one.astype(jnp.float32), bias_one.astype(jnp.float32)
    )
    normed_low = norm_one.astype(jnp.bfloat16)
    bias_float = bias_qv.astype(jnp.float32)
    bias_full = jnp.concatenate(
        [bias_float[:model_width], jnp.zeros((model_width,), jnp.float32), bias_float[model_width:]]
    )
    mixed_proj = (
        jnp.dot(normed_low, weight_qkv, preferred_element_type=jnp.float32) + bias_full
    ).astype(jnp.bfloat16)
    query_flat = mixed_proj[:, :model_width].reshape(seq_count, ctx_rows, model_width)
    key_flat = mixed_proj[:, model_width : 2 * model_width].reshape(
        seq_count, ctx_rows, model_width
    )
    value_flat = mixed_proj[:, 2 * model_width :].reshape(seq_count, ctx_rows, model_width)
    query_heads = query_flat.reshape(seq_count, ctx_rows, HEADS, HEAD_DIM)
    own_index = lax.axis_index("ctx")
    position = own_index * ctx_rows
    query_pos = position + jnp.arange(ctx_rows, dtype=jnp.int32)
    last_pos = position + ctx_rows - 1
    start_state = (
        jnp.full((seq_count, ctx_rows, HEADS), masked_value, jnp.float32),
        jnp.zeros((seq_count, ctx_rows, HEADS), jnp.float32),
        jnp.zeros((seq_count, ctx_rows, HEADS, HEAD_DIM), jnp.float32),
    )
    key_piece = lax.all_gather(key_flat, "ctx", axis=1, tiled=True)
    value_piece = lax.all_gather(value_flat, "ctx", axis=1, tiled=True)
    piece_rows = key_piece.shape[1]

    def compute(running):
        run_max, run_sum, accum = running
        key_split = key_piece.reshape(seq_count, piece_rows, HEADS, HEAD_DIM)
        value_split = value_piece.reshape(seq_count, piece_rows, HEADS, HEAD_DIM)
        scores = (
            jnp.einsum(
                "bqhd,bkhd->bqhk", query_heads, key_split, preferred_element_type=jnp.float32
            )
            * 0.125
        )
        key_pos = jnp.arange(piece_rows, dtype=jnp.int32)
        allowed = (key_pos[None, :] <= query_pos[:, None])[None, :, None, :]
        scores = jnp.where(allowed, scores, masked_value)
        new_max = jnp.maximum(run_max, jnp.max(scores, -1))
        weights_exp = jnp.where(allowed, jnp.exp(scores - new_max[..., None]), 0.0)
        new_sum = jnp.sum(weights_exp, -1)
        product = jnp.einsum(
            "bqhk,bkhd->bqhd",
            weights_exp.astype(jnp.bfloat16),
            value_split,
            preferred_element_type=jnp.float32,
        )
        return (new_max, new_sum, product)

    run_max, run_sum, accum = lax.cond(jnp.int32(0) <= last_pos, compute, keep_same, start_state)
    log_total = run_max + jnp.log(run_sum)
    attended = accum / run_sum[..., None]
    attended_low = attended.reshape(row_count, model_width).astype(jnp.bfloat16)
    middle = (
        inputs
        + jnp.dot(attended_low, weight_proj, preferred_element_type=jnp.float32)
        + bias_proj.astype(jnp.float32)
    )
    norm_two, norm_two_pull = jax.vjp(
        layer_norm, middle, gain_two.astype(jnp.float32), bias_two.astype(jnp.float32)
    )
    normed_two = norm_two.astype(jnp.bfloat16)
    pre_act = jnp.dot(normed_two, weight_fc, preferred_element_type=jnp.float32) + bias_fc.astype(
        jnp.float32
    )
    activated, gelu_pull = jax.vjp(partial(jax.nn.gelu, approximate=True), pre_act)
    hidden_low = activated.astype(jnp.bfloat16)
    output = (
        middle
        + jnp.dot(hidden_low, weight_out, preferred_element_type=jnp.float32)
        + bias_out.astype(jnp.float32)
    )
    layer_out = output.astype(jnp.bfloat16).reshape(tokens.shape)
    grad_out = cotangent.reshape(row_count, model_width)
    grad_out_float = grad_out.astype(jnp.float32)
    grad_w_out = jnp.einsum("rf,rd->fd", hidden_low, grad_out, preferred_element_type=jnp.float32)
    grad_b_out = jnp.sum(grad_out_float, 0)
    grad_hidden = jnp.einsum("rd,fd->rf", grad_out, weight_out, preferred_element_type=jnp.float32)
    (grad_pre,) = gelu_pull(grad_hidden)
    grad_pre_low = grad_pre.astype(jnp.bfloat16)
    grad_w_fc = jnp.einsum(
        "rd,rf->df", normed_two, grad_pre_low, preferred_element_type=jnp.float32
    )
    grad_b_fc = jnp.sum(grad_pre_low.astype(jnp.float32), 0)
    grad_norm_two = jnp.einsum(
        "rf,df->rd", grad_pre_low, weight_fc, preferred_element_type=jnp.float32
    )
    grad_mid_norm, grad_g_two, grad_b_two = norm_two_pull(grad_norm_two)
    grad_middle = grad_out_float + grad_mid_norm
    grad_branch = grad_middle.astype(jnp.bfloat16)
    grad_w_proj = jnp.einsum(
        "rd,re->de", attended_low, grad_branch, preferred_element_type=jnp.float32
    )
    grad_b_proj = jnp.sum(grad_branch.astype(jnp.float32), 0)
    grad_attended = jnp.einsum(
        "re,de->rd", grad_branch, weight_proj, preferred_element_type=jnp.float32
    ).astype(jnp.bfloat16)
    grad_att_flat = grad_attended.reshape(seq_count, ctx_rows, model_width)
    grad_att_heads = grad_att_flat.reshape(seq_count, ctx_rows, HEADS, HEAD_DIM)
    delta_mine = jnp.sum(grad_att_heads.astype(jnp.float32) * attended, -1)
    zero_heads = jnp.zeros((seq_count, ctx_rows, HEADS, HEAD_DIM), jnp.float32)
    cycle_count = lax.axis_size("ctx")

    def cycle_turn(turn, state):
        owner = (own_index - turn) % cycle_count
        first_row = owner * ctx_rows

        def visit(inner):
            key_piece, value_piece, grad_k, grad_v, grad_q = inner
            key_split = key_piece.reshape(seq_count, ctx_rows, HEADS, HEAD_DIM)
            value_split = value_piece.reshape(seq_count, ctx_rows, HEADS, HEAD_DIM)
            piece_pos = first_row + jnp.arange(ctx_rows, dtype=jnp.int32)
            scores = (
                jnp.einsum(
                    "bqhd,bkhd->bqhk", query_heads, key_split, preferred_element_type=jnp.float32
                )
                * 0.125
            )
            allowed = (piece_pos[None, :] <= query_pos[:, None])[None, :, None, :]
            probs = jnp.where(allowed, jnp.exp(scores - log_total[..., None]), 0.0)
            grad_probs = jnp.einsum(
                "bqhd,bkhd->bqhk", grad_att_heads, value_split, preferred_element_type=jnp.float32
            )
            grad_scores = (probs * (grad_probs - delta_mine[..., None])).astype(jnp.bfloat16)
            grad_q = (
                grad_q
                + jnp.einsum(
                    "bqhk,bkhd->bqhd", grad_scores, key_split, preferred_element_type=jnp.float32
                )
                * 0.125
            )
            grad_k = (
                grad_k
                + jnp.einsum(
                    "bqhk,bqhd->bkhd", grad_scores, query_heads, preferred_element_type=jnp.float32
                )
                * 0.125
            )
            grad_v = grad_v + jnp.einsum(
                "bqhk,bqhd->bkhd",
                probs.astype(jnp.bfloat16),
                grad_att_heads,
                preferred_element_type=jnp.float32,
            )
            return (key_piece, value_piece, grad_k, grad_v, grad_q)

        key_piece, value_piece, grad_k, grad_v, grad_q = lax.cond(
            owner <= own_index, visit, keep_same, state
        )
        key_piece, value_piece = shifted((key_piece, value_piece), "ctx", 1)
        grad_k, grad_v = (
            from_behind(grad_k.astype(jnp.bfloat16), "ctx", 1).astype(grad_k.dtype),
            from_behind(grad_v.astype(jnp.bfloat16), "ctx", 1).astype(grad_v.dtype),
        )
        return (key_piece, value_piece, grad_k, grad_v, grad_q)

    cycle_state = lax.fori_loop(
        0, cycle_count, cycle_turn, (key_flat, value_flat, zero_heads, zero_heads, zero_heads)
    )
    grad_k, grad_v, grad_q = (cycle_state[2], cycle_state[3], cycle_state[4])
    grad_mixed = jnp.concatenate(
        [
            grad_q.reshape(row_count, model_width),
            grad_k.reshape(row_count, model_width),
            grad_v.reshape(row_count, model_width),
        ],
        axis=1,
    ).astype(jnp.bfloat16)
    grad_w_qkv = jnp.einsum("rd,re->de", normed_low, grad_mixed, preferred_element_type=jnp.float32)
    grad_bias_all = jnp.sum(grad_mixed.astype(jnp.float32), 0)
    grad_b_qv = jnp.concatenate([grad_bias_all[:model_width], grad_bias_all[2 * model_width :]])
    grad_norm_one = jnp.einsum(
        "re,de->rd", grad_mixed, weight_qkv, preferred_element_type=jnp.float32
    )
    grad_in_norm, grad_g_one, grad_b_one = norm_one_pull(grad_norm_one)
    grad_tokens = (grad_middle + grad_in_norm).astype(jnp.bfloat16).reshape(tokens.shape)
    local_grads = (
        grad_g_one,
        grad_b_one,
        grad_w_qkv,
        grad_b_qv,
        grad_w_proj,
        grad_b_proj,
        grad_g_two,
        grad_b_two,
        grad_w_fc,
        grad_b_fc,
        grad_w_out,
        grad_b_out,
    )
    partial_grads = (
        lax.psum_scatter(
            local_grads[0].astype(jnp.bfloat16), "batch", scatter_dimension=0, tiled=True
        ).astype(jnp.float32),
        lax.psum_scatter(
            local_grads[1].astype(jnp.bfloat16), "batch", scatter_dimension=0, tiled=True
        ).astype(jnp.float32),
        lax.psum_scatter(
            local_grads[2].astype(jnp.bfloat16), "batch", scatter_dimension=0, tiled=True
        ).astype(jnp.float32),
        lax.psum_scatter(
            local_grads[3].astype(jnp.bfloat16), "batch", scatter_dimension=0, tiled=True
        ).astype(jnp.float32),
        lax.psum_scatter(
            local_grads[4].astype(jnp.bfloat16), "batch", scatter_dimension=0, tiled=True
        ).astype(jnp.float32),
        lax.psum_scatter(
            local_grads[5].astype(jnp.bfloat16), "batch", scatter_dimension=0, tiled=True
        ).astype(jnp.float32),
        lax.psum_scatter(
            local_grads[6].astype(jnp.bfloat16), "batch", scatter_dimension=0, tiled=True
        ).astype(jnp.float32),
        lax.psum_scatter(
            local_grads[7].astype(jnp.bfloat16), "batch", scatter_dimension=0, tiled=True
        ).astype(jnp.float32),
        lax.psum_scatter(
            local_grads[8].astype(jnp.bfloat16), "batch", scatter_dimension=0, tiled=True
        ).astype(jnp.float32),
        lax.psum_scatter(
            local_grads[9].astype(jnp.bfloat16), "batch", scatter_dimension=0, tiled=True
        ).astype(jnp.float32),
        lax.psum_scatter(
            local_grads[10].astype(jnp.bfloat16), "batch", scatter_dimension=0, tiled=True
        ).astype(jnp.float32),
        lax.psum_scatter(
            local_grads[11].astype(jnp.bfloat16), "batch", scatter_dimension=0, tiled=True
        ).astype(jnp.float32),
    )
    summed_grads = lax.psum(
        (
            partial_grads[0],
            partial_grads[1],
            partial_grads[2],
            partial_grads[3],
            partial_grads[4],
            partial_grads[5],
            partial_grads[6],
            partial_grads[7],
            partial_grads[8],
            partial_grads[9],
            partial_grads[10],
            partial_grads[11],
        ),
        "ctx",
    )
    return (
        layer_out,
        grad_tokens,
        summed_grads[0],
        summed_grads[1],
        summed_grads[2],
        summed_grads[3],
        summed_grads[4],
        summed_grads[5],
        summed_grads[6],
        summed_grads[7],
        summed_grads[8],
        summed_grads[9],
        summed_grads[10],
        summed_grads[11],
    )


def solution(mesh):
    placed = (
        P("batch", "ctx", None),
        P("batch", "ctx", None),
        P("batch"),
        P("batch"),
        P("batch", None),
        P("batch"),
        P("batch", None),
        P("batch"),
        P("batch"),
        P("batch"),
        P("batch", None),
        P("batch"),
        P("batch", None),
        P("batch"),
    )
    return jax.shard_map(
        per_device,
        mesh=mesh,
        in_specs=placed,
        out_specs=(
            P("batch", "ctx", None),
            P("batch", "ctx", None),
            P("batch"),
            P("batch"),
            P("batch", None),
            P("batch"),
            P("batch", None),
            P("batch"),
            P("batch"),
            P("batch"),
            P("batch", None),
            P("batch"),
            P("batch", None),
            P("batch"),
        ),
        check_vma=False,
    )
```

profile of v0, /device:TPU:0, one launch (start us, length us, event | category | flops | bytes accessed | tf_op | source)
XLA Modules:
  0.0 1264.4 jit_solution(45196582895574934)
XLA Ops:
  9.3 6.0 all-gather.3
  16.0 5.3 all-gather.2
  21.3 5.2 all-gather.4
  27.8 30.9 %all-gather.16.cloned.1.call-done = bf16[1024,3072]{1,0:T(8,128)(2,1)} async-done(((bf16[256,3072]{1,0:T(8,128)(2,1)}), bf16[1024,3072]{1,0:T(8,128)(2,1)}) %all-gather.16.cloned.1.call-update) | async-done | bytes 6291472 | tf_op jit(solution)/shard_map/all_gather | solution.py:70
  71.4 5.1 all_gather.53
  87.5 25.6 %all-gather.24.cloned.1.call-done = bf16[1024,1024]{1,0:T(8,128)(2,1)} async-done(((bf16[128,1024]{1,0:T(8,128)(2,1)}), bf16[1024,1024]{1,0:T(8,128)(2,1)}) %all-gather.24.cloned.1.call-update) | async-done | bytes 2097168 | tf_op jit(solution)/shard_map/all_gather | solution.py:110
  113.1 50.5 %all-gather.26.cloned.1.call-done = bf16[1024,1024]{1,0:T(8,128)(2,1)} async-done(((bf16[128,1024]{1,0:T(8,128)(2,1)}), bf16[1024,1024]{1,0:T(8,128)(2,1)}) %all-gather.26.cloned.1.call-update) | async-done | bytes 2097168 | tf_op jit(solution)/shard_map/all_gather | solution.py:111
  163.6 18.9 %conditional.2 = (f32[1,128,16]{1,2,0:T(8,128)}, f32[1,128,16,64]{1,3,2,0:T(8,128)S(1)}, f32[1,128,16]{1,2,0:T(8,128)S(1)}) conditional(s32[]{:T(128)} %convert_element_type.209, () %tuple.50, (s32[]{:T(128)}, bf16[1,1024,1024]{2,1,0:T(8,128)(2,1)}, bf16[1,128,16,64]{1,3,2,0:T(8,128)(2,1)}, bf16[1,1024,1024]{2,1,0:T(8,128)(2,1)}, ...), branch_computations={%region_2.0_spmd.clone, %region_3.6_spmd.clone} | conditional | flops 564267136 | bytes 81077848 | solution.py:138
  175.6 6.3 fusion.28
  188.5 57.4 %all-gather.20.cloned.1.call-done = bf16[1024,4096]{1,0:T(8,128)(2,1)} async-done(((bf16[256,4096]{1,0:T(8,128)(2,1)}), bf16[1024,4096]{1,0:T(8,128)(2,1)}) %all-gather.20.cloned.1.call-update) | async-done | bytes 8388624 | tf_op jit(solution)/shard_map/all_gather | solution.py:76
  250.7 54.9 %all-gather.22.cloned.1.call-done = bf16[4096,1024]{1,0:T(8,128)(2,1)} async-done(((bf16[1024,1024]{1,0:T(8,128)(2,1)}), bf16[4096,1024]{1,0:T(8,128)(2,1)}) %all-gather.22.cloned.1.call-update) | async-done | bytes 8388624 | tf_op jit(solution)/shard_map/all_gather | solution.py:78
  305.6 7.2 fusion.82
  323.7 224.8 %while.24 = (s32[]{:T(128)}, bf16[1,128,1024]{1,2,0:T(8,128)(2,1)}, bf16[1,128,1024]{1,2,0:T(8,128)(2,1)S(1)}, f32[1,128,16,64]{1,3,2,0:T(8,128)S(1)}, f32[1,128...) while((s32[]{:T(128)}, bf16[1,128,1024]{1,2,0:T(8,128)(2,1)}, ...), condition=%wide.region_14.15_spmd.clone, body=%wide.region_11.14_spmd.clone.sunk | while | flops 171065616 | bytes 20237936 | solution.py:245
  355.8 6.5 collective-permute-start.2
  389.2 7.3 collective-permute-start.3
  413.8 5.9 collective-permute-start.2
  423.2 6.2 collective-permute-start
  449.6 5.6 collective-permute-start
  455.1 8.6 collective-permute-start.1
  475.7 8.4 collective-permute-start
  502.7 6.3 collective-permute-start
  524.8 5.3 collective-permute-start.3
  539.4 5.4 collective-permute-done.2
  555.7 5.7 convolution_convert_fusion.1
  562.3 8.3 convolution_convert_fusion
  579.2 5.1 fusion.75
  584.7 11.8 all-reduce.9
  597.8 6.3 fusion.47
  604.1 17.2 %reduce-scatter.5.cloned.1.call-done = bf16[256,3072]{1,0:T(8,128)(2,1)} async-done(((bf16[1024,3072]{1,0:T(8,128)(2,1)}), bf16[256,3072]{1,0:T(8,128)(2,1)}) %reduce-scatter.5.cloned.1.call-update) | async-done | bytes 1572880 | tf_op jit(solution)/shard_map/reduce_scatter | solution.py:286
  621.3 74.3 %reduce-scatter.9.cloned.1.call-done = bf16[256,4096]{1,0:T(8,128)(2,1)} async-done(((bf16[1024,4096]{1,0:T(8,128)(2,1)}), bf16[256,4096]{1,0:T(8,128)(2,1)}) %reduce-scatter.9.cloned.1.call-update) | async-done | bytes 2097168 | tf_op jit(solution)/shard_map/reduce_scatter | solution.py:304
  695.6 74.3 %reduce-scatter.11.cloned.1.call-done = bf16[1024,1024]{1,0:T(8,128)(2,1)} async-done(((bf16[4096,1024]{1,0:T(8,128)(2,1)}), bf16[1024,1024]{1,0:T(8,128)(2,1)}) %reduce-scatter.11.cloned.1.call-update) | async-done | bytes 2097168 | tf_op jit(solution)/shard_map/reduce_scatter | solution.py:310
  770.0 487.6 %all-reduce.11 = (f32[256]{0:T(256)}, f32[256]{0:T(256)}, f32[256,3072]{1,0:T(8,128)}, f32[512]{0:T(512)}, f32[256,1024]{1,0:T(8,128)}, /*index=5*/f32[256]{0:T(...) all-reduce(f32[256]{0:T(256)S(1)} %get-tuple-element.588, ...), channel_id=1, replica_groups=mesh['batch'=4,'ctx'=8] {'ctx'}, use_global_device_ids=true, to_apply=%region_19.20 | all-reduce | flops 3148800 | bytes 18898944 | tf_op jit(solution)/shard_map/psum | solution.py:317
  (274 shorter events, 240.4 us)
Async XLA Ops:
  7.2 51.6 %all-gather.16.cloned.1.call-start = ((), (), s32[]{:S(2)}) async-start(), calls=%async_computation.4 | async-start | bytes 7864320 | tf_op jit(solution)/shard_map/all_gather | solution.py:70
  7.9 105.2 %all-gather.24.cloned.1.call-start = ((), (), s32[]{:S(2)}) async-start(), calls=%async_computation.12 | async-start | bytes 2359296 | tf_op jit(solution)/shard_map/all_gather | solution.py:110
  63.7 100.0 %all-gather.26.cloned.1.call-start = ((), (), s32[]{:S(2)}) async-start(), calls=%async_computation.13 | async-start | bytes 2359296 | tf_op jit(solution)/shard_map/all_gather | solution.py:111
  64.4 121.8 %all-gather.18.cloned.1.call-start = ((), (), s32[]{:S(2)}) async-start(), calls=%async_computation.5 | async-start | bytes 2621440 | tf_op jit(solution)/shard_map/all_gather | solution.py:72
  65.0 180.9 %all-gather.20.cloned.1.call-start = ((), (), s32[]{:S(2)}) async-start(), calls=%async_computation.6 | async-start | bytes 10485760 | tf_op jit(solution)/shard_map/all_gather | solution.py:76
  65.6 240.0 %all-gather.22.cloned.1.call-start = ((), (), s32[]{:S(2)}) async-start(), calls=%async_computation.7 | async-start | bytes 10485760 | tf_op jit(solution)/shard_map/all_gather | solution.py:78
  66.2 537.9 %reduce-scatter.7.cloned.1.call-start = ((), (), s32[]{:S(2)}) async-start(), calls=%async_computation.9 | async-start | bytes 2621440 | tf_op jit(solution)/shard_map/reduce_scatter | solution.py:292
  319.2 302.1 %reduce-scatter.5.cloned.1.call-start = ((), (), s32[]{:S(2)}) async-start(), calls=%async_computation.8 | async-start | bytes 7864320 | tf_op jit(solution)/shard_map/reduce_scatter | solution.py:286
  330.8 15.3 %collective-permute-start.3 = (bf16[1,128,16,64]{1,3,2,0:T(8,128)(2,1)S(1)}, bf16[1,128,16,64]{1,3,2,0:T(8,128)(2,1)S(1)}, u32[]{:S(2)}, u32[]{:S(2)}) collective-permute-start(bf16[1,128,16,64]{1,3,2,0:T(8,128)(2,1)S(1)} %convert_element_type.364), channel_id=1, source_target_pairs={{7,0},{0,1},{1,2},{2,3},{3,4},{4,5},{5,6},{6,7},{15,8},{8,9},{9,10... | collective-permute-start | bytes 786440 | tf_op jit(solution)/shard_map/while/body/eval_jaxpr/ppermute | solution.py:25
  332.4 16.3 %collective-permute-start = (bf16[1,128,1024]{1,2,0:T(8,128)(2,1)S(1)}, bf16[1,128,1024]{1,2,0:T(8,128)(2,1)}, u32[]{:S(2)}, u32[]{:S(2)}) collective-permute-start(bf16[1,128,1024]{1,2,0:T(8,128)(2,1)S(1)} %copy.89), channel_id=1, source_target_pairs={{0,1},{1,2},{2,3},{3,4},{4,5},{5,6},{6,7},{8,9},{9,10},{10,11},{11... | collective-permute-start | bytes 786440 | tf_op jit(solution)/shard_map/while/body/eval_jaxpr/ppermute | solution.py:19
  336.4 17.2 %collective-permute-start.1 = (bf16[1,128,1024]{1,2,0:T(8,128)(2,1)S(1)}, bf16[1,128,1024]{1,2,0:T(8,128)(2,1)S(1)}, u32[]{:S(2)}, u32[]{:S(2)}) collective-permute-start(bf16[1,128,1024]{1,2,0:T(8,128)(2,1)S(1)} %copy.90), channel_id=1, source_target_pairs={{0,1},{1,2},{2,3},{3,4},{4,5},{5,6},{6,7},{8,9},{9,10},{10,11},{11... | collective-permute-start | bytes 786440 | tf_op jit(solution)/shard_map/while/body/eval_jaxpr/ppermute | solution.py:19
  355.8 16.5 %collective-permute-start.2 = (bf16[1,128,16,64]{1,3,2,0:T(8,128)(2,1)S(1)}, bf16[1,128,16,64]{1,3,2,0:T(8,128)(2,1)S(1)}, u32[]{:S(2)}, u32[]{:S(2)}) collective-permute-start(bf16[1,128,16,64]{1,3,2,0:T(8,128)(2,1)S(1)} %convert_element_type.362), channel_id=1, source_target_pairs={{7,0},{0,1},{1,2},{2,3},{3,4},{4,5},{5,6},{6,7},{15,8},{8,9},{9,10... | collective-permute-start | bytes 786440 | tf_op jit(solution)/shard_map/while/body/eval_jaxpr/ppermute | solution.py:25
  364.8 15.5 %collective-permute-start = (bf16[1,128,1024]{1,2,0:T(8,128)(2,1)S(1)}, bf16[1,128,1024]{1,2,0:T(8,128)(2,1)}, u32[]{:S(2)}, u32[]{:S(2)}) collective-permute-start(bf16[1,128,1024]{1,2,0:T(8,128)(2,1)S(1)} %copy.89), channel_id=1, source_target_pairs={{0,1},{1,2},{2,3},{3,4},{4,5},{5,6},{6,7},{8,9},{9,10},{10,11},{11... | collective-permute-start | bytes 786440 | tf_op jit(solution)/shard_map/while/body/eval_jaxpr/ppermute | solution.py:19
  368.0 16.4 %collective-permute-start.1 = (bf16[1,128,1024]{1,2,0:T(8,128)(2,1)S(1)}, bf16[1,128,1024]{1,2,0:T(8,128)(2,1)S(1)}, u32[]{:S(2)}, u32[]{:S(2)}) collective-permute-start(bf16[1,128,1024]{1,2,0:T(8,128)(2,1)S(1)} %copy.90), channel_id=1, source_target_pairs={{0,1},{1,2},{2,3},{3,4},{4,5},{5,6},{6,7},{8,9},{9,10},{10,11},{11... | collective-permute-start | bytes 786440 | tf_op jit(solution)/shard_map/while/body/eval_jaxpr/ppermute | solution.py:19
  386.6 16.7 %collective-permute-start.2 = (bf16[1,128,16,64]{1,3,2,0:T(8,128)(2,1)S(1)}, bf16[1,128,16,64]{1,3,2,0:T(8,128)(2,1)S(1)}, u32[]{:S(2)}, u32[]{:S(2)}) collective-permute-start(bf16[1,128,16,64]{1,3,2,0:T(8,128)(2,1)S(1)} %convert_element_type.362), channel_id=1, source_target_pairs={{7,0},{0,1},{1,2},{2,3},{3,4},{4,5},{5,6},{6,7},{15,8},{8,9},{9,10... | collective-permute-start | bytes 786440 | tf_op jit(solution)/shard_map/while/body/eval_jaxpr/ppermute | solution.py:25
  389.2 17.3 %collective-permute-start.3 = (bf16[1,128,16,64]{1,3,2,0:T(8,128)(2,1)S(1)}, bf16[1,128,16,64]{1,3,2,0:T(8,128)(2,1)S(1)}, u32[]{:S(2)}, u32[]{:S(2)}) collective-permute-start(bf16[1,128,16,64]{1,3,2,0:T(8,128)(2,1)S(1)} %convert_element_type.364), channel_id=1, source_target_pairs={{7,0},{0,1},{1,2},{2,3},{3,4},{4,5},{5,6},{6,7},{15,8},{8,9},{9,10... | collective-permute-start | bytes 786440 | tf_op jit(solution)/shard_map/while/body/eval_jaxpr/ppermute | solution.py:25
  413.8 20.1 %collective-permute-start.2 = (bf16[1,128,16,64]{1,3,2,0:T(8,128)(2,1)S(1)}, bf16[1,128,16,64]{1,3,2,0:T(8,128)(2,1)S(1)}, u32[]{:S(2)}, u32[]{:S(2)}) collective-permute-start(bf16[1,128,16,64]{1,3,2,0:T(8,128)(2,1)S(1)} %convert_element_type.362), channel_id=1, source_target_pairs={{7,0},{0,1},{1,2},{2,3},{3,4},{4,5},{5,6},{6,7},{15,8},{8,9},{9,10... | collective-permute-start | bytes 786440 | tf_op jit(solution)/shard_map/while/body/eval_jaxpr/ppermute | solution.py:25
  419.7 16.5 %collective-permute-start.3 = (bf16[1,128,16,64]{1,3,2,0:T(8,128)(2,1)S(1)}, bf16[1,128,16,64]{1,3,2,0:T(8,128)(2,1)S(1)}, u32[]{:S(2)}, u32[]{:S(2)}) collective-permute-start(bf16[1,128,16,64]{1,3,2,0:T(8,128)(2,1)S(1)} %convert_element_type.364), channel_id=1, source_target_pairs={{7,0},{0,1},{1,2},{2,3},{3,4},{4,5},{5,6},{6,7},{15,8},{8,9},{9,10... | collective-permute-start | bytes 786440 | tf_op jit(solution)/shard_map/while/body/eval_jaxpr/ppermute | solution.py:25
  442.4 21.3 %collective-permute-start.2 = (bf16[1,128,16,64]{1,3,2,0:T(8,128)(2,1)S(1)}, bf16[1,128,16,64]{1,3,2,0:T(8,128)(2,1)S(1)}, u32[]{:S(2)}, u32[]{:S(2)}) collective-permute-start(bf16[1,128,16,64]{1,3,2,0:T(8,128)(2,1)S(1)} %convert_element_type.362), channel_id=1, source_target_pairs={{7,0},{0,1},{1,2},{2,3},{3,4},{4,5},{5,6},{6,7},{15,8},{8,9},{9,10... | collective-permute-start | bytes 786440 | tf_op jit(solution)/shard_map/while/body/eval_jaxpr/ppermute | solution.py:25
  446.1 19.1 %collective-permute-start.3 = (bf16[1,128,16,64]{1,3,2,0:T(8,128)(2,1)S(1)}, bf16[1,128,16,64]{1,3,2,0:T(8,128)(2,1)S(1)}, u32[]{:S(2)}, u32[]{:S(2)}) collective-permute-start(bf16[1,128,16,64]{1,3,2,0:T(8,128)(2,1)S(1)} %convert_element_type.364), channel_id=1, source_target_pairs={{7,0},{0,1},{1,2},{2,3},{3,4},{4,5},{5,6},{6,7},{15,8},{8,9},{9,10... | collective-permute-start | bytes 786440 | tf_op jit(solution)/shard_map/while/body/eval_jaxpr/ppermute | solution.py:25
  449.6 16.5 %collective-permute-start = (bf16[1,128,1024]{1,2,0:T(8,128)(2,1)S(1)}, bf16[1,128,1024]{1,2,0:T(8,128)(2,1)}, u32[]{:S(2)}, u32[]{:S(2)}) collective-permute-start(bf16[1,128,1024]{1,2,0:T(8,128)(2,1)S(1)} %copy.89), channel_id=1, source_target_pairs={{0,1},{1,2},{2,3},{3,4},{4,5},{5,6},{6,7},{8,9},{9,10},{10,11},{11... | collective-permute-start | bytes 786440 | tf_op jit(solution)/shard_map/while/body/eval_jaxpr/ppermute | solution.py:19
  469.8 20.7 %collective-permute-start.2 = (bf16[1,128,16,64]{1,3,2,0:T(8,128)(2,1)S(1)}, bf16[1,128,16,64]{1,3,2,0:T(8,128)(2,1)S(1)}, u32[]{:S(2)}, u32[]{:S(2)}) collective-permute-start(bf16[1,128,16,64]{1,3,2,0:T(8,128)(2,1)S(1)} %convert_element_type.362), channel_id=1, source_target_pairs={{7,0},{0,1},{1,2},{2,3},{3,4},{4,5},{5,6},{6,7},{15,8},{8,9},{9,10... | collective-permute-start | bytes 786440 | tf_op jit(solution)/shard_map/while/body/eval_jaxpr/ppermute | solution.py:25
  472.4 20.9 %collective-permute-start.3 = (bf16[1,128,16,64]{1,3,2,0:T(8,128)(2,1)S(1)}, bf16[1,128,16,64]{1,3,2,0:T(8,128)(2,1)S(1)}, u32[]{:S(2)}, u32[]{:S(2)}) collective-permute-start(bf16[1,128,16,64]{1,3,2,0:T(8,128)(2,1)S(1)} %convert_element_type.364), channel_id=1, source_target_pairs={{7,0},{0,1},{1,2},{2,3},{3,4},{4,5},{5,6},{6,7},{15,8},{8,9},{9,10... | collective-permute-start | bytes 786440 | tf_op jit(solution)/shard_map/while/body/eval_jaxpr/ppermute | solution.py:25
  475.7 18.5 %collective-permute-start = (bf16[1,128,1024]{1,2,0:T(8,128)(2,1)S(1)}, bf16[1,128,1024]{1,2,0:T(8,128)(2,1)}, u32[]{:S(2)}, u32[]{:S(2)}) collective-permute-start(bf16[1,128,1024]{1,2,0:T(8,128)(2,1)S(1)} %copy.89), channel_id=1, source_target_pairs={{0,1},{1,2},{2,3},{3,4},{4,5},{5,6},{6,7},{8,9},{9,10},{10,11},{11... | collective-permute-start | bytes 786440 | tf_op jit(solution)/shard_map/while/body/eval_jaxpr/ppermute | solution.py:19
  496.4 21.4 %collective-permute-start.2 = (bf16[1,128,16,64]{1,3,2,0:T(8,128)(2,1)S(1)}, bf16[1,128,16,64]{1,3,2,0:T(8,128)(2,1)S(1)}, u32[]{:S(2)}, u32[]{:S(2)}) collective-permute-start(bf16[1,128,16,64]{1,3,2,0:T(8,128)(2,1)S(1)} %convert_element_type.362), channel_id=1, source_target_pairs={{7,0},{0,1},{1,2},{2,3},{3,4},{4,5},{5,6},{6,7},{15,8},{8,9},{9,10... | collective-permute-start | bytes 786440 | tf_op jit(solution)/shard_map/while/body/eval_jaxpr/ppermute | solution.py:25
  498.7 22.0 %collective-permute-start.3 = (bf16[1,128,16,64]{1,3,2,0:T(8,128)(2,1)S(1)}, bf16[1,128,16,64]{1,3,2,0:T(8,128)(2,1)S(1)}, u32[]{:S(2)}, u32[]{:S(2)}) collective-permute-start(bf16[1,128,16,64]{1,3,2,0:T(8,128)(2,1)S(1)} %convert_element_type.364), channel_id=1, source_target_pairs={{7,0},{0,1},{1,2},{2,3},{3,4},{4,5},{5,6},{6,7},{15,8},{8,9},{9,10... | collective-permute-start | bytes 786440 | tf_op jit(solution)/shard_map/while/body/eval_jaxpr/ppermute | solution.py:25
  502.7 18.8 %collective-permute-start = (bf16[1,128,1024]{1,2,0:T(8,128)(2,1)S(1)}, bf16[1,128,1024]{1,2,0:T(8,128)(2,1)}, u32[]{:S(2)}, u32[]{:S(2)}) collective-permute-start(bf16[1,128,1024]{1,2,0:T(8,128)(2,1)S(1)} %copy.89), channel_id=1, source_target_pairs={{0,1},{1,2},{2,3},{3,4},{4,5},{5,6},{6,7},{8,9},{9,10},{10,11},{11... | collective-permute-start | bytes 786440 | tf_op jit(solution)/shard_map/while/body/eval_jaxpr/ppermute | solution.py:19
  523.7 21.1 %collective-permute-start.2 = (bf16[1,128,16,64]{1,3,2,0:T(8,128)(2,1)S(1)}, bf16[1,128,16,64]{1,3,2,0:T(8,128)(2,1)S(1)}, u32[]{:S(2)}, u32[]{:S(2)}) collective-permute-start(bf16[1,128,16,64]{1,3,2,0:T(8,128)(2,1)S(1)} %convert_element_type.362), channel_id=1, source_target_pairs={{7,0},{0,1},{1,2},{2,3},{3,4},{4,5},{5,6},{6,7},{15,8},{8,9},{9,10... | collective-permute-start | bytes 786440 | tf_op jit(solution)/shard_map/while/body/eval_jaxpr/ppermute | solution.py:25
  524.8 22.9 %collective-permute-start.3 = (bf16[1,128,16,64]{1,3,2,0:T(8,128)(2,1)S(1)}, bf16[1,128,16,64]{1,3,2,0:T(8,128)(2,1)S(1)}, u32[]{:S(2)}, u32[]{:S(2)}) collective-permute-start(bf16[1,128,16,64]{1,3,2,0:T(8,128)(2,1)S(1)} %convert_element_type.364), channel_id=1, source_target_pairs={{7,0},{0,1},{1,2},{2,3},{3,4},{4,5},{5,6},{6,7},{15,8},{8,9},{9,10... | collective-permute-start | bytes 786440 | tf_op jit(solution)/shard_map/while/body/eval_jaxpr/ppermute | solution.py:25
  530.0 18.5 %collective-permute-start = (bf16[1,128,1024]{1,2,0:T(8,128)(2,1)S(1)}, bf16[1,128,1024]{1,2,0:T(8,128)(2,1)}, u32[]{:S(2)}, u32[]{:S(2)}) collective-permute-start(bf16[1,128,1024]{1,2,0:T(8,128)(2,1)S(1)} %copy.89), channel_id=1, source_target_pairs={{0,1},{1,2},{2,3},{3,4},{4,5},{5,6},{6,7},{8,9},{9,10},{10,11},{11... | collective-permute-start | bytes 786440 | tf_op jit(solution)/shard_map/while/body/eval_jaxpr/ppermute | solution.py:19
  554.5 141.1 %reduce-scatter.9.cloned.1.call-start = ((), (), s32[]{:S(2)}) async-start(), calls=%async_computation.10 | async-start | bytes 10485760 | tf_op jit(solution)/shard_map/reduce_scatter | solution.py:304
  561.4 208.6 %reduce-scatter.11.cloned.1.call-start = ((), (), s32[]{:S(2)}) async-start(), calls=%async_computation.11 | async-start | bytes 10485760 | tf_op jit(solution)/shard_map/reduce_scatter | solution.py:310
  (32 other events, 417.3 us)
Sparse Core Ops, SparseCore 0:
  9.6 49.1 all-gather.15
  63.8 49.2 all-gather.23
  115.8 47.7 all-gather.25
  165.1 21.0 all-gather.17
  187.6 58.2 all-gather.19
  247.3 58.2 all-gather.21
  319.3 31.4 reduce-scatter.6
  554.6 66.6 reduce-scatter.4
  623.9 71.7 reduce-scatter.8
  698.2 71.6 reduce-scatter.10
where the time goes:
time: 1270 us; the launch traced here: 1260 us
  blocking collectives  541 us (43%)
  waiting for transfers between devices  452 us (36%)
  starting transfers between devices  136 us (11%)
  matrix products  68.4 us (5%)
  other arithmetic  26 us (2%)
  local copies, waits for them, and re-layouts  23.5 us (2%)
  between operations  16.5 us (1%)
    psum x1, blocking collectives, per_device(): lax.psum((partial_grads[0], partial_grads[1], partial_grads[2], partial_g...  488 us
    ppermute x16, starting transfers between devices, shifted(): return lax.ppermute(block, axis, route)  78.6 us
    reduce_scatter x1, waiting for transfers between devices, per_device(): lax.psum_scatter(local_grads[10].astype(jnp.bfloat16), 'batch', scatter_d...  74.3 us
    reduce_scatter x1, waiting for transfers between devices, per_device(): lax.psum_scatter(local_grads[8].astype(jnp.bfloat16), 'batch', scatter_di...  74.3 us
    all_gather x1, waiting for transfers between devices, per_device(): lax.all_gather(fc_weight, 'batch', axis=0, tiled=True)  57.4 us
    ppermute x16, starting transfers between devices, from_behind(): return lax.ppermute(block, axis, route)  56.6 us
    all_gather x1, waiting for transfers between devices, per_device(): lax.all_gather(out_weight, 'batch', axis=0, tiled=True)  54.9 us
    all_gather x1, waiting for transfers between devices, per_device(): value_piece = lax.all_gather(value_flat, 'ctx', axis=1, tiled=True)  50.5 us
  transfers between devices with their start and end apart: 42, of which 31 were waited for; matrix products, arithmetic and copies ran while one was open for 8% of the time, Pallas kernels for 0%

commit v1 on v0

--- a/solution.py
+++ b/solution.py
@@ -1,8 +1,11 @@
 from functools import partial
+from types import SimpleNamespace
 
 import jax
 import jax.numpy as jnp
 from jax import lax
+from jax.experimental import pallas as pl
+from jax.experimental.pallas import tpu as pltpu
 from jax.sharding import PartitionSpec as P
 
 HEADS = 16
@@ -349,6 +352,963 @@
     )
 
 
+BF, F32 = jnp.bfloat16, jnp.float32
+NN = (((1,), (0,)), ((), ()))
+NT = (((1,), (1,)), ((), ()))
+TN = (((0,), (0,)), ((), ()))
+MESH = pl.DeviceIdType.MESH
+NB, NC, WIDTH, ROWS, FF, PAIR = 4, 8, 1024, 128, 4096, 128
+SHARD = WIDTH // NB
+LENGTH = ROWS * NC
+SMALL_ROWS = 16
+
+
+def mm(left, right, dims=NN):
+    return lax.dot_general(left, right, dims, preferred_element_type=F32)
+
+
+def run(when, action):
+    if when is None:
+        action()
+    else:
+        pl.when(when)(action)
+
+
+def both(one, two):
+    return two if one is None else (one if two is None else jnp.logical_and(one, two))
+
+
+class Net:
+    def __init__(self, b, c, send_sems, recv_sems):
+        self.b, self.c, self.z, self.x = b, c, c // 2, c % 2
+        self.side = c + 1 - 2 * self.x
+        self.core = b % 2
+        self.sib = b + 1 - 2 * self.core
+        self.across = lax.rem(b + 2, NB)
+        self.diag = lax.rem(self.sib + 2, NB)
+        self.send_sems, self.recv_sems = send_sems, recv_sems
+        self.sent, self.taken, self.pending = 0, 0, []
+
+    def slots(self, count):
+        base = self.taken
+        self.taken += count
+        assert self.taken <= self.recv_sems.shape[0]
+        return base
+
+    def send(self, src, dst, device, slot, when=None):
+        assert self.sent < self.send_sems.shape[0]
+        copy = pltpu.make_async_remote_copy(
+            src_ref=src,
+            dst_ref=dst,
+            send_sem=self.send_sems.at[self.sent],
+            recv_sem=self.recv_sems.at[slot],
+            device_id=device,
+            device_id_type=MESH,
+        )
+        self.sent += 1
+        run(when, copy.start)
+        self.pending.append((when, copy))
+
+    def wait(self, slot, ref):
+        pltpu.make_async_remote_copy(
+            src_ref=ref,
+            dst_ref=ref,
+            send_sem=self.send_sems.at[0],
+            recv_sem=self.recv_sems.at[slot],
+            device_id=(self.sib, self.c),
+            device_id_type=MESH,
+        ).wait_recv()
+
+    def drain(self):
+        for when, copy in self.pending:
+            run(when, copy.wait_send)
+
+
+class GatherCtx:
+    def __init__(self, net, views, count):
+        self.net, self.views, self.count = net, views, count
+        self.along, self.beside = net.slots(4 * count), net.slots(4 * count)
+
+    def hand_on(self, zz, srcs, up, down):
+        net, count = self.net, self.count
+        dsts = self.views(2 * zz + net.x)
+        for i in range(count):
+            if up is not False:
+                net.send(srcs[i], dsts[i], (net.b, net.c + 2), self.along + zz * count + i, up)
+            if down is not False:
+                net.send(srcs[i], dsts[i], (net.b, net.c - 2), self.along + zz * count + i, down)
+
+    def beside_send(self, zz, srcs, when):
+        net, count = self.net, self.count
+        dsts = self.views(2 * zz + net.x)
+        for i in range(count):
+            net.send(srcs[i], dsts[i], (net.b, net.side), self.beside + zz * count + i, when)
+
+    def start(self, srcs):
+        net = self.net
+        self.hand_on(net.z, srcs, net.z < 3, net.z > 0)
+        self.beside_send(net.z, srcs, None)
+
+    def stage(self, d):
+        net, count = self.net, self.count
+        for sign in (-1, 1):
+            zz = net.z + sign * d
+            here = zz >= 0 if sign < 0 else zz <= 3
+            refs = self.views(2 * zz + net.x)
+
+            def arrive(refs=refs, zz=zz):
+                for i in range(count):
+                    net.wait(self.along + zz * count + i, refs[i])
+
+            pl.when(here)(arrive)
+            if d < 3:
+                if sign < 0:
+                    self.hand_on(zz, refs, both(here, net.z < 3), False)
+                else:
+                    self.hand_on(zz, refs, False, both(here, net.z > 0))
+            self.beside_send(zz, refs, here)
+
+    def finish(self):
+        net, count = self.net, self.count
+        for zz in range(4):
+            refs = self.views(2 * zz + 1 - net.x)
+            for i in range(count):
+                net.wait(self.beside + zz * count + i, refs[i])
+
+
+def chunks(ref):
+    if len(ref.shape) == 3:
+        return ref.shape[0], lambda i: (i,)
+    rows = min(32, ref.shape[0])
+    return ref.shape[0] // rows, lambda i: (pl.ds(pl.multiple_of(i * rows, rows), rows),)
+
+
+def add_into(target, terms, dtype=BF):
+    count, at = chunks(target)
+
+    def body(i, carry):
+        total = terms[0][at(i)].astype(F32)
+        for term in terms[1:]:
+            total = total + term[at(i)].astype(F32)
+        target[at(i)] = total.astype(dtype)
+        return carry
+
+    lax.fori_loop(0, count, body, 0)
+
+
+class ReduceCtx:
+    def __init__(self, net, mine, beside, up, down):
+        self.net, self.mine, self.beside, self.up, self.down = net, mine, beside, up, down
+        self.s_beside, self.s_up, self.s_down = net.slots(4), net.slots(4), net.slots(4)
+
+    def start(self, order=(3, 0, 2, 1)):
+        net = self.net
+        for zz in order:
+            net.send(self.mine(2 * zz + 1 - net.x), self.beside.at[zz], (net.b, net.side), self.s_beside + zz)
+
+    def fold(self, zz):
+        net = self.net
+        net.wait(self.s_beside + zz, self.beside.at[zz])
+        add_into(self.mine(2 * zz + net.x), [self.mine(2 * zz + net.x), self.beside.at[zz]])
+
+    def stage(self, d):
+        net = self.net
+        for sign in (1, -1):
+            zz = net.z + sign * d
+            here = zz <= 3 if sign > 0 else zz >= 0
+            inner = net.z >= 1 if sign > 0 else net.z <= 2
+            box, slot = (self.up, self.s_up) if sign > 0 else (self.down, self.s_down)
+            mine = self.mine(2 * zz + net.x)
+
+            def work(zz=zz, inner=inner, box=box, slot=slot, mine=mine):
+                self.fold(zz)
+
+                @pl.when(inner)
+                def _():
+                    net.wait(slot + zz, box.at[zz])
+                    add_into(mine, [mine, box.at[zz]])
+
+            pl.when(here)(work)
+            net.send(mine, box.at[zz], (net.b, net.c + 2 * sign), slot + zz, here)
+
+    def finish(self, target):
+        net, z = self.net, self.net.z
+        net.wait(self.s_beside + z, self.beside.at[z])
+        mine, beside = self.mine(net.c), self.beside.at[z]
+
+        @pl.when(z >= 1)
+        def _():
+            net.wait(self.s_up + z, self.up.at[z])
+
+        @pl.when(z <= 2)
+        def _():
+            net.wait(self.s_down + z, self.down.at[z])
+
+        pl.when(z == 0)(lambda: add_into(target, [mine, beside, self.down.at[z]]))
+        pl.when(z == 3)(lambda: add_into(target, [mine, beside, self.up.at[z]]))
+        pl.when(jnp.logical_and(z > 0, z < 3))(
+            lambda: add_into(target, [mine, beside, self.up.at[z], self.down.at[z]])
+        )
+
+
+class SwapCtx:
+    def __init__(self, net, src, dst, count):
+        self.net, self.src, self.dst, self.count = net, src, dst, count
+        self.base = net.slots(NC * count)
+
+    def start(self):
+        net, count = self.net, self.count
+        for step in range(1, NC):
+            j = lax.rem(net.c + step, NC)
+            srcs, dsts = self.src(j), self.dst(net.c)
+            for i in range(count):
+                net.send(srcs[i], dsts[i], (net.b, j), self.base + net.c * count + i)
+        for one, two in zip(self.src(net.c), self.dst(net.c)):
+            two[...] = one[...]
+
+    def finish(self):
+        net, count = self.net, self.count
+        for step in range(1, NC):
+            j = lax.rem(net.c - step + NC, NC)
+            dsts = self.dst(j)
+            for i in range(count):
+                net.wait(self.base + j * count + i, dsts[i])
+
+
+class GatherBatch:
+    def __init__(self, net, views, count=1):
+        self.net, self.views, self.count = net, views, count
+        self.base = net.slots(NB * count)
+
+    def start(self, srcs):
+        net = self.net
+        dsts = self.views(net.b)
+        for i in range(self.count):
+            slot = self.base + net.b * self.count + i
+            net.send(srcs[i], dsts[i], (net.across, net.c), slot)
+        for i in range(self.count):
+            slot = self.base + net.b * self.count + i
+            net.send(srcs[i], dsts[i], (net.sib, net.c), slot)
+
+    def relay(self):
+        net = self.net
+        refs = self.views(net.across)
+        for i in range(self.count):
+            slot = self.base + net.across * self.count + i
+            net.wait(slot, refs[i])
+            net.send(refs[i], refs[i], (net.sib, net.c), slot)
+
+    def finish(self):
+        net = self.net
+        for j in (net.sib, net.diag):
+            refs = self.views(j)
+            for i in range(self.count):
+                net.wait(self.base + j * self.count + i, refs[i])
+
+
+class ReduceBatch:
+    def __init__(self, net, mine, boxes):
+        self.net, self.mine, self.boxes = net, mine, boxes
+        self.base = net.slots(3)
+
+    def give(self):
+        net = self.net
+        net.send(self.mine(net.diag), self.boxes.at[0], (net.sib, net.c), self.base)
+
+    def cross(self):
+        net = self.net
+        net.wait(self.base, self.boxes.at[0])
+        block = self.mine(net.across)
+        add_into(block, [block, self.boxes.at[0]])
+        net.send(block, self.boxes.at[1], (net.across, net.c), self.base + 1)
+
+    def keep(self):
+        net = self.net
+        net.send(self.mine(net.sib), self.boxes.at[2], (net.sib, net.c), self.base + 2)
+
+    def finish(self):
+        net = self.net
+        net.wait(self.base + 2, self.boxes.at[2])
+        net.wait(self.base + 1, self.boxes.at[1])
+        return [self.mine(net.b), self.boxes.at[1], self.boxes.at[2]]
+
+
+def row_of(parts, index):
+    return jnp.concatenate([parts[j, index : index + 1, :] for j in range(NB)], axis=1)
+
+
+def put_row(target, index, row):
+    for j in range(NB):
+        target[j, index : index + 1, :] = row[:, j * SHARD : (j + 1) * SHARD]
+
+
+def rows_of(block, size):
+    return lambda j: block.at[pl.ds(pl.multiple_of(j * size, size), size)]
+
+
+def normalise(inputs):
+    centre = inputs - jnp.mean(inputs, -1, keepdims=True)
+    spread = jnp.mean(centre * centre, -1, keepdims=True)
+    scale = lax.rsqrt(spread + epsilon)
+    return centre * scale, scale
+
+
+def head_lanes(h, rows):
+    lane = lax.broadcasted_iota(jnp.int32, (rows, PAIR), 1)
+    return (lane >= h * HEAD_DIM) & (lane < (h + 1) * HEAD_DIM)
+
+
+QB = 256
+
+
+def scores_of(keys, query, masked):
+    scores = mm(keys, query, NT) * 0.125
+    if masked:
+        key_pos = lax.broadcasted_iota(jnp.int32, scores.shape, 0)
+        query_pos = lax.broadcasted_iota(jnp.int32, scores.shape, 1)
+        scores = jnp.where(key_pos <= query_pos, scores, masked_value)
+    return scores
+
+
+def attend(mix, value_t, att, lse, work, low_work):
+    value_t[...] = mix[:, 2 * PAIR :].astype(F32).T.astype(BF)
+    for qb in range(LENGTH // QB):
+        here = slice(qb * QB, (qb + 1) * QB)
+        outs = []
+        for h in range(2):
+            query = jnp.where(head_lanes(h, QB), mix[here, :PAIR], jnp.zeros((), BF))
+            top = None
+            for kb in range(qb + 1):
+                keys = slice(kb * QB, (kb + 1) * QB)
+                scores = scores_of(mix[keys, PAIR : 2 * PAIR], query, kb == qb)
+                work[h, keys, :] = scores
+                peak = jnp.max(scores, axis=0, keepdims=True)
+                top = peak if top is None else jnp.maximum(top, peak)
+            total = None
+            for kb in range(qb + 1):
+                keys = slice(kb * QB, (kb + 1) * QB)
+                grown = jnp.exp(work[h, keys, :] - top)
+                part = jnp.sum(grown, axis=0, keepdims=True)
+                total = part if total is None else total + part
+                low_work[h, keys, :] = grown.astype(BF)
+            count = (qb + 1) * QB
+            lanes = slice(h * HEAD_DIM, (h + 1) * HEAD_DIM)
+            out = mm(value_t[lanes, :count], low_work[h, :count, :])
+            outs.append(out / total)
+            lse[h * 4 + qb : h * 4 + qb + 1, :] = top + jnp.log(total)
+        att[here, :] = jnp.concatenate(outs, axis=0).T.astype(BF)
+
+
+def attend_back(mix, key_t, dout, lse, gmix, grad_k, grad_v, work, more, low_work, low_more):
+    key_t[...] = mix[:, PAIR : 2 * PAIR].astype(F32).T.astype(BF)
+    grad_k[...] = jnp.zeros_like(grad_k)
+    grad_v[...] = jnp.zeros_like(grad_v)
+    for qb in range(LENGTH // QB):
+        here = slice(qb * QB, (qb + 1) * QB)
+        outs = []
+        count = (qb + 1) * QB
+        for h in range(2):
+            lanes = head_lanes(h, QB)
+            query = jnp.where(lanes, mix[here, :PAIR], jnp.zeros((), BF))
+            grad = jnp.where(lanes, dout[here, :], jnp.zeros((), BF))
+            level = lse[h * 4 + qb : h * 4 + qb + 1, :]
+            delta = None
+            for kb in range(qb + 1):
+                keys = slice(kb * QB, (kb + 1) * QB)
+                probs = jnp.exp(scores_of(mix[keys, PAIR : 2 * PAIR], query, kb == qb) - level)
+                grad_probs = mm(mix[keys, 2 * PAIR :], grad, NT)
+                part = jnp.sum(probs * grad_probs, axis=0, keepdims=True)
+                delta = part if delta is None else delta + part
+                work[h, keys, :] = probs
+                more[h, keys, :] = grad_probs
+                low_work[h, keys, :] = probs.astype(BF)
+            for kb in range(qb + 1):
+                keys = slice(kb * QB, (kb + 1) * QB)
+                low_more[h, keys, :] = (work[h, keys, :] * (more[h, keys, :] - delta)).astype(BF)
+            grad_v[:count, :] += mm(low_work[h, :count, :], grad)
+            grad_k[:count, :] += mm(low_more[h, :count, :], query)
+            rows = slice(h * HEAD_DIM, (h + 1) * HEAD_DIM)
+            outs.append(mm(key_t[rows, :count], low_more[h, :count, :]) * 0.125)
+        gmix[here, :PAIR] = jnp.concatenate(outs, axis=0).T.astype(BF)
+    gmix[:, PAIR : 2 * PAIR] = (grad_k[...] * 0.125).astype(BF)
+    gmix[:, 2 * PAIR :] = grad_v[...].astype(BF)
+
+
+gelu_scale = 0.7978845608028654
+gelu_cubic = 0.044715
+
+
+def gelu_pair(x):
+    square = x * x
+    bent = jnp.tanh(gelu_scale * x * (1.0 + gelu_cubic * square))
+    half = 0.5 * (1.0 + bent)
+    slope = half + 0.5 * x * (1.0 - bent * bent) * (gelu_scale * (1.0 + 3.0 * gelu_cubic * square))
+    return x * half, slope
+
+
+SCRATCH = dict(
+    parts=((NB, SMALL_ROWS, SHARD), F32),
+    qv_rows=((16, PAIR), F32),
+    wpair=((WIDTH, 3 * PAIR), BF),
+    wfull=((WIDTH, 3 * WIDTH), BF),
+    wproj_all=((WIDTH, WIDTH), BF),
+    wfc_mine=((WIDTH, WIDTH), BF),
+    wout_mine=((WIDTH, WIDTH), BF),
+    g_all=((NB * ROWS, WIDTH), BF),
+    hat_one=((ROWS, WIDTH), F32),
+    scale_one=((ROWS, 1), F32),
+    n_one=((LENGTH, WIDTH), BF),
+    mix=((LENGTH, 3 * PAIR), BF),
+    turned=((PAIR, LENGTH), BF),
+    att=((LENGTH, PAIR), BF),
+    lse=((8, QB), F32),
+    work=((2, LENGTH, QB), F32),
+    more=((2, LENGTH, QB), F32),
+    low_work=((2, LENGTH, QB), BF),
+    low_more=((2, LENGTH, QB), BF),
+    att_own=((ROWS, WIDTH), BF),
+    middle=((ROWS, WIDTH), F32),
+    hat_two=((ROWS, WIDTH), F32),
+    scale_two=((ROWS, 1), F32),
+    n_two=((NB * ROWS, WIDTH), BF),
+    hidden=((NB * ROWS, WIDTH), BF),
+    grad_pre=((NB * ROWS, WIDTH), BF),
+    p_norm=((NB * ROWS, WIDTH), BF),
+    p_norm_box=((3, ROWS, WIDTH), BF),
+    p_layer=((NB * ROWS, WIDTH), BF),
+    p_layer_box=((3, ROWS, WIDTH), BF),
+    p_out=((WIDTH, WIDTH), BF),
+    out_beside=((4, ROWS, WIDTH), BF),
+    out_up=((4, ROWS, WIDTH), BF),
+    out_down=((4, ROWS, WIDTH), BF),
+    out_block=((ROWS, WIDTH), BF),
+    p_fc=((NB, NC, 32, WIDTH), BF),
+    fc_beside=((4, NB, 32, WIDTH), BF),
+    fc_up=((4, NB, 32, WIDTH), BF),
+    fc_down=((4, NB, 32, WIDTH), BF),
+    fc_sum=((NB, 32, WIDTH), BF),
+    fc_block=((32, FF), BF),
+    p_proj=((WIDTH, WIDTH), BF),
+    p_proj_box=((3, SHARD, WIDTH), BF),
+    proj_sum=((SHARD, WIDTH), BF),
+    proj_beside=((4, 32, WIDTH), BF),
+    proj_up=((4, 32, WIDTH), BF),
+    proj_down=((4, 32, WIDTH), BF),
+    proj_block=((32, WIDTH), BF),
+    grad_middle=((ROWS, WIDTH), F32),
+    branch=((ROWS, WIDTH), BF),
+    g_att=((ROWS, WIDTH), BF),
+    dout=((LENGTH, PAIR), BF),
+    gmix=((LENGTH, 3 * PAIR), BF),
+    grad_k=((LENGTH, PAIR), F32),
+    grad_v=((LENGTH, PAIR), F32),
+    gmix_own=((ROWS, 3 * WIDTH), BF),
+    p_qkv=((WIDTH, 3 * PAIR), BF),
+    p_qkv_box=((3, SHARD, 3 * PAIR), BF),
+    qkv_block=((SHARD, 3 * PAIR), BF),
+    gn_one=((ROWS, WIDTH), F32),
+    gs=((NB, SMALL_ROWS, SHARD), F32),
+    gqv=((16, PAIR), F32),
+    gs_box=((NB, SMALL_ROWS, SHARD), F32),
+    gs_sum=((SMALL_ROWS, SHARD), F32),
+    gs_far=((NC, SMALL_ROWS, SHARD), F32),
+)
+SENDS, RECVS, LOCALS = 320, 400, 24
+
+
+def layer_kernel(
+    tokens, cotangent, small, wqkv, wproj, wfc, wout,
+    layer_out, grad_tokens, grad_small, o_qkv, o_proj, o_fc, o_out,
+    *scratch, stop=99,
+):
+    s = SimpleNamespace(**dict(zip(SCRATCH, scratch)))
+    send_sems, recv_sems, local_sems = scratch[len(SCRATCH) :]
+    b, c = lax.axis_index("batch"), lax.axis_index("ctx")
+    net = Net(b, c, send_sems, recv_sems)
+    locals_open = []
+
+    def local(src, dst):
+        copy = pltpu.make_async_copy(src, dst, local_sems.at[len(locals_open)])
+        copy.start()
+        locals_open.append(copy)
+        return copy
+
+    def own(ref, size):
+        return rows_of(ref, size)(b)
+
+    def cols(ref, start):
+        return ref.at[:, pl.ds(pl.multiple_of(start, 128), PAIR)]
+
+    get_pair = [
+        local(cols(wqkv, t * WIDTH + c * PAIR), own(s.wpair, SHARD).at[:, t * PAIR : (t + 1) * PAIR])
+        for t in range(3)
+    ]
+    get_proj = local(wproj, own(s.wproj_all, SHARD))
+    get_fc = local(wfc.at[:, pl.ds(pl.multiple_of(b * WIDTH, WIDTH), WIDTH)], own(s.wfc_mine, SHARD))
+    get_out = local(wout, s.wout_mine)
+    get_full = local(wqkv, own(s.wfull, SHARD))
+    get_g = local(cotangent, own(s.g_all, ROWS))
+
+    barrier = pltpu.get_barrier_semaphore()
+    others = [(lax.rem(b + i, NB), c) for i in range(1, NB)]
+    others += [(b, lax.rem(c + i, NC)) for i in range(1, NC)]
+    for device in others:
+        pl.semaphore_signal(barrier, inc=1, device_id=device, device_id_type=MESH)
+    pl.semaphore_wait(barrier, len(others))
+
+    small_slots, pair_slots, fc_slots = net.slots(NB), net.slots(NB * 3), net.slots(NB)
+    for i in range(1, NB):
+        j = lax.rem(b + i, NB)
+        net.send(small, s.parts.at[b], (j, c), small_slots + b)
+    for i in range(1, NB):
+        j = lax.rem(b + i, NB)
+        for t in range(3):
+            net.send(
+                cols(wqkv, t * WIDTH + c * PAIR),
+                own(s.wpair, SHARD).at[:, t * PAIR : (t + 1) * PAIR],
+                (j, c),
+                pair_slots + b * 3 + t,
+            )
+
+    scale, hat = s.scale_one, s.hat_one
+
+    def norm_rows(i, carry):
+        at = pl.ds(pl.multiple_of(i * 32, 32), 32)
+        hat[at, :], scale[at, :] = normalise(tokens[at, :].astype(F32))
+        return carry
+
+    lax.fori_loop(0, ROWS // 32, norm_rows, 0)
+    s.parts[pl.ds(b, 1)] = small[...][None]
+    for i in range(1, NB):
+        j = lax.rem(b + i, NB)
+        net.wait(small_slots + j, s.parts.at[j])
+    gain, bias = row_of(s.parts, 0), row_of(s.parts, 1)
+    n_mine = rows_of(s.n_one, ROWS)(c)
+
+    def gain_rows(i, carry):
+        at = pl.ds(pl.multiple_of(i * 32, 32), 32)
+        n_mine[at, :] = (hat[at, :] * gain + bias).astype(BF)
+        return carry
+
+    lax.fori_loop(0, ROWS // 32, gain_rows, 0)
+    gather_one = GatherCtx(net, lambda j: [rows_of(s.n_one, ROWS)(j)], 1)
+    gather_one.start([n_mine])
+    gather_g = GatherBatch(net, lambda j: [rows_of(s.g_all, ROWS)(j)])
+    gather_g.start([cotangent])
+    gather_proj = GatherBatch(net, lambda j: [rows_of(s.wproj_all, SHARD)(j)])
+    gather_proj.start([wproj])
+    for p in range(NC):
+        at = p * PAIR
+        row, lane = 2 + (at % 512) // SHARD, at % SHARD
+        s.qv_rows[p : p + 1, :] = s.parts[at // 512, row : row + 1, lane : lane + PAIR]
+        s.qv_rows[8 + p : 9 + p, :] = s.parts[2 + at // 512, row : row + 1, lane : lane + PAIR]
+    gather_one.stage(1)
+    for i in range(1, NB):
+        j = lax.rem(b + i, NB)
+        net.send(
+            wfc.at[:, pl.ds(pl.multiple_of(j * WIDTH, WIDTH), WIDTH)],
+            own(s.wfc_mine, SHARD),
+            (j, c),
+            fc_slots + b,
+        )
+    gather_one.stage(2)
+    gather_g.relay()
+    gather_one.stage(3)
+    gather_one.finish()
+    for copy in get_pair:
+        copy.wait()
+    for i in range(1, NB):
+        j = lax.rem(b + i, NB)
+        for t in range(3):
+            net.wait(pair_slots + j * 3 + t, rows_of(s.wpair, SHARD)(j).at[:, t * PAIR : (t + 1) * PAIR])
+    mix_bias = jnp.concatenate(
+        [s.qv_rows[pl.ds(c, 1), :], jnp.zeros((1, PAIR), F32), s.qv_rows[pl.ds(8 + c, 1), :]], axis=1
+    )
+
+    def mix_rows(i, carry):
+        at = pl.ds(pl.multiple_of(i * QB, QB), QB)
+        s.mix[at, :] = (mm(s.n_one[at, :], s.wpair[...]) + mix_bias).astype(BF)
+        return carry
+
+    lax.fori_loop(0, LENGTH // QB, mix_rows, 0)
+    gather_proj.relay()
+
+    attend(s.mix, s.turned, s.att, s.lse, s.work, s.low_work)
+    swap_att = SwapCtx(
+        net, lambda j: [rows_of(s.att, ROWS)(j)], lambda j: [cols(s.att_own, j * PAIR)], 1
+    )
+    swap_att.start()
+    get_proj.wait()
+    gather_proj.finish()
+    swap_att.finish()
+    proj_bias = row_of(s.parts, 4)
+
+    def middle_cols(i, carry):
+        at = pl.ds(pl.multiple_of(i * 256, 256), 256)
+        s.middle[:, at] = mm(s.att_own[...], s.wproj_all[:, at]) + tokens[:, at].astype(F32)
+        return carry
+
+    lax.fori_loop(0, WIDTH // 256, middle_cols, 0)
+    gain_two, bias_two = row_of(s.parts, 5), row_of(s.parts, 6)
+    n_two_mine = own(s.n_two, ROWS)
+
+    def norm_two_rows(i, carry):
+        at = pl.ds(pl.multiple_of(i * 32, 32), 32)
+        middle = s.middle[at, :] + proj_bias
+        s.middle[at, :] = middle
+        norm, width = normalise(middle)
+        s.hat_two[at, :], s.scale_two[at, :] = norm, width
+        n_two_mine[at, :] = (norm * gain_two + bias_two).astype(BF)
+        return carry
+
+    lax.fori_loop(0, ROWS // 32, norm_two_rows, 0)
+
+    def halves(ref, j):
+        block = rows_of(ref, ROWS)(j)
+        return [block.at[0:64], block.at[64:128]]
+
+    gather_two = GatherBatch(net, lambda j: halves(s.n_two, j), 2)
+    gather_two.start(halves(s.n_two, b))
+    gather_two.relay()
+    for copy in (get_fc, get_out, get_g, get_full):
+        copy.wait()
+    gather_g.finish()
+    for i in range(1, NB):
+        j = lax.rem(b + i, NB)
+        net.wait(fc_slots + j, rows_of(s.wfc_mine, SHARD)(j))
+    gather_two.finish()
+
+    s.gs[...] = jnp.zeros_like(s.gs)
+    for n in range(4):
+        at = slice(n * 256, (n + 1) * 256)
+        pre = mm(s.n_two[...], s.wfc_mine[:, at]) + small[7 + n : 8 + n, :]
+        value, slope = gelu_pair(pre)
+        s.hidden[:, at] = value.astype(BF)
+        grad = (mm(s.g_all[...], s.wout_mine[at, :], NT) * slope).astype(BF)
+        s.grad_pre[:, at] = grad
+        s.gs[pl.ds(b, 1), 7 + n : 8 + n, :] = jnp.sum(grad.astype(F32), 0, keepdims=True)[None]
+
+    reduce_out = ReduceCtx(net, rows_of(s.p_out, ROWS), s.out_beside, s.out_up, s.out_down)
+
+    def out_rows(i, carry):
+        at = pl.ds(pl.multiple_of(i * 256, 256), 256)
+        s.p_out[at, :] = mm(s.hidden[:, at], s.g_all[...], TN).astype(BF)
+        return carry
+
+    lax.fori_loop(0, 4, out_rows, 0)
+    reduce_out.start()
+
+    reduce_norm = ReduceBatch(net, rows_of(s.p_norm, ROWS), s.p_norm_box)
+
+    def norm_block(j):
+        at = pl.ds(pl.multiple_of(j * ROWS, ROWS), ROWS)
+        s.p_norm[at, :] = mm(s.grad_pre[at, :], s.wfc_mine[...], NT).astype(BF)
+
+    norm_block(net.diag)
+    reduce_norm.give()
+    norm_block(net.across)
+    reduce_norm.cross()
+    norm_block(net.sib)
+    reduce_norm.keep()
+    norm_block(b)
+    reduce_fc = ReduceCtx(net, lambda j: s.p_fc.at[:, j], s.fc_beside, s.fc_up, s.fc_down)
+
+    def fc_rows(i, carry):
+        at = pl.ds(pl.multiple_of(i * 256, 256), 256)
+        s.p_fc[pl.ds(i, 1)] = (
+            mm(s.n_two[:, at], s.grad_pre[...], TN).astype(BF).reshape(1, NC, 32, WIDTH)
+        )
+        return carry
+
+    lax.fori_loop(0, 4, fc_rows, 0)
+    terms = reduce_norm.finish()
+    g_mine = own(s.g_all, ROWS)
+    grad_gain, grad_bias, sum_branch, sum_g = [jnp.zeros((1, WIDTH), F32)] * 4
+
+    def back_rows(i, carry):
+        at = pl.ds(pl.multiple_of(i * 32, 32), 32)
+        grad_gain, grad_bias, sum_branch, sum_g = carry
+        grad = terms[0][at, :].astype(F32) + terms[1][at, :].astype(F32) + terms[2][at, :].astype(F32)
+        norm = s.hat_two[at, :]
+        scaled = grad * gain_two
+        inner = scaled - jnp.mean(scaled, -1, keepdims=True)
+        inner = inner - norm * jnp.mean(scaled * norm, -1, keepdims=True)
+        g = g_mine[at, :].astype(F32)
+        total = g + s.scale_two[at, :] * inner
+        s.grad_middle[at, :] = total
+        low = total.astype(BF)
+        s.branch[at, :] = low
+        return (
+            grad_gain + jnp.sum(grad * norm, 0, keepdims=True),
+            grad_bias + jnp.sum(grad, 0, keepdims=True),
+            sum_branch + jnp.sum(low.astype(F32), 0, keepdims=True),
+            sum_g + jnp.sum(g, 0, keepdims=True),
+        )
+
+    sums = lax.fori_loop(0, ROWS // 32, back_rows, (grad_gain, grad_bias, sum_branch, sum_g))
+    put_row(s.gs, 5, sums[0])
+    put_row(s.gs, 6, sums[1])
+    put_row(s.gs, 4, sums[2])
+    put_row(s.gs, 11, sums[3])
+
+    def att_cols(i, carry):
+        at = pl.ds(pl.multiple_of(i * 256, 256), 256)
+        s.g_att[:, at] = mm(s.branch[...], s.wproj_all[at, :], NT).astype(BF)
+        return carry
+
+    lax.fori_loop(0, 4, att_cols, 0)
+    swap_grad = SwapCtx(
+        net, lambda j: [cols(s.g_att, j * PAIR)], lambda j: [rows_of(s.dout, ROWS)(j)], 1
+    )
+    swap_grad.start()
+
+    reduce_layer = ReduceBatch(net, rows_of(s.p_layer, ROWS), s.p_layer_box)
+
+    def layer_block(j):
+        at = pl.ds(pl.multiple_of(j * ROWS, ROWS), ROWS)
+        s.p_layer[at, :] = mm(s.hidden[at, :], s.wout_mine[...]).astype(BF)
+
+    layer_block(net.diag)
+    reduce_layer.give()
+    layer_block(net.across)
+    reduce_layer.cross()
+    layer_block(net.sib)
+    reduce_layer.keep()
+    layer_block(b)
+    reduce_proj = ReduceBatch(net, rows_of(s.p_proj, SHARD), s.p_proj_box)
+
+    def proj_rows(i, carry):
+        at = pl.ds(pl.multiple_of(i * 256, 256), 256)
+        s.p_proj[at, :] = mm(s.att_own[:, at], s.branch[...], TN).astype(BF)
+        return carry
+
+    lax.fori_loop(0, 4, proj_rows, 0)
+    reduce_proj.give()
+    reduce_proj.cross()
+    reduce_proj.keep()
+    gather_full = GatherBatch(net, lambda j: [rows_of(s.wfull, SHARD)(j)])
+    gather_full.start([wqkv])
+    swap_grad.finish()
+
+    attend_back(
+        s.mix, s.turned, s.dout, s.lse, s.gmix, s.grad_k, s.grad_v, s.work, s.more, s.low_work, s.low_more
+    )
+    swap_mix = SwapCtx(
+        net,
+        lambda j: [rows_of(s.gmix, ROWS)(j).at[:, t * PAIR : (t + 1) * PAIR] for t in range(3)],
+        lambda j: [cols(s.gmix_own, t * WIDTH + j * PAIR) for t in range(3)],
+        3,
+    )
+    swap_mix.start()
+    reduce_qkv = ReduceBatch(net, rows_of(s.p_qkv, SHARD), s.p_qkv_box)
+
+    def qkv_block(j):
+        at = pl.ds(pl.multiple_of(j * SHARD, SHARD), SHARD)
+        s.p_qkv[at, :] = mm(s.n_one[:, at], s.gmix[...], TN).astype(BF)
+
+    qkv_block(net.diag)
+    reduce_qkv.give()
+    qkv_block(net.across)
+    reduce_qkv.cross()
+    qkv_block(net.sib)
+    reduce_qkv.keep()
+    qkv_block(b)
+    s.gqv[...] = jnp.zeros_like(s.gqv)
+    s.gqv[pl.ds(c, 1), :] = jnp.sum(s.gmix[:, :PAIR].astype(F32), 0, keepdims=True)
+    s.gqv[pl.ds(8 + c, 1), :] = jnp.sum(s.gmix[:, 2 * PAIR :].astype(F32), 0, keepdims=True)
+    for p in range(NC):
+        at = p * PAIR
+        row, lane = 2 + (at % 512) // SHARD, at % SHARD
+        s.gs[at // 512, row : row + 1, lane : lane + PAIR] = s.gqv[p : p + 1, :]
+        s.gs[2 + at // 512, row : row + 1, lane : lane + PAIR] = s.gqv[8 + p : 9 + p, :]
+
+    reduce_out.stage(3)
+    reduce_out.stage(2)
+    reduce_out.stage(1)
+    reduce_out.finish(s.out_block)
+    gather_out = GatherCtx(net, lambda j: [rows_of(o_out, ROWS)(j)], 1)
+    gather_out.start([s.out_block])
+    keep_out = local(s.out_block, rows_of(o_out, ROWS)(c))
+    reduce_fc.start()
+    gather_full.relay()
+
+    layer_bias = row_of(s.parts, 11)
+    terms = reduce_layer.finish()
+
+    def layer_rows(i, carry):
+        at = pl.ds(pl.multiple_of(i * 32, 32), 32)
+        total = terms[0][at, :].astype(F32) + terms[1][at, :].astype(F32) + terms[2][at, :].astype(F32)
+        layer_out[at, :] = (s.middle[at, :] + total + layer_bias).astype(BF)
+        return carry
+
+    lax.fori_loop(0, ROWS // 32, layer_rows, 0)
+    terms = reduce_qkv.finish()
+    add_into(s.qkv_block, terms)
+    gather_qkv = GatherCtx(
+        net, lambda j: [cols(o_qkv, t * WIDTH + j * PAIR) for t in range(3)], 3
+    )
+    qkv_parts = [s.qkv_block.at[:, t * PAIR : (t + 1) * PAIR] for t in range(3)]
+    gather_qkv.start(qkv_parts)
+    keep_qkv = [local(one, cols(o_qkv, t * WIDTH + c * PAIR)) for t, one in enumerate(qkv_parts)]
+    add_into(s.proj_sum, reduce_proj.finish())
+    reduce_part = ReduceCtx(net, rows_of(s.proj_sum, 32), s.proj_beside, s.proj_up, s.proj_down)
+    reduce_part.start()
+
+    gather_full.finish()
+    swap_mix.finish()
+
+    def one_cols(i, carry):
+        at = pl.ds(pl.multiple_of(i * 256, 256), 256)
+        s.gn_one[:, at] = mm(s.gmix_own[...], s.wfull[at, :], NT)
+        return carry
+
+    lax.fori_loop(0, 4, one_cols, 0)
+
+    def token_rows(i, carry):
+        at = pl.ds(pl.multiple_of(i * 32, 32), 32)
+        grad_gain, grad_bias = carry
+        grad, norm = s.gn_one[at, :], s.hat_one[at, :]
+        scaled = grad * gain
+        inner = scaled - jnp.mean(scaled, -1, keepdims=True)
+        inner = inner - norm * jnp.mean(scaled * norm, -1, keepdims=True)
+        grad_tokens[at, :] = (s.grad_middle[at, :] + s.scale_one[at, :] * inner).astype(BF)
+        return (
+            grad_gain + jnp.sum(grad * norm, 0, keepdims=True),
+            grad_bias + jnp.sum(grad, 0, keepdims=True),
+        )
+
+    sums = lax.fori_loop(0, ROWS // 32, token_rows, (jnp.zeros((1, WIDTH), F32),) * 2)
+    put_row(s.gs, 0, sums[0])
+    put_row(s.gs, 1, sums[1])
+    gs_slots, far_slots = net.slots(NB), net.slots(NC)
+    for i in range(1, NB):
+        j = lax.rem(b + i, NB)
+        net.send(s.gs.at[j], s.gs_box.at[b], (j, c), gs_slots + b)
+
+    reduce_part.stage(3)
+    gather_out.stage(1)
+    reduce_part.stage(2)
+    reduce_fc.stage(3)
+    reduce_part.stage(1)
+    gather_out.stage(2)
+    reduce_part.finish(s.proj_block)
+    gather_part = GatherCtx(net, lambda j: [rows_of(o_proj, 32)(j)], 1)
+    gather_part.start([s.proj_block])
+    keep_part = local(s.proj_block, rows_of(o_proj, 32)(c))
+    reduce_fc.stage(2)
+    gather_out.stage(3)
+    reduce_fc.stage(1)
+    gather_qkv.stage(1)
+    reduce_fc.finish(s.fc_sum)
+    swap_slots = net.slots(NB)
+    for i in range(1, NB):
+        j = lax.rem(b + i, NB)
+        net.send(
+            s.fc_sum.at[j],
+            s.fc_block.at[:, pl.ds(pl.multiple_of(b * WIDTH, WIDTH), WIDTH)],
+            (j, c),
+            swap_slots + b,
+        )
+    at = pl.ds(pl.multiple_of(b * WIDTH, WIDTH), WIDTH)
+    s.fc_block[:, at] = s.fc_sum[pl.ds(b, 1)][0]
+    gather_qkv.stage(2)
+    total = s.gs[pl.ds(b, 1)][0]
+    for i in range(1, NB):
+        j = lax.rem(b + i, NB)
+        net.wait(gs_slots + j, s.gs_box.at[j])
+        total = total + s.gs_box[pl.ds(j, 1)][0]
+    s.gs_sum[...] = total
+    for i in range(1, NC):
+        j = lax.rem(c + i, NC)
+        net.send(s.gs_sum, s.gs_far.at[c], (b, j), far_slots + c)
+    for i in range(1, NB):
+        j = lax.rem(b + i, NB)
+        net.wait(swap_slots + j, s.fc_block.at[:, pl.ds(pl.multiple_of(j * WIDTH, WIDTH), WIDTH)])
+    gather_fc = GatherCtx(net, lambda j: [rows_of(o_fc, 32)(j)], 1)
+    gather_fc.start([s.fc_block])
+    keep_fc = local(s.fc_block, rows_of(o_fc, 32)(c))
+    gather_part.stage(1)
+    gather_qkv.stage(3)
+    gather_part.stage(2)
+    gather_part.stage(3)
+    for i in range(1, NC):
+        j = lax.rem(c - i + NC, NC)
+        net.wait(far_slots + j, s.gs_far.at[j])
+        total = total + s.gs_far[pl.ds(j, 1)][0]
+    grad_small[...] = total
+    gather_fc.stage(1)
+    gather_fc.stage(2)
+    gather_fc.stage(3)
+    for gather in (gather_out, gather_qkv, gather_part, gather_fc):
+        gather.finish()
+    for copy in [keep_out, keep_part, keep_fc] + keep_qkv:
+        copy.wait()
+    net.drain()
+
+
+def per_device_fast(
+    tokens, cotangent, ln1_gain, ln1_bias, qkv_weight, qv_bias, proj_weight, proj_bias,
+    ln2_gain, ln2_bias, fc_weight, fc_bias, out_weight, out_bias,
+):
+    small = jnp.concatenate(
+        [ln1_gain, ln1_bias, qv_bias, proj_bias, ln2_gain, ln2_bias, fc_bias, out_bias,
+         jnp.zeros((4 * SHARD,), BF)]
+    ).astype(F32).reshape(SMALL_ROWS, SHARD)
+    vmem, anywhere = pl.BlockSpec(memory_space=pltpu.VMEM), pl.BlockSpec(memory_space=pl.ANY)
+    shape = jax.ShapeDtypeStruct
+    layer, grad_in, grad_small, w_qkv, w_proj, w_fc, w_out = pl.pallas_call(
+        layer_kernel,
+        out_shape=(
+            shape((ROWS, WIDTH), BF),
+            shape((ROWS, WIDTH), BF),
+            shape((SMALL_ROWS, SHARD), F32),
+            shape((SHARD, 3 * WIDTH), BF),
+            shape((SHARD, WIDTH), BF),
+            shape((SHARD, FF), BF),
+            shape((FF // NB, WIDTH), BF),
+        ),
+        in_specs=[vmem, vmem, vmem, anywhere, anywhere, anywhere, anywhere],
+        out_specs=(vmem, vmem, vmem, anywhere, anywhere, anywhere, anywhere),
+        scratch_shapes=[pltpu.VMEM(*item) for item in SCRATCH.values()]
+        + [
+            pltpu.SemaphoreType.DMA((SENDS,)),
+            pltpu.SemaphoreType.DMA((RECVS,)),
+            pltpu.SemaphoreType.DMA((LOCALS,)),
+        ],
+        compiler_params=pltpu.CompilerParams(
+            collective_id=0, has_side_effects=True, vmem_limit_bytes=VMEM_BYTES
+        ),
+    )(
+        tokens.reshape(ROWS, WIDTH), cotangent.reshape(ROWS, WIDTH), small,
+        qkv_weight, proj_weight, fc_weight, out_weight,
+    )
+    flat = grad_small.reshape(-1)
+    sizes = [SHARD, SHARD, 2 * SHARD, SHARD, SHARD, SHARD, 4 * SHARD, SHARD]
+    smalls, at = [], 0
+    for size in sizes:
+        smalls.append(lax.slice(flat, (at,), (at + size,)))
+        at += size
+    return (
+        layer.reshape(tokens.shape),
+        grad_in.reshape(tokens.shape),
+        smalls[0],
+        smalls[1],
+        w_qkv.astype(F32),
+        smalls[2],
+        w_proj.astype(F32),
+        smalls[3],
+        smalls[4],
+        smalls[5],
+        w_fc.astype(F32),
+        smalls[6],
+        w_out.astype(F32),
+        smalls[7],
+    )
+
+
+VMEM_BYTES = 62 * 1024 * 1024
+
+
 def solution(mesh):
     placed = (
         P("batch", "ctx", None),
@@ -366,8 +1326,9 @@
         P("batch", None),
         P("batch"),
     )
+    fits = dict(mesh.shape) == {"batch": NB, "ctx": NC}
     return jax.shard_map(
-        per_device,
+        per_device_fast if fits else per_device,
         mesh=mesh,
         in_specs=placed,
         out_specs=(

time: 1270 us -> 275 us (0.22)
  blocking collectives: 541 us -> 0 us
  waiting for transfers between devices: 452 us -> 0 us
  Pallas kernels: 0 us -> 251 us
  starting transfers between devices: 136 us -> 0 us
  matrix products: 68.4 us -> 0 us
  other arithmetic: 26 us -> 9.83 us
  between operations: 16.5 us -> 0.68 us
    psum x1 -> x0, blocking collectives: 488 us -> none  [per_device(): lax.psum((partial_grads[0], partial_grads[1], partial_grads[2], partial_g...]
    pallas_call x0 -> x1, Pallas kernels: none -> 251 us  [per_device_fast(): pl.pallas_call(layer_kernel, out_shape=(shape((ROWS, WIDTH), BF), shape((...]
    all_gather x6 -> x0, waiting for transfers between devices: 222 us -> none  [the longest x1 57.4 us: per_device(): lax.all_gather(fc_weight, 'batch', axis=0, tiled=True)]
    reduce_scatter x4 -> x0, waiting for transfers between devices: 166 us -> none  [the longest x1 74.3 us: per_device(): lax.psum_scatter(local_grads[10].astype(jnp.bfloat16), 'batch', scatter_d...]
    ppermute x32 -> x0, starting transfers between devices: 135 us -> none  [the longest x16 78.6 us: shifted(): return lax.ppermute(block, axis, route)]
    dot_general x19 -> x0, matrix products: 68.4 us -> none  [the longest x1 8.29 us: per_device(): jnp.einsum('rf,rd->fd', hidden_low, grad_out, preferred_element_type=jnp....]
    ppermute x32 -> x0, waiting for transfers between devices: 60.9 us -> none  [the longest x16 38.4 us: from_behind(): return lax.ppermute(block, axis, route)]
    all_gather x8 -> x0, blocking collectives: 41.9 us -> none  [the longest x1 5.99 us: per_device(): lax.all_gather(ln1_bias, 'batch', axis=0, tiled=True)]
  transfers between devices with their start and end apart: 42 -> 0, of which waited for: 31 -> 0; matrix products, arithmetic and copies ran while one was open for 8% -> 0% of each run, Pallas kernels for 0% -> 0%
where the time goes in v1:
time: 275 us
  Pallas kernels  251 us (91%)
  local copies, waits for them, and re-layouts  12.8 us (5%)
  other arithmetic  9.83 us (4%)
    pallas_call x1, Pallas kernels, per_device_fast(): pl.pallas_call(layer_kernel, out_shape=(shape((ROWS, WIDTH), BF), shape((...  251 us
    unnamed x24, local copies, waits for them, and re-layouts  10.8 us

profile of v1, /device:TPU:0, one launch (start us, length us, event | category | flops | bytes accessed | tf_op | source)
XLA Modules:
  0.0 274.6 jit_solution(6707013850905237575)
XLA Ops:
  0.7 0.9 dynamic-update-slice
  1.5 0.8 dynamic-update-slice.1
  2.3 0.9 dynamic-update-slice.2
  3.2 0.8 dynamic-update-slice.3
  4.0 0.8 dynamic-update-slice.4
  4.9 0.8 dynamic-update-slice.5
  5.7 0.8 dynamic-update-slice.6
  6.6 0.8 dynamic-update-slice.7
  7.4 0.6 reshape.57.small
  8.0 251.3 %shard_map.245 = (bf16[128,1024]{1,0:T(8,128)(2,1)}, bf16[128,1024]{1,0:T(8,128)(2,1)}, f32[16,256]{1,0:T(8,128)}, bf16[256,3072]{1,0:T(8,128)(2,1)}, bf16[256,1...) custom-call(bf16[128,1024]{1,0:T(8,128)(2,1)} %bitcast.18, bf16[128,1024]{1,0:T(8,128)(2,1)} %bitcast.19, ...), custom_call_target="tpu_custom_call" | custom-call | tf_op jit(solution)/shard_map/pallas_call | solution.py:1259
  259.3 1.5 fusion
  260.8 0.7 slice_bitcast_fusion
  261.5 0.6 copy.29
  262.1 0.7 slice_bitcast_fusion.1
  262.8 0.6 copy.28
  263.4 0.0 copy-start
  263.4 4.2 %convert_element_type.23 = f32[256,4096]{1,0:T(8,128)} convert(bf16[256,4096]{1,0:T(8,128)(2,1)} %get-tuple-element.26) | non-fusion elementwise | flops 1048576 | bytes 6291456 | tf_op jit(solution)/shard_map/convert_element_type | solution.py:1302
  267.6 0.0 copy-done
  267.6 0.0 copy-start.1
  267.6 2.5 convert_element_type.24
  270.1 0.0 copy-done.1
  270.1 0.0 copy-start.2
  270.1 0.0 copy-start.4
  270.1 2.0 convert_element_type.21
  272.1 0.0 copy-start.3
  272.1 0.0 copy-done.2
  272.1 1.1 convert_element_type.22
  273.2 0.0 copy-done.4
  273.2 0.7 copy.41
  273.9 0.0 copy-done.3
  273.9 0.7 copy.42
  (2 shorter events, 0.0 us)
Async XLA Ops:
  263.4 4.3 %copy-start = (bf16[1024,1024]{1,0:T(8,128)(2,1)S(1)}, bf16[1024,1024]{1,0:T(8,128)(2,1)}, u32[]{:S(2)}) copy-start(bf16[1024,1024]{1,0:T(8,128)(2,1)} %get-tuple-element.27) | copy-start | bytes 6291460
  267.6 2.5 copy-start.1
  270.1 2.0 copy-start.2
  270.1 3.1 %copy-start.4 = (bf16[128,1024]{1,0:T(8,128)(2,1)S(1)}, bf16[128,1024]{1,0:T(8,128)(2,1)}, u32[]{:S(2)}) copy-start(bf16[128,1024]{1,0:T(8,128)(2,1)} %get-tuple-element.21) | copy-start | bytes 786436
  272.1 1.8 copy-start.3

commit v2 on v1

--- a/solution.py
+++ b/solution.py
@@ -378,6 +378,18 @@
     return two if one is None else (one if two is None else jnp.logical_and(one, two))
 
 
+class Marks:
+    def __init__(self):
+        self.scope = None
+
+    def __call__(self, name):
+        if self.scope is not None:
+            self.scope.__exit__(None, None, None)
+        self.scope = None if name is None else jax.named_scope(name)
+        if self.scope is not None:
+            self.scope.__enter__()
+
+
 class Net:
     def __init__(self, b, c, send_sems, recv_sems):
         self.b, self.c, self.z, self.x = b, c, c // 2, c % 2
@@ -387,7 +399,7 @@
         self.across = lax.rem(b + 2, NB)
         self.diag = lax.rem(self.sib + 2, NB)
         self.send_sems, self.recv_sems = send_sems, recv_sems
-        self.sent, self.taken, self.pending = 0, 0, []
+        self.taken, self.pending = 0, []
 
     def slots(self, count):
         base = self.taken
@@ -396,18 +408,20 @@
         return base
 
     def send(self, src, dst, device, slot, when=None):
-        assert self.sent < self.send_sems.shape[0]
+        index = len(self.pending)
+        if index == self.send_sems.shape[0]:
+            done, copy, index = self.pending.pop(0)
+            run(done, copy.wait_send)
         copy = pltpu.make_async_remote_copy(
             src_ref=src,
             dst_ref=dst,
-            send_sem=self.send_sems.at[self.sent],
+            send_sem=self.send_sems.at[index],
             recv_sem=self.recv_sems.at[slot],
             device_id=device,
             device_id_type=MESH,
         )
-        self.sent += 1
         run(when, copy.start)
-        self.pending.append((when, copy))
+        self.pending.append((when, copy, index))
 
     def wait(self, slot, ref):
         pltpu.make_async_remote_copy(
@@ -420,34 +434,26 @@
         ).wait_recv()
 
     def drain(self):
-        for when, copy in self.pending:
+        for when, copy, _ in self.pending:
             run(when, copy.wait_send)
 
 
 class GatherCtx:
-    def __init__(self, net, views, count):
-        self.net, self.views, self.count = net, views, count
+    def __init__(self, net, views, count, turn=False):
+        self.net, self.views, self.count, self.turn = net, views, count, turn
         self.along, self.beside = net.slots(4 * count), net.slots(4 * count)
-
-    def hand_on(self, zz, srcs, up, down):
+        self.turned = net.slots(2) if turn else None
+
+    def begin(self, i, src):
         net, count = self.net, self.count
-        dsts = self.views(2 * zz + net.x)
-        for i in range(count):
-            if up is not False:
-                net.send(srcs[i], dsts[i], (net.b, net.c + 2), self.along + zz * count + i, up)
-            if down is not False:
-                net.send(srcs[i], dsts[i], (net.b, net.c - 2), self.along + zz * count + i, down)
-
-    def beside_send(self, zz, srcs, when):
-        net, count = self.net, self.count
-        dsts = self.views(2 * zz + net.x)
-        for i in range(count):
-            net.send(srcs[i], dsts[i], (net.b, net.side), self.beside + zz * count + i, when)
+        dst, at = self.views(net.c)[i], net.z * count + i
+        net.send(src, dst, (net.b, net.side), self.beside + at)
+        net.send(src, dst, (net.b, net.c + 2), self.along + at, net.z < 3)
+        net.send(src, dst, (net.b, net.c - 2), self.along + at, net.z > 0)
 
     def start(self, srcs):
-        net = self.net
-        self.hand_on(net.z, srcs, net.z < 3, net.z > 0)
-        self.beside_send(net.z, srcs, None)
+        for i, src in enumerate(srcs):
+            self.begin(i, src)
 
     def stage(self, d):
         net, count = self.net, self.count
@@ -455,25 +461,48 @@
             zz = net.z + sign * d
             here = zz >= 0 if sign < 0 else zz <= 3
             refs = self.views(2 * zz + net.x)
-
-            def arrive(refs=refs, zz=zz):
-                for i in range(count):
-                    net.wait(self.along + zz * count + i, refs[i])
-
-            pl.when(here)(arrive)
+            onward = both(here, net.z < 3 if sign < 0 else net.z > 0)
+            dsts = self.views(2 * zz + net.x)
+            for i in range(count):
+                slot = self.along + zz * count + i
+                pl.when(here)(lambda slot=slot, ref=refs[i]: net.wait(slot, ref))
+                if d < 3:
+                    net.send(refs[i], dsts[i], (net.b, net.c - 2 * sign), slot, onward)
+                goes = here
+                if self.turn and i == count - 1:
+                    goes = both(here, jnp.logical_and(zz > 0, zz < 3))
+                net.send(refs[i], dsts[i], (net.b, net.side), self.beside + zz * count + i, goes)
+        if self.turn:
+            if d == 1:
+                self.corner()
+            self.pass_on(d)
+
+    def piece(self, end):
+        return self.views(2 * end + 1 - self.net.x)[self.count - 1]
+
+    def corner(self):
+        net, count = self.net, self.count
+        for end, step in ((0, 2), (3, -2)):
+            ref, slot = self.piece(end), self.beside + end * count + count - 1
+            pl.when(net.z == end)(lambda slot=slot, ref=ref: net.wait(slot, ref))
+            net.send(ref, ref, (net.b, net.c + step), self.turned + (end > 0), net.z == end)
+
+    def pass_on(self, d):
+        net = self.net
+        for end, step in ((0, 2), (3, -2)):
+            here = net.z == (end + d if end == 0 else end - d)
+            ref, slot = self.piece(end), self.turned + (end > 0)
+            pl.when(here)(lambda slot=slot, ref=ref: net.wait(slot, ref))
             if d < 3:
-                if sign < 0:
-                    self.hand_on(zz, refs, both(here, net.z < 3), False)
-                else:
-                    self.hand_on(zz, refs, False, both(here, net.z > 0))
-            self.beside_send(zz, refs, here)
+                net.send(ref, ref, (net.b, net.c + step), slot, here)
 
     def finish(self):
         net, count = self.net, self.count
         for zz in range(4):
             refs = self.views(2 * zz + 1 - net.x)
             for i in range(count):
-                net.wait(self.beside + zz * count + i, refs[i])
+                if not (self.turn and i == count - 1 and zz in (0, 3)):
+                    net.wait(self.beside + zz * count + i, refs[i])
 
 
 def chunks(ref):
@@ -496,45 +525,46 @@
     lax.fori_loop(0, count, body, 0)
 
 
-class ReduceCtx:
-    def __init__(self, net, mine, beside, up, down):
-        self.net, self.mine, self.beside, self.up, self.down = net, mine, beside, up, down
-        self.s_beside, self.s_up, self.s_down = net.slots(4), net.slots(4), net.slots(4)
-
-    def start(self, order=(3, 0, 2, 1)):
+class ReduceLine:
+    def __init__(self, net, mine, up, down):
+        self.net, self.mine, self.up, self.down = net, mine, up, down
+        self.s_up, self.s_down = net.slots(4), net.slots(4)
+
+    def give(self, k, upward, when):
         net = self.net
-        for zz in order:
-            net.send(self.mine(2 * zz + 1 - net.x), self.beside.at[zz], (net.b, net.side), self.s_beside + zz)
-
-    def fold(self, zz):
-        net = self.net
-        net.wait(self.s_beside + zz, self.beside.at[zz])
-        add_into(self.mine(2 * zz + net.x), [self.mine(2 * zz + net.x), self.beside.at[zz]])
-
-    def stage(self, d):
-        net = self.net
-        for sign in (1, -1):
-            zz = net.z + sign * d
-            here = zz <= 3 if sign > 0 else zz >= 0
-            inner = net.z >= 1 if sign > 0 else net.z <= 2
-            box, slot = (self.up, self.s_up) if sign > 0 else (self.down, self.s_down)
-            mine = self.mine(2 * zz + net.x)
-
-            def work(zz=zz, inner=inner, box=box, slot=slot, mine=mine):
-                self.fold(zz)
-
-                @pl.when(inner)
-                def _():
-                    net.wait(slot + zz, box.at[zz])
-                    add_into(mine, [mine, box.at[zz]])
-
-            pl.when(here)(work)
-            net.send(mine, box.at[zz], (net.b, net.c + 2 * sign), slot + zz, here)
+        if upward:
+            net.send(self.mine(k), self.up.at[k], (net.b, net.c + 2), self.s_up + k, when)
+        else:
+            net.send(self.mine(k), self.down.at[k], (net.b, net.c - 2), self.s_down + k, when)
+
+    def take(self, k, upward, when):
+        box, slot = (self.up, self.s_up) if upward else (self.down, self.s_down)
+        mine = self.mine(k)
+
+        @pl.when(when)
+        def _():
+            self.net.wait(slot + k, box.at[k])
+            add_into(mine, [mine, box.at[k]])
+
+        self.give(k, upward, when)
+
+    def launch(self):
+        for k in (1, 2, 3):
+            self.give(4 - k, True, self.net.z == 0)
+            self.give(k - 1, False, self.net.z == 3)
+
+    def pass_one(self):
+        for k in (0, 1):
+            self.take(3 - k, True, self.net.z == 1)
+            self.take(k, False, self.net.z == 2)
+
+    def pass_two(self):
+        self.take(0, False, self.net.z == 1)
+        self.take(3, True, self.net.z == 2)
 
     def finish(self, target):
         net, z = self.net, self.net.z
-        net.wait(self.s_beside + z, self.beside.at[z])
-        mine, beside = self.mine(net.c), self.beside.at[z]
+        mine = self.mine(z)
 
         @pl.when(z >= 1)
         def _():
@@ -544,11 +574,30 @@
         def _():
             net.wait(self.s_down + z, self.down.at[z])
 
-        pl.when(z == 0)(lambda: add_into(target, [mine, beside, self.down.at[z]]))
-        pl.when(z == 3)(lambda: add_into(target, [mine, beside, self.up.at[z]]))
+        pl.when(z == 0)(lambda: add_into(target, [mine, self.down.at[z]]))
+        pl.when(z == 3)(lambda: add_into(target, [mine, self.up.at[z]]))
         pl.when(jnp.logical_and(z > 0, z < 3))(
-            lambda: add_into(target, [mine, beside, self.up.at[z], self.down.at[z]])
+            lambda: add_into(target, [mine, self.up.at[z], self.down.at[z]])
         )
+
+
+class ReduceCtx:
+    def __init__(self, net, mine, beside, up, down):
+        self.net, self.mine, self.beside = net, mine, beside
+        self.slots = net.slots(4)
+        self.line = ReduceLine(net, lambda k: mine(2 * k + net.x), up, down)
+
+    def start(self):
+        net = self.net
+        for k in (3, 0, 2, 1):
+            net.send(self.mine(2 * k + 1 - net.x), self.beside.at[k], (net.b, net.side), self.slots + k)
+
+    def fold(self):
+        for k in (3, 0, 2, 1):
+            self.net.wait(self.slots + k, self.beside.at[k])
+            mine = self.line.mine(k)
+            add_into(mine, [mine, self.beside.at[k]])
+        self.line.launch()
 
 
 class SwapCtx:
@@ -556,15 +605,20 @@
         self.net, self.src, self.dst, self.count = net, src, dst, count
         self.base = net.slots(NC * count)
 
+    def give(self, j):
+        net, count = self.net, self.count
+        srcs, dsts = self.src(j), self.dst(net.c)
+        for i in range(count):
+            net.send(srcs[i], dsts[i], (net.b, j), self.base + net.c * count + i, net.c != j)
+
+        @pl.when(net.c == j)
+        def _():
+            for one, two in zip(srcs, dsts):
+                two[...] = one[...]
+
     def start(self):
-        net, count = self.net, self.count
-        for step in range(1, NC):
-            j = lax.rem(net.c + step, NC)
-            srcs, dsts = self.src(j), self.dst(net.c)
-            for i in range(count):
-                net.send(srcs[i], dsts[i], (net.b, j), self.base + net.c * count + i)
-        for one, two in zip(self.src(net.c), self.dst(net.c)):
-            two[...] = one[...]
+        for j in range(NC):
+            self.give(j)
 
     def finish(self):
         net, count = self.net, self.count
@@ -573,6 +627,26 @@
             dsts = self.dst(j)
             for i in range(count):
                 net.wait(self.base + j * count + i, dsts[i])
+
+
+class GatherSide:
+    def __init__(self, net, views):
+        self.net, self.views = net, views
+        self.far, self.near = net.slots(NB), net.slots(NB)
+
+    def give(self, j, src):
+        net = self.net
+        net.send(src, self.views(j), (net.b, net.side), self.far + j)
+
+    def relay(self, j):
+        net, ref = self.net, self.views(j)
+        net.wait(self.far + j, ref)
+        net.send(ref, ref, (net.sib, net.c), self.near + j)
+
+    def finish(self):
+        net = self.net
+        for j in (net.sib, net.diag):
+            net.wait(self.near + j, self.views(j))
 
 
 class GatherBatch:
@@ -670,9 +744,9 @@
     return scores
 
 
-def attend(mix, value_t, att, lse, work, low_work):
+def attend(mix, value_t, att, lse, work, low_work, ready):
     value_t[...] = mix[:, 2 * PAIR :].astype(F32).T.astype(BF)
-    for qb in range(LENGTH // QB):
+    for qb in reversed(range(LENGTH // QB)):
         here = slice(qb * QB, (qb + 1) * QB)
         outs = []
         for h in range(2):
@@ -697,13 +771,14 @@
             outs.append(out / total)
             lse[h * 4 + qb : h * 4 + qb + 1, :] = top + jnp.log(total)
         att[here, :] = jnp.concatenate(outs, axis=0).T.astype(BF)
-
-
-def attend_back(mix, key_t, dout, lse, gmix, grad_k, grad_v, work, more, low_work, low_more):
+        ready(qb)
+
+
+def attend_back(mix, key_t, dout, lse, gmix, grad_k, grad_v, work, more, low_work, low_more, ready):
     key_t[...] = mix[:, PAIR : 2 * PAIR].astype(F32).T.astype(BF)
     grad_k[...] = jnp.zeros_like(grad_k)
     grad_v[...] = jnp.zeros_like(grad_v)
-    for qb in range(LENGTH // QB):
+    for qb in reversed(range(LENGTH // QB)):
         here = slice(qb * QB, (qb + 1) * QB)
         outs = []
         count = (qb + 1) * QB
@@ -730,8 +805,9 @@
             rows = slice(h * HEAD_DIM, (h + 1) * HEAD_DIM)
             outs.append(mm(key_t[rows, :count], low_more[h, :count, :]) * 0.125)
         gmix[here, :PAIR] = jnp.concatenate(outs, axis=0).T.astype(BF)
-    gmix[:, PAIR : 2 * PAIR] = (grad_k[...] * 0.125).astype(BF)
-    gmix[:, 2 * PAIR :] = grad_v[...].astype(BF)
+        gmix[here, PAIR : 2 * PAIR] = (grad_k[here, :] * 0.125).astype(BF)
+        gmix[here, 2 * PAIR :] = grad_v[here, :].astype(BF)
+        ready(qb)
 
 
 gelu_scale = 0.7978845608028654
@@ -747,6 +823,7 @@
 
 
 SCRATCH = dict(
+    small=((SMALL_ROWS, SHARD), F32),
     parts=((NB, SMALL_ROWS, SHARD), F32),
     qv_rows=((16, PAIR), F32),
     wpair=((WIDTH, 3 * PAIR), BF),
@@ -777,17 +854,19 @@
     p_norm_box=((3, ROWS, WIDTH), BF),
     p_layer=((NB * ROWS, WIDTH), BF),
     p_layer_box=((3, ROWS, WIDTH), BF),
-    p_out=((WIDTH, WIDTH), BF),
-    out_beside=((4, ROWS, WIDTH), BF),
-    out_up=((4, ROWS, WIDTH), BF),
-    out_down=((4, ROWS, WIDTH), BF),
+    g_side=((NB * ROWS, WIDTH), BF),
+    n_side=((NB * ROWS, WIDTH), BF),
+    hidden_side=((NB * ROWS, WIDTH // 2), BF),
+    pre_side=((NB * ROWS, WIDTH // 2), BF),
+    p_out=((2, 256, WIDTH), BF),
+    out_up=((2, 4, 64, WIDTH), BF),
+    out_down=((2, 4, 64, WIDTH), BF),
     out_block=((ROWS, WIDTH), BF),
-    p_fc=((NB, NC, 32, WIDTH), BF),
-    fc_beside=((4, NB, 32, WIDTH), BF),
-    fc_up=((4, NB, 32, WIDTH), BF),
-    fc_down=((4, NB, 32, WIDTH), BF),
-    fc_sum=((NB, 32, WIDTH), BF),
-    fc_block=((32, FF), BF),
+    p_fc=((2, NB, 4, 64, 256), BF),
+    fc_up=((2, 4, NB, 64, 256), BF),
+    fc_down=((2, 4, NB, 64, 256), BF),
+    fc_sum=((2, NB, 64, 256), BF),
+    fc_block=((64, FF // 2), BF),
     p_proj=((WIDTH, WIDTH), BF),
     p_proj_box=((3, SHARD, WIDTH), BF),
     proj_sum=((SHARD, WIDTH), BF),
@@ -802,7 +881,8 @@
     gmix=((LENGTH, 3 * PAIR), BF),
     grad_k=((LENGTH, PAIR), F32),
     grad_v=((LENGTH, PAIR), F32),
-    gmix_own=((ROWS, 3 * WIDTH), BF),
+    gmix_own=((NC, ROWS, 3 * PAIR), BF),
+    gmix_all=((ROWS, 3 * WIDTH), BF),
     p_qkv=((WIDTH, 3 * PAIR), BF),
     p_qkv_box=((3, SHARD, 3 * PAIR), BF),
     qkv_block=((SHARD, 3 * PAIR), BF),
@@ -813,18 +893,20 @@
     gs_sum=((SMALL_ROWS, SHARD), F32),
     gs_far=((NC, SMALL_ROWS, SHARD), F32),
 )
-SENDS, RECVS, LOCALS = 320, 400, 24
-
-
-def layer_kernel(
-    tokens, cotangent, small, wqkv, wproj, wfc, wout,
-    layer_out, grad_tokens, grad_small, o_qkv, o_proj, o_fc, o_out,
-    *scratch, stop=99,
-):
+SENDS, RECVS, LOCALS = 96, 248, 16
+
+
+def layer_kernel(*refs):
+    tokens, cotangent = refs[:2]
+    vectors = refs[2:10]
+    wqkv, wproj, wfc, wout = refs[10:14]
+    layer_out, grad_tokens, grad_small, o_qkv, o_proj, o_fc, o_out = refs[14:21]
+    scratch = refs[21:]
     s = SimpleNamespace(**dict(zip(SCRATCH, scratch)))
     send_sems, recv_sems, local_sems = scratch[len(SCRATCH) :]
     b, c = lax.axis_index("batch"), lax.axis_index("ctx")
     net = Net(b, c, send_sems, recv_sems)
+    mark = Marks()
     locals_open = []
 
     def local(src, dst):
@@ -836,32 +918,54 @@
     def own(ref, size):
         return rows_of(ref, size)(b)
 
-    def cols(ref, start):
-        return ref.at[:, pl.ds(pl.multiple_of(start, 128), PAIR)]
-
+    def cols(ref, start, count=PAIR):
+        return ref.at[:, pl.ds(pl.multiple_of(start, 128), count)]
+
+    def halves(ref, size, j):
+        block = rows_of(ref, size)(j)
+        return [block.at[0 : size // 2], block.at[size // 2 : size]]
+
+    mark("enter")
     get_pair = [
         local(cols(wqkv, t * WIDTH + c * PAIR), own(s.wpair, SHARD).at[:, t * PAIR : (t + 1) * PAIR])
         for t in range(3)
     ]
     get_proj = local(wproj, own(s.wproj_all, SHARD))
-    get_fc = local(wfc.at[:, pl.ds(pl.multiple_of(b * WIDTH, WIDTH), WIDTH)], own(s.wfc_mine, SHARD))
+    get_fc = local(cols(wfc, b * WIDTH, WIDTH), own(s.wfc_mine, SHARD))
     get_out = local(wout, s.wout_mine)
     get_full = local(wqkv, own(s.wfull, SHARD))
     get_g = local(cotangent, own(s.g_all, ROWS))
 
+    s.small[...] = jnp.zeros_like(s.small)
+    row = 0
+    for vector in vectors:
+        for i in range(vector.shape[0] // SHARD):
+            piece = vector[i * SHARD : (i + 1) * SHARD].astype(F32)
+            s.small[row : row + 1, :] = piece.reshape(1, SHARD)
+            row += 1
+
+    mark("barrier")
     barrier = pltpu.get_barrier_semaphore()
     others = [(lax.rem(b + i, NB), c) for i in range(1, NB)]
     others += [(b, lax.rem(c + i, NC)) for i in range(1, NC)]
     for device in others:
         pl.semaphore_signal(barrier, inc=1, device_id=device, device_id_type=MESH)
+    scale, hat = s.scale_one, s.hat_one
+
+    def norm_rows(i, carry):
+        at = pl.ds(pl.multiple_of(i * 32, 32), 32)
+        hat[at, :], scale[at, :] = normalise(tokens[at, :].astype(F32))
+        return carry
+
+    lax.fori_loop(0, ROWS // 32, norm_rows, 0)
     pl.semaphore_wait(barrier, len(others))
 
-    small_slots, pair_slots, fc_slots = net.slots(NB), net.slots(NB * 3), net.slots(NB)
-    for i in range(1, NB):
-        j = lax.rem(b + i, NB)
-        net.send(small, s.parts.at[b], (j, c), small_slots + b)
-    for i in range(1, NB):
-        j = lax.rem(b + i, NB)
+    mark("send_params")
+    batch_others = [lax.rem(b + i, NB) for i in range(1, NB)]
+    small_slots, pair_slots = net.slots(NB), net.slots(NB * 3)
+    for j in batch_others:
+        net.send(s.small, s.parts.at[b], (j, c), small_slots + b)
+    for j in batch_others:
         for t in range(3):
             net.send(
                 cols(wqkv, t * WIDTH + c * PAIR),
@@ -870,17 +974,9 @@
                 pair_slots + b * 3 + t,
             )
 
-    scale, hat = s.scale_one, s.hat_one
-
-    def norm_rows(i, carry):
-        at = pl.ds(pl.multiple_of(i * 32, 32), 32)
-        hat[at, :], scale[at, :] = normalise(tokens[at, :].astype(F32))
-        return carry
-
-    lax.fori_loop(0, ROWS // 32, norm_rows, 0)
-    s.parts[pl.ds(b, 1)] = small[...][None]
-    for i in range(1, NB):
-        j = lax.rem(b + i, NB)
+    mark("norm_one")
+    s.parts[pl.ds(b, 1)] = s.small[...][None]
+    for j in batch_others:
         net.wait(small_slots + j, s.parts.at[j])
     gain, bias = row_of(s.parts, 0), row_of(s.parts, 1)
     n_mine = rows_of(s.n_one, ROWS)(c)
@@ -891,10 +987,10 @@
         return carry
 
     lax.fori_loop(0, ROWS // 32, gain_rows, 0)
-    gather_one = GatherCtx(net, lambda j: [rows_of(s.n_one, ROWS)(j)], 1)
-    gather_one.start([n_mine])
-    gather_g = GatherBatch(net, lambda j: [rows_of(s.g_all, ROWS)(j)])
-    gather_g.start([cotangent])
+
+    mark("gather_one_start")
+    gather_one = GatherCtx(net, lambda j: halves(s.n_one, ROWS, j), 2, True)
+    gather_one.start(halves(s.n_one, ROWS, c))
     gather_proj = GatherBatch(net, lambda j: [rows_of(s.wproj_all, SHARD)(j)])
     gather_proj.start([wproj])
     for p in range(NC):
@@ -902,25 +998,39 @@
         row, lane = 2 + (at % 512) // SHARD, at % SHARD
         s.qv_rows[p : p + 1, :] = s.parts[at // 512, row : row + 1, lane : lane + PAIR]
         s.qv_rows[8 + p : 9 + p, :] = s.parts[2 + at // 512, row : row + 1, lane : lane + PAIR]
+    mark("gather_one_1")
     gather_one.stage(1)
-    for i in range(1, NB):
-        j = lax.rem(b + i, NB)
+
+    fc_slots, fc_near_slots = net.slots(NB), net.slots(NB)
+    half, pair_z = net.z % 2, net.c + 2 - 4 * (net.z % 2)
+    half_rows = pl.ds(pl.multiple_of(half * (SHARD // 2), SHARD // 2), SHARD // 2)
+    net.send(cols(wfc, net.sib * WIDTH, WIDTH), own(s.wfc_mine, SHARD), (net.sib, c), fc_slots + b)
+    for j in (net.across, net.diag):
         net.send(
-            wfc.at[:, pl.ds(pl.multiple_of(j * WIDTH, WIDTH), WIDTH)],
-            own(s.wfc_mine, SHARD),
+            wfc.at[half_rows, pl.ds(pl.multiple_of(j * WIDTH, WIDTH), WIDTH)],
+            own(s.wfc_mine, SHARD).at[half_rows],
             (j, c),
             fc_slots + b,
         )
+    mark("gather_one_2")
     gather_one.stage(2)
-    gather_g.relay()
+    gather_g = GatherBatch(net, lambda j: [rows_of(s.g_all, ROWS)(j)])
+    gather_g.start([cotangent])
+    mark("gather_one_3")
     gather_one.stage(3)
+    side_slot = net.slots(1)
+    g_mine = own(s.g_all, ROWS)
+    gather_gs = GatherSide(net, rows_of(s.g_side, ROWS))
+    gather_gs.give(b, cotangent)
+    mark("gather_one_finish")
     gather_one.finish()
+    mark("wait_pair")
     for copy in get_pair:
         copy.wait()
-    for i in range(1, NB):
-        j = lax.rem(b + i, NB)
+    for j in batch_others:
         for t in range(3):
             net.wait(pair_slots + j * 3 + t, rows_of(s.wpair, SHARD)(j).at[:, t * PAIR : (t + 1) * PAIR])
+    mark("mix")
     mix_bias = jnp.concatenate(
         [s.qv_rows[pl.ds(c, 1), :], jnp.zeros((1, PAIR), F32), s.qv_rows[pl.ds(8 + c, 1), :]], axis=1
     )
@@ -931,16 +1041,29 @@
         return carry
 
     lax.fori_loop(0, LENGTH // QB, mix_rows, 0)
-    gather_proj.relay()
-
-    attend(s.mix, s.turned, s.att, s.lse, s.work, s.low_work)
+
+    mark("attend")
     swap_att = SwapCtx(
         net, lambda j: [rows_of(s.att, ROWS)(j)], lambda j: [cols(s.att_own, j * PAIR)], 1
     )
-    swap_att.start()
+
+    def att_ready(qb):
+        swap_att.give(2 * qb)
+        swap_att.give(2 * qb + 1)
+
+    attend(s.mix, s.turned, s.att, s.lse, s.work, s.low_work, att_ready)
+    mark("relays")
+    gather_proj.relay()
+    for j in (net.across, net.diag):
+        block = rows_of(s.wfc_mine, SHARD)(j).at[half_rows]
+        net.wait(fc_slots + j, block)
+        net.send(block, block, (b, pair_z), fc_near_slots + j)
     get_proj.wait()
     gather_proj.finish()
+    mark("swap_att_finish")
     swap_att.finish()
+
+    mark("middle")
     proj_bias = row_of(s.parts, 4)
 
     def middle_cols(i, carry):
@@ -963,41 +1086,52 @@
 
     lax.fori_loop(0, ROWS // 32, norm_two_rows, 0)
 
-    def halves(ref, j):
-        block = rows_of(ref, ROWS)(j)
-        return [block.at[0:64], block.at[64:128]]
-
-    gather_two = GatherBatch(net, lambda j: halves(s.n_two, j), 2)
-    gather_two.start(halves(s.n_two, b))
+    mark("gather_two")
+    gather_two = GatherBatch(net, lambda j: halves(s.n_two, ROWS, j), 2)
+    gather_two.start(halves(s.n_two, ROWS, b))
+    n_beside = own(s.n_side, ROWS)
+    gather_g.relay()
+    gather_gs.give(net.across, rows_of(s.g_all, ROWS)(net.across))
+    gather_gs.relay(b)
+    net.send(n_two_mine, n_beside, (b, net.side), side_slot)
+    s.gs[...] = jnp.zeros_like(s.gs)
+    mark("gather_two_relay")
     gather_two.relay()
+    mark("wait_feed")
     for copy in (get_fc, get_out, get_g, get_full):
         copy.wait()
     gather_g.finish()
-    for i in range(1, NB):
-        j = lax.rem(b + i, NB)
-        net.wait(fc_slots + j, rows_of(s.wfc_mine, SHARD)(j))
+    net.wait(fc_slots + net.sib, rows_of(s.wfc_mine, SHARD)(net.sib))
+    other_rows = pl.ds(pl.multiple_of((1 - half) * (SHARD // 2), SHARD // 2), SHARD // 2)
+    for j in (net.across, net.diag):
+        net.wait(fc_near_slots + j, rows_of(s.wfc_mine, SHARD)(j).at[other_rows])
+    mark("gather_two_finish")
     gather_two.finish()
 
-    s.gs[...] = jnp.zeros_like(s.gs)
-    for n in range(4):
-        at = slice(n * 256, (n + 1) * 256)
-        pre = mm(s.n_two[...], s.wfc_mine[:, at]) + small[7 + n : 8 + n, :]
+    mark("feed")
+    hidden_slots, pre_slots = net.slots(2), net.slots(2)
+
+    def feed_cols(i, carry):
+        n = lax.rem(2 * (1 - net.x) + i, 4)
+        at = pl.ds(pl.multiple_of(n * 256, 256), 256)
+        pre = mm(s.n_two[...], s.wfc_mine[:, at]) + s.small[pl.ds(7 + n, 1), :]
         value, slope = gelu_pair(pre)
         s.hidden[:, at] = value.astype(BF)
         grad = (mm(s.g_all[...], s.wout_mine[at, :], NT) * slope).astype(BF)
         s.grad_pre[:, at] = grad
-        s.gs[pl.ds(b, 1), 7 + n : 8 + n, :] = jnp.sum(grad.astype(F32), 0, keepdims=True)[None]
-
-    reduce_out = ReduceCtx(net, rows_of(s.p_out, ROWS), s.out_beside, s.out_up, s.out_down)
-
-    def out_rows(i, carry):
-        at = pl.ds(pl.multiple_of(i * 256, 256), 256)
-        s.p_out[at, :] = mm(s.hidden[:, at], s.g_all[...], TN).astype(BF)
+        s.gs[pl.ds(b, 1), pl.ds(7 + n, 1), :] = jnp.sum(grad.astype(F32), 0, keepdims=True)[None]
         return carry
 
-    lax.fori_loop(0, 4, out_rows, 0)
-    reduce_out.start()
-
+    for i in range(2):
+        feed_cols(i, 0)
+        source = cols(s.hidden, (2 * (1 - net.x) + i) * 256, 256)
+        net.send(source, s.hidden_side.at[:, i * 256 : (i + 1) * 256], (b, net.side), hidden_slots + i)
+    for i in range(2):
+        source = cols(s.grad_pre, (2 * (1 - net.x) + i) * 256, 256)
+        net.send(source, s.pre_side.at[:, i * 256 : (i + 1) * 256], (b, net.side), pre_slots + i)
+    lax.fori_loop(2, 4, feed_cols, 0)
+
+    mark("p_norm")
     reduce_norm = ReduceBatch(net, rows_of(s.p_norm, ROWS), s.p_norm_box)
 
     def norm_block(j):
@@ -1011,19 +1145,45 @@
     norm_block(net.sib)
     reduce_norm.keep()
     norm_block(b)
-    reduce_fc = ReduceCtx(net, lambda j: s.p_fc.at[:, j], s.fc_beside, s.fc_up, s.fc_down)
-
-    def fc_rows(i, carry):
-        at = pl.ds(pl.multiple_of(i * 256, 256), 256)
-        s.p_fc[pl.ds(i, 1)] = (
-            mm(s.n_two[:, at], s.grad_pre[...], TN).astype(BF).reshape(1, NC, 32, WIDTH)
-        )
-        return carry
-
-    lax.fori_loop(0, 4, fc_rows, 0)
+
+    mark("sides")
+    gather_ns = GatherBatch(net, lambda j: [rows_of(s.n_side, ROWS)(j)])
+    net.wait(side_slot, n_beside)
+    gather_ns.start([n_beside])
+    gather_gs.relay(net.across)
+    gather_gs.finish()
+
+    def out_views(j):
+        return [rows_of(o_out, 64)(8 * (j % 2) + 4 * i + j // 2) for i in range(2)]
+
+    reduce_out = [
+        ReduceLine(net, rows_of(s.p_out.at[i], 64), s.out_up.at[i], s.out_down.at[i]) for i in range(2)
+    ]
+    gather_out = GatherCtx(net, out_views, 2, True)
+
+    def p_out(i):
+        at = slice(i * 256, (i + 1) * 256)
+        net.wait(hidden_slots + i, s.hidden_side.at[:, at])
+        mine = cols(s.hidden, net.x * 512 + i * 256, 256)
+        s.p_out[i] = (
+            mm(mine[...], s.g_all[...], TN) + mm(s.hidden_side[:, at], s.g_side[...], TN)
+        ).astype(BF)
+        reduce_out[i].launch()
+
+    keep = []
+
+    def out_done(i):
+        part = s.out_block.at[i * 64 : (i + 1) * 64]
+        reduce_out[i].finish(part)
+        gather_out.begin(i, part)
+        keep.append(local(part, out_views(c)[i]))
+
+    mark("p_out_0")
+    p_out(0)
+    mark("wait_norm")
     terms = reduce_norm.finish()
-    g_mine = own(s.g_all, ROWS)
-    grad_gain, grad_bias, sum_branch, sum_g = [jnp.zeros((1, WIDTH), F32)] * 4
+
+    mark("back_two")
 
     def back_rows(i, carry):
         at = pl.ds(pl.multiple_of(i * 32, 32), 32)
@@ -1045,7 +1205,7 @@
             sum_g + jnp.sum(g, 0, keepdims=True),
         )
 
-    sums = lax.fori_loop(0, ROWS // 32, back_rows, (grad_gain, grad_bias, sum_branch, sum_g))
+    sums = lax.fori_loop(0, ROWS // 32, back_rows, (jnp.zeros((1, WIDTH), F32),) * 4)
     put_row(s.gs, 5, sums[0])
     put_row(s.gs, 6, sums[1])
     put_row(s.gs, 4, sums[2])
@@ -1057,11 +1217,35 @@
         return carry
 
     lax.fori_loop(0, 4, att_cols, 0)
+    mark("swap_grad")
     swap_grad = SwapCtx(
         net, lambda j: [cols(s.g_att, j * PAIR)], lambda j: [rows_of(s.dout, ROWS)(j)], 1
     )
     swap_grad.start()
 
+    mark("p_out_1")
+    p_out(1)
+    mark("out_0_one")
+    reduce_out[0].pass_one()
+    mark("p_proj")
+    reduce_proj = ReduceBatch(net, rows_of(s.p_proj, SHARD), s.p_proj_box)
+
+    def proj_rows(i, carry):
+        at = pl.ds(pl.multiple_of(i * 256, 256), 256)
+        s.p_proj[at, :] = mm(s.att_own[:, at], s.branch[...], TN).astype(BF)
+        return carry
+
+    lax.fori_loop(0, 4, proj_rows, 0)
+    reduce_proj.give()
+    mark("ns_relay")
+    gather_ns.relay()
+    reduce_proj.cross()
+    reduce_proj.keep()
+    mark("out_0_two")
+    reduce_out[0].pass_two()
+    mark("out_1_one")
+    reduce_out[1].pass_one()
+    mark("p_layer")
     reduce_layer = ReduceBatch(net, rows_of(s.p_layer, ROWS), s.p_layer_box)
 
     def layer_block(j):
@@ -1075,31 +1259,53 @@
     layer_block(net.sib)
     reduce_layer.keep()
     layer_block(b)
-    reduce_proj = ReduceBatch(net, rows_of(s.p_proj, SHARD), s.p_proj_box)
-
-    def proj_rows(i, carry):
-        at = pl.ds(pl.multiple_of(i * 256, 256), 256)
-        s.p_proj[at, :] = mm(s.att_own[:, at], s.branch[...], TN).astype(BF)
-        return carry
-
-    lax.fori_loop(0, 4, proj_rows, 0)
-    reduce_proj.give()
-    reduce_proj.cross()
-    reduce_proj.keep()
-    gather_full = GatherBatch(net, lambda j: [rows_of(s.wfull, SHARD)(j)])
-    gather_full.start([wqkv])
+    mark("out_0_done")
+    out_done(0)
+    mark("out_1_two")
+    reduce_out[1].pass_two()
+    mark("swap_grad_finish")
     swap_grad.finish()
-
-    attend_back(
-        s.mix, s.turned, s.dout, s.lse, s.gmix, s.grad_k, s.grad_v, s.work, s.more, s.low_work, s.low_more
-    )
+    mark("ns_finish")
+    gather_ns.finish()
+
+    reduce_fc = [
+        ReduceLine(net, lambda zz, i=i: s.p_fc.at[i, :, zz], s.fc_up.at[i], s.fc_down.at[i])
+        for i in range(2)
+    ]
+
+    def p_fc(i):
+        at = slice(i * 256, (i + 1) * 256)
+        net.wait(pre_slots + i, s.pre_side.at[:, at])
+        mine = cols(s.grad_pre, net.x * 512 + i * 256, 256)
+
+        def fc_rows(k, carry):
+            rows = pl.ds(pl.multiple_of(k * 256, 256), 256)
+            total = mm(s.n_two[:, rows], mine[...], TN) + mm(s.n_side[:, rows], s.pre_side[:, at], TN)
+            s.p_fc[i, pl.ds(k, 1)] = total.astype(BF).reshape(1, 4, 64, 256)
+            return carry
+
+        lax.fori_loop(0, 4, fc_rows, 0)
+        reduce_fc[i].launch()
+
+    mark("p_fc_0")
+    p_fc(0)
+
+    mark("attend_back")
     swap_mix = SwapCtx(
         net,
-        lambda j: [rows_of(s.gmix, ROWS)(j).at[:, t * PAIR : (t + 1) * PAIR] for t in range(3)],
-        lambda j: [cols(s.gmix_own, t * WIDTH + j * PAIR) for t in range(3)],
-        3,
-    )
-    swap_mix.start()
+        lambda j: [rows_of(s.gmix, ROWS)(j)],
+        lambda j: [s.gmix_own.at[j]],
+        1,
+    )
+    attend_back(
+        s.mix, s.turned, s.dout, s.lse, s.gmix, s.grad_k, s.grad_v,
+        s.work, s.more, s.low_work, s.low_more, lambda qb: None,
+    )
+    mark("out_1_done")
+    out_done(1)
+    mark("fc_0_one")
+    reduce_fc[0].pass_one()
+    mark("p_qkv")
     reduce_qkv = ReduceBatch(net, rows_of(s.p_qkv, SHARD), s.p_qkv_box)
 
     def qkv_block(j):
@@ -1110,9 +1316,26 @@
     reduce_qkv.give()
     qkv_block(net.across)
     reduce_qkv.cross()
+    gather_full = GatherBatch(net, lambda j: [rows_of(s.wfull, SHARD)(j)])
+    gather_full.start([wqkv])
     qkv_block(net.sib)
     reduce_qkv.keep()
     qkv_block(b)
+    mark("p_fc_1")
+    p_fc(1)
+    mark("fc_0_two")
+    reduce_fc[0].pass_two()
+    mark("proj_sum")
+    add_into(s.proj_sum, reduce_proj.finish())
+    reduce_part = ReduceCtx(net, rows_of(s.proj_sum, 32), s.proj_beside, s.proj_up, s.proj_down)
+    reduce_part.start()
+    mark("gather_out_1")
+    gather_out.stage(1)
+    mark("fc_1_one")
+    reduce_fc[1].pass_one()
+    swap_mix.give(0)
+    swap_mix.give(1)
+    mark("gqv")
     s.gqv[...] = jnp.zeros_like(s.gqv)
     s.gqv[pl.ds(c, 1), :] = jnp.sum(s.gmix[:, :PAIR].astype(F32), 0, keepdims=True)
     s.gqv[pl.ds(8 + c, 1), :] = jnp.sum(s.gmix[:, 2 * PAIR :].astype(F32), 0, keepdims=True)
@@ -1122,44 +1345,97 @@
         s.gs[at // 512, row : row + 1, lane : lane + PAIR] = s.gqv[p : p + 1, :]
         s.gs[2 + at // 512, row : row + 1, lane : lane + PAIR] = s.gqv[8 + p : 9 + p, :]
 
-    reduce_out.stage(3)
-    reduce_out.stage(2)
-    reduce_out.stage(1)
-    reduce_out.finish(s.out_block)
-    gather_out = GatherCtx(net, lambda j: [rows_of(o_out, ROWS)(j)], 1)
-    gather_out.start([s.out_block])
-    keep_out = local(s.out_block, rows_of(o_out, ROWS)(c))
-    reduce_fc.start()
-    gather_full.relay()
-
+    mark("wait_qkv")
+    terms = reduce_qkv.finish()
+    add_into(s.qkv_block, terms)
+    gather_qkv = GatherCtx(net, lambda j: halves(o_qkv.at[j], SHARD, 0), 2, True)
+    gather_qkv.start(halves(s.qkv_block, SHARD, 0))
+    keep.append(local(s.qkv_block, o_qkv.at[c]))
+    swap_slots = net.slots(2 * NB)
+
+    def fc_done(i):
+        reduce_fc[i].finish(s.fc_sum.at[i])
+        for j in batch_others:
+            net.send(
+                s.fc_sum.at[i, j], cols(s.fc_block, b * 512 + i * 256, 256), (j, c), swap_slots + 2 * b + i
+            )
+        s.fc_block[:, pl.ds(pl.multiple_of(b * 512 + i * 256, 256), 256)] = s.fc_sum[i, pl.ds(b, 1)][0]
+
+    mark("fc_0_done")
+    fc_done(0)
+    swap_mix.give(2)
+    swap_mix.give(3)
+    mark("part_fold")
+    reduce_part.fold()
+    mark("fc_1_two")
+    reduce_fc[1].pass_two()
+    mark("gather_out_2")
+    gather_out.stage(2)
+    swap_mix.give(4)
+    swap_mix.give(5)
+    mark("part_one")
+    reduce_part.line.pass_one()
+    mark("layer_out")
     layer_bias = row_of(s.parts, 11)
-    terms = reduce_layer.finish()
+    layer_terms = reduce_layer.finish()
 
     def layer_rows(i, carry):
         at = pl.ds(pl.multiple_of(i * 32, 32), 32)
-        total = terms[0][at, :].astype(F32) + terms[1][at, :].astype(F32) + terms[2][at, :].astype(F32)
-        layer_out[at, :] = (s.middle[at, :] + total + layer_bias).astype(BF)
+        total = [term[at, :].astype(F32) for term in layer_terms]
+        layer_out[at, :] = (s.middle[at, :] + (total[0] + total[1] + total[2]) + layer_bias).astype(BF)
         return carry
 
     lax.fori_loop(0, ROWS // 32, layer_rows, 0)
-    terms = reduce_qkv.finish()
-    add_into(s.qkv_block, terms)
-    gather_qkv = GatherCtx(
-        net, lambda j: [cols(o_qkv, t * WIDTH + j * PAIR) for t in range(3)], 3
-    )
-    qkv_parts = [s.qkv_block.at[:, t * PAIR : (t + 1) * PAIR] for t in range(3)]
-    gather_qkv.start(qkv_parts)
-    keep_qkv = [local(one, cols(o_qkv, t * WIDTH + c * PAIR)) for t, one in enumerate(qkv_parts)]
-    add_into(s.proj_sum, reduce_proj.finish())
-    reduce_part = ReduceCtx(net, rows_of(s.proj_sum, 32), s.proj_beside, s.proj_up, s.proj_down)
-    reduce_part.start()
-
+    mark("fc_1_done")
+    fc_done(1)
+    swap_mix.give(6)
+    swap_mix.give(7)
+    mark("part_two")
+    reduce_part.line.pass_two()
+    mark("gather_qkv_1")
+    gather_qkv.stage(1)
+    mark("gather_out_3")
+    gather_out.stage(3)
+    mark("fc_swap")
+    for j in batch_others:
+        for i in range(2):
+            net.wait(swap_slots + 2 * j + i, cols(s.fc_block, j * 512 + i * 256, 256))
+
+    def fc_views(j):
+        block = o_fc.at[j % 2, pl.ds(pl.multiple_of((j // 2) * 64, 64), 64)]
+        return [block.at[0:32], block.at[32:64]]
+
+    gather_fc = GatherCtx(net, fc_views, 2, True)
+    gather_fc.start([s.fc_block.at[0:32], s.fc_block.at[32:64]])
+    keep.append(local(s.fc_block, o_fc.at[net.x, pl.ds(pl.multiple_of(net.z * 64, 64), 64)]))
+    mark("part_finish")
+    reduce_part.line.finish(s.proj_block)
+    gather_part = GatherCtx(net, lambda j: [rows_of(o_proj, 32)(j)], 1)
+    gather_part.start([s.proj_block])
+    keep.append(local(s.proj_block, rows_of(o_proj, 32)(c)))
+    mark("gather_qkv_2")
+    gather_qkv.stage(2)
+    mark("gather_part_1")
+    gather_part.stage(1)
+    mark("gather_fc_1")
+    gather_fc.stage(1)
+    mark("full_relay")
+    gather_full.relay()
+    mark("gather_qkv_3")
+    gather_qkv.stage(3)
+
+    mark("wait_mix")
     gather_full.finish()
     swap_mix.finish()
+    for j in range(NC):
+        for t in range(3):
+            to, at = t * WIDTH + j * PAIR, t * PAIR
+            s.gmix_all[:, to : to + PAIR] = s.gmix_own[j, :, at : at + PAIR]
+    mark("grad_tokens")
 
     def one_cols(i, carry):
         at = pl.ds(pl.multiple_of(i * 256, 256), 256)
-        s.gn_one[:, at] = mm(s.gmix_own[...], s.wfull[at, :], NT)
+        s.gn_one[:, at] = mm(s.gmix_all[...], s.wfull[at, :], NT)
         return carry
 
     lax.fori_loop(0, 4, one_cols, 0)
@@ -1181,79 +1457,79 @@
     put_row(s.gs, 0, sums[0])
     put_row(s.gs, 1, sums[1])
     gs_slots, far_slots = net.slots(NB), net.slots(NC)
-    for i in range(1, NB):
-        j = lax.rem(b + i, NB)
+    for j in batch_others:
         net.send(s.gs.at[j], s.gs_box.at[b], (j, c), gs_slots + b)
 
-    reduce_part.stage(3)
-    gather_out.stage(1)
-    reduce_part.stage(2)
-    reduce_fc.stage(3)
-    reduce_part.stage(1)
-    gather_out.stage(2)
-    reduce_part.finish(s.proj_block)
-    gather_part = GatherCtx(net, lambda j: [rows_of(o_proj, 32)(j)], 1)
-    gather_part.start([s.proj_block])
-    keep_part = local(s.proj_block, rows_of(o_proj, 32)(c))
-    reduce_fc.stage(2)
-    gather_out.stage(3)
-    reduce_fc.stage(1)
-    gather_qkv.stage(1)
-    reduce_fc.finish(s.fc_sum)
-    swap_slots = net.slots(NB)
-    for i in range(1, NB):
-        j = lax.rem(b + i, NB)
-        net.send(
-            s.fc_sum.at[j],
-            s.fc_block.at[:, pl.ds(pl.multiple_of(b * WIDTH, WIDTH), WIDTH)],
-            (j, c),
-            swap_slots + b,
-        )
-    at = pl.ds(pl.multiple_of(b * WIDTH, WIDTH), WIDTH)
-    s.fc_block[:, at] = s.fc_sum[pl.ds(b, 1)][0]
-    gather_qkv.stage(2)
+    mark("gs_sum")
     total = s.gs[pl.ds(b, 1)][0]
-    for i in range(1, NB):
-        j = lax.rem(b + i, NB)
+    for j in batch_others:
         net.wait(gs_slots + j, s.gs_box.at[j])
         total = total + s.gs_box[pl.ds(j, 1)][0]
     s.gs_sum[...] = total
     for i in range(1, NC):
         j = lax.rem(c + i, NC)
         net.send(s.gs_sum, s.gs_far.at[c], (b, j), far_slots + c)
-    for i in range(1, NB):
-        j = lax.rem(b + i, NB)
-        net.wait(swap_slots + j, s.fc_block.at[:, pl.ds(pl.multiple_of(j * WIDTH, WIDTH), WIDTH)])
-    gather_fc = GatherCtx(net, lambda j: [rows_of(o_fc, 32)(j)], 1)
-    gather_fc.start([s.fc_block])
-    keep_fc = local(s.fc_block, rows_of(o_fc, 32)(c))
-    gather_part.stage(1)
-    gather_qkv.stage(3)
+    mark("gather_part_2")
     gather_part.stage(2)
+    mark("gather_fc_2")
+    gather_fc.stage(2)
+    mark("gather_part_3")
     gather_part.stage(3)
+    mark("gather_fc_3")
+    gather_fc.stage(3)
+    mark("far_sum")
     for i in range(1, NC):
         j = lax.rem(c - i + NC, NC)
         net.wait(far_slots + j, s.gs_far.at[j])
         total = total + s.gs_far[pl.ds(j, 1)][0]
     grad_small[...] = total
-    gather_fc.stage(1)
-    gather_fc.stage(2)
-    gather_fc.stage(3)
-    for gather in (gather_out, gather_qkv, gather_part, gather_fc):
-        gather.finish()
-    for copy in [keep_out, keep_part, keep_fc] + keep_qkv:
+    mark("out_end")
+    gather_out.finish()
+    mark("qkv_end")
+    gather_qkv.finish()
+    mark("part_end")
+    gather_part.finish()
+    mark("fc_end")
+    gather_fc.finish()
+    mark("drain")
+    for copy in keep:
         copy.wait()
     net.drain()
+    mark(None)
+
+
+VECTOR_ROWS = (1, 1, 2, 1, 1, 1, 4, 1)
+STEPS = 8
+
+
+def widen_kernel(layer, grad_in, small, w_qkv, w_proj, w_fc, w_out, *outs):
+    o_layer, o_grad_in, o_qkv, o_proj, o_fc, o_out = outs[:6]
+    o_layer[...] = layer[...]
+    o_grad_in[...] = grad_in[...]
+    for j in range(NC):
+        for t in range(3):
+            to, at = t * WIDTH + j * PAIR, t * PAIR
+            o_qkv[:, to : to + PAIR] = w_qkv[j, :, at : at + PAIR].astype(F32)
+    o_proj[...] = w_proj[...].astype(F32)
+    o_out[...] = w_out[...].astype(F32)
+    for j in range(NB):
+        for x in range(2):
+            to, at = j * WIDTH + x * 512, j * 512
+            o_fc[:, to : to + 512] = w_fc[x, :, at : at + 512].astype(F32)
+
+    @pl.when(pl.program_id(0) == 0)
+    def _():
+        row = 0
+        for out in outs[6:]:
+            for i in range(out.shape[0] // SHARD):
+                out[i * SHARD : (i + 1) * SHARD] = small[row, :]
+                row += 1
 
 
 def per_device_fast(
     tokens, cotangent, ln1_gain, ln1_bias, qkv_weight, qv_bias, proj_weight, proj_bias,
     ln2_gain, ln2_bias, fc_weight, fc_bias, out_weight, out_bias,
 ):
-    small = jnp.concatenate(
-        [ln1_gain, ln1_bias, qv_bias, proj_bias, ln2_gain, ln2_bias, fc_bias, out_bias,
-         jnp.zeros((4 * SHARD,), BF)]
-    ).astype(F32).reshape(SMALL_ROWS, SHARD)
     vmem, anywhere = pl.BlockSpec(memory_space=pltpu.VMEM), pl.BlockSpec(memory_space=pl.ANY)
     shape = jax.ShapeDtypeStruct
     layer, grad_in, grad_small, w_qkv, w_proj, w_fc, w_out = pl.pallas_call(
@@ -1262,12 +1538,12 @@
             shape((ROWS, WIDTH), BF),
             shape((ROWS, WIDTH), BF),
             shape((SMALL_ROWS, SHARD), F32),
-            shape((SHARD, 3 * WIDTH), BF),
+            shape((NC, SHARD, 3 * PAIR), BF),
             shape((SHARD, WIDTH), BF),
-            shape((SHARD, FF), BF),
+            shape((2, SHARD, FF // 2), BF),
             shape((FF // NB, WIDTH), BF),
         ),
-        in_specs=[vmem, vmem, vmem, anywhere, anywhere, anywhere, anywhere],
+        in_specs=[vmem] * 10 + [anywhere] * 4,
         out_specs=(vmem, vmem, vmem, anywhere, anywhere, anywhere, anywhere),
         scratch_shapes=[pltpu.VMEM(*item) for item in SCRATCH.values()]
         + [
@@ -1279,30 +1555,63 @@
             collective_id=0, has_side_effects=True, vmem_limit_bytes=VMEM_BYTES
         ),
     )(
-        tokens.reshape(ROWS, WIDTH), cotangent.reshape(ROWS, WIDTH), small,
+        tokens.reshape(ROWS, WIDTH), cotangent.reshape(ROWS, WIDTH),
+        ln1_gain, ln1_bias, qv_bias, proj_bias, ln2_gain, ln2_bias, fc_bias, out_bias,
         qkv_weight, proj_weight, fc_weight, out_weight,
     )
-    flat = grad_small.reshape(-1)
-    sizes = [SHARD, SHARD, 2 * SHARD, SHARD, SHARD, SHARD, 4 * SHARD, SHARD]
-    smalls, at = [], 0
-    for size in sizes:
-        smalls.append(lax.slice(flat, (at,), (at + size,)))
-        at += size
+
+    def rows(count, width):
+        return pl.BlockSpec((count // STEPS, width), lambda i: (i, 0))
+
+    half = pl.BlockSpec((2, SHARD // STEPS, FF // 2), lambda i: (0, i, 0))
+    smalls = [pl.BlockSpec((n * SHARD,), lambda i: (0,)) for n in VECTOR_ROWS]
+    layer, grad_in, w_qkv, w_proj, w_fc, w_out, *vectors = pl.pallas_call(
+        widen_kernel,
+        grid=(STEPS,),
+        out_shape=(
+            shape((ROWS, WIDTH), BF),
+            shape((ROWS, WIDTH), BF),
+            shape((SHARD, 3 * WIDTH), F32),
+            shape((SHARD, WIDTH), F32),
+            shape((SHARD, FF), F32),
+            shape((FF // NB, WIDTH), F32),
+            *[shape((n * SHARD,), F32) for n in VECTOR_ROWS],
+        ),
+        in_specs=[
+            rows(ROWS, WIDTH),
+            rows(ROWS, WIDTH),
+            pl.BlockSpec((SMALL_ROWS, SHARD), lambda i: (0, 0)),
+            pl.BlockSpec((NC, SHARD // STEPS, 3 * PAIR), lambda i: (0, i, 0)),
+            rows(SHARD, WIDTH),
+            half,
+            rows(FF // NB, WIDTH),
+        ],
+        out_specs=(
+            rows(ROWS, WIDTH),
+            rows(ROWS, WIDTH),
+            rows(SHARD, 3 * WIDTH),
+            rows(SHARD, WIDTH),
+            rows(SHARD, FF),
+            rows(FF // NB, WIDTH),
+            *smalls,
+        ),
+        compiler_params=pltpu.CompilerParams(vmem_limit_bytes=VMEM_BYTES),
+    )(layer, grad_in, grad_small, w_qkv, w_proj, w_fc, w_out)
     return (
         layer.reshape(tokens.shape),
         grad_in.reshape(tokens.shape),
-        smalls[0],
-        smalls[1],
-        w_qkv.astype(F32),
-        smalls[2],
-        w_proj.astype(F32),
-        smalls[3],
-        smalls[4],
-        smalls[5],
-        w_fc.astype(F32),
-        smalls[6],
-        w_out.astype(F32),
-        smalls[7],
+        vectors[0],
+        vectors[1],
+        w_qkv,
+        vectors[2],
+        w_proj,
+        vectors[3],
+        vectors[4],
+        vectors[5],
+        w_fc,
+        vectors[6],
+        w_out,
+        vectors[7],
     )
 
 

time: 275 us -> 201 us (0.73)
  Pallas kernels: 251 us -> 200 us
  local copies, waits for them, and re-layouts: 12.8 us -> 0 us
  other arithmetic: 9.83 us -> 0 us
    pallas_call x1, Pallas kernels: 251 us -> 191 us  [per_device_fast(): pl.pallas_call(layer_kernel, out_shape=(shape((ROWS, WIDTH), BF), shape((...]
    unnamed x24 -> x0, local copies, waits for them, and re-layouts: 10.8 us -> none
    convert_element_type x4 -> x0, other arithmetic: 9.83 us -> none  [the longest x1 4.25 us: per_device_fast(): w_fc.astype(F32)]
    pallas_call x0 -> x1, Pallas kernels: none -> 9.37 us  [per_device_fast(): pl.pallas_call(widen_kernel, grid=(STEPS,), out_shape=(shape((ROWS, WIDTH...]
where the time goes in v2:
time: 201 us
  Pallas kernels  200 us (100%)
    pallas_call x1, Pallas kernels, per_device_fast(): pl.pallas_call(layer_kernel, out_shape=(shape((ROWS, WIDTH), BF), shape((...  191 us
    pallas_call x1, Pallas kernels, per_device_fast(): pl.pallas_call(widen_kernel, grid=(STEPS,), out_shape=(shape((ROWS, WIDTH...  9.37 us

profile of v2, /device:TPU:0, one launch (start us, length us, event | category | flops | bytes accessed | tf_op | source)
XLA Modules:
  0.0 201.0 jit_solution(7434823174427612962)
XLA Ops:
  0.7 190.8 %shard_map.245 = (bf16[128,1024]{1,0:T(8,128)(2,1)}, bf16[128,1024]{1,0:T(8,128)(2,1)}, f32[16,256]{1,0:T(8,128)}, bf16[8,256,384]{2,1,0:T(8,128)(2,1)}, bf16[25...) custom-call(bf16[128,1024]{1,0:T(8,128)(2,1)} %bitcast.4, ...), custom_call_target="tpu_custom_call" | custom-call | tf_op jit(solution)/shard_map/pallas_call | solution.py:1535
  191.5 9.4 %shard_map.246 = (bf16[128,1024]{1,0:T(8,128)(2,1)}, bf16[128,1024]{1,0:T(8,128)(2,1)}, f32[256,3072]{1,0:T(8,128)}, f32[256,1024]{1,0:T(8,128)}, f32[256,4096]{...) custom-call(bf16[128,1024]{1,0:T(8,128)(2,1)} %get-tuple-element.35., ...), custom_call_target="tpu_custom_call" | custom-call | tf_op jit(solution)/shard_map/pallas_call | solution.py:1568

commit v3 on v2

--- a/solution.py
+++ b/solution.py
@@ -378,18 +378,6 @@
     return two if one is None else (one if two is None else jnp.logical_and(one, two))
 
 
-class Marks:
-    def __init__(self):
-        self.scope = None
-
-    def __call__(self, name):
-        if self.scope is not None:
-            self.scope.__exit__(None, None, None)
-        self.scope = None if name is None else jax.named_scope(name)
-        if self.scope is not None:
-            self.scope.__enter__()
-
-
 class Net:
     def __init__(self, b, c, send_sems, recv_sems):
         self.b, self.c, self.z, self.x = b, c, c // 2, c % 2
@@ -472,10 +460,6 @@
                 if self.turn and i == count - 1:
                     goes = both(here, jnp.logical_and(zz > 0, zz < 3))
                 net.send(refs[i], dsts[i], (net.b, net.side), self.beside + zz * count + i, goes)
-        if self.turn:
-            if d == 1:
-                self.corner()
-            self.pass_on(d)
 
     def piece(self, end):
         return self.views(2 * end + 1 - self.net.x)[self.count - 1]
@@ -672,12 +656,20 @@
             net.wait(slot, refs[i])
             net.send(refs[i], refs[i], (net.sib, net.c), slot)
 
+    def take(self, j):
+        refs = self.views(j)
+        for i in range(self.count):
+            self.net.wait(self.base + j * self.count + i, refs[i])
+
+    def near(self):
+        self.take(self.net.sib)
+
+    def far(self):
+        self.take(self.net.diag)
+
     def finish(self):
-        net = self.net
-        for j in (net.sib, net.diag):
-            refs = self.views(j)
-            for i in range(self.count):
-                net.wait(self.base + j * self.count + i, refs[i])
+        self.near()
+        self.far()
 
 
 class ReduceBatch:
@@ -774,7 +766,7 @@
         ready(qb)
 
 
-def attend_back(mix, key_t, dout, lse, gmix, grad_k, grad_v, work, more, low_work, low_more, ready):
+def attend_back(mix, key_t, dout, lse, gmix, grad_k, grad_v, work, more, low_work, low_more):
     key_t[...] = mix[:, PAIR : 2 * PAIR].astype(F32).T.astype(BF)
     grad_k[...] = jnp.zeros_like(grad_k)
     grad_v[...] = jnp.zeros_like(grad_v)
@@ -807,7 +799,6 @@
         gmix[here, :PAIR] = jnp.concatenate(outs, axis=0).T.astype(BF)
         gmix[here, PAIR : 2 * PAIR] = (grad_k[here, :] * 0.125).astype(BF)
         gmix[here, 2 * PAIR :] = grad_v[here, :].astype(BF)
-        ready(qb)
 
 
 gelu_scale = 0.7978845608028654
@@ -866,7 +857,7 @@
     fc_up=((2, 4, NB, 64, 256), BF),
     fc_down=((2, 4, NB, 64, 256), BF),
     fc_sum=((2, NB, 64, 256), BF),
-    fc_block=((64, FF // 2), BF),
+    fc_block=((2, 64, WIDTH), BF),
     p_proj=((WIDTH, WIDTH), BF),
     p_proj_box=((3, SHARD, WIDTH), BF),
     proj_sum=((SHARD, WIDTH), BF),
@@ -893,7 +884,8 @@
     gs_sum=((SMALL_ROWS, SHARD), F32),
     gs_far=((NC, SMALL_ROWS, SHARD), F32),
 )
-SENDS, RECVS, LOCALS = 96, 248, 16
+TURN_OUT, TURN_FC = (False, True), (False, True)
+SENDS, RECVS, LOCALS = 64, 260, 16
 
 
 def layer_kernel(*refs):
@@ -906,7 +898,7 @@
     send_sems, recv_sems, local_sems = scratch[len(SCRATCH) :]
     b, c = lax.axis_index("batch"), lax.axis_index("ctx")
     net = Net(b, c, send_sems, recv_sems)
-    mark = Marks()
+    v = SimpleNamespace(keep=[])
     locals_open = []
 
     def local(src, dst):
@@ -925,357 +917,345 @@
         block = rows_of(ref, size)(j)
         return [block.at[0 : size // 2], block.at[size // 2 : size]]
 
-    mark("enter")
-    get_pair = [
-        local(cols(wqkv, t * WIDTH + c * PAIR), own(s.wpair, SHARD).at[:, t * PAIR : (t + 1) * PAIR])
-        for t in range(3)
+    def loop(count, size, body):
+        def step(i, carry):
+            body(pl.ds(pl.multiple_of(i * size, size), size))
+            return carry
+
+        lax.fori_loop(0, count, step, 0)
+
+    batch_others = [lax.rem(b + i, NB) for i in range(1, NB)]
+
+    small_slots, fc_slots, fc_near_slots = net.slots(NB), net.slots(NB), net.slots(NB)
+    hidden_slots, pre_slots, side_slot, swap_slots = net.slots(4), net.slots(4), net.slots(1), net.slots(2 * NB)
+    proj_slots, proj_side_slot, proj_near_slots = net.slots(NB), net.slots(1), net.slots(2)
+    gs_slots, far_slots = net.slots(NB), net.slots(NC)
+    gather_pair = GatherBatch(net, lambda j: [rows_of(s.wpair, SHARD)(j)])
+    gather_one = GatherCtx(net, lambda j: halves(s.n_one, ROWS, j), 2, True)
+    gather_g = GatherBatch(net, lambda j: [rows_of(s.g_all, ROWS)(j)])
+    gather_gs = GatherSide(net, rows_of(s.g_side, ROWS))
+    gather_ns = GatherBatch(net, lambda j: [rows_of(s.n_side, ROWS)(j)])
+    gather_two = GatherBatch(net, lambda j: halves(s.n_two, ROWS, j), 2)
+    gather_full = [
+        GatherBatch(net, lambda j, i=i: [rows_of(s.wfull, SHARD // 2)(2 * j + i)]) for i in range(2)
     ]
-    get_proj = local(wproj, own(s.wproj_all, SHARD))
-    get_fc = local(cols(wfc, b * WIDTH, WIDTH), own(s.wfc_mine, SHARD))
-    get_out = local(wout, s.wout_mine)
-    get_full = local(wqkv, own(s.wfull, SHARD))
-    get_g = local(cotangent, own(s.g_all, ROWS))
-
-    s.small[...] = jnp.zeros_like(s.small)
-    row = 0
-    for vector in vectors:
-        for i in range(vector.shape[0] // SHARD):
-            piece = vector[i * SHARD : (i + 1) * SHARD].astype(F32)
-            s.small[row : row + 1, :] = piece.reshape(1, SHARD)
-            row += 1
-
-    mark("barrier")
-    barrier = pltpu.get_barrier_semaphore()
-    others = [(lax.rem(b + i, NB), c) for i in range(1, NB)]
-    others += [(b, lax.rem(c + i, NC)) for i in range(1, NC)]
-    for device in others:
-        pl.semaphore_signal(barrier, inc=1, device_id=device, device_id_type=MESH)
+    swap_att = SwapCtx(
+        net, lambda j: [rows_of(s.att, ROWS)(j)], lambda j: [cols(s.att_own, j * PAIR)], 1
+    )
+    swap_grad = SwapCtx(
+        net, lambda j: [cols(s.g_att, j * PAIR)], lambda j: [rows_of(s.dout, ROWS)(j)], 1
+    )
+    swap_mix = SwapCtx(
+        net, lambda j: [rows_of(s.gmix, ROWS)(j)], lambda j: [s.gmix_own.at[j]], 1
+    )
+    reduce_norm = ReduceBatch(net, rows_of(s.p_norm, ROWS), s.p_norm_box)
+    reduce_layer = ReduceBatch(net, rows_of(s.p_layer, ROWS), s.p_layer_box)
+    reduce_proj = ReduceBatch(net, rows_of(s.p_proj, SHARD), s.p_proj_box)
+    reduce_qkv = ReduceBatch(net, rows_of(s.p_qkv, SHARD), s.p_qkv_box)
+    reduce_part = ReduceCtx(net, rows_of(s.proj_sum, 32), s.proj_beside, s.proj_up, s.proj_down)
+    reduce_out = [
+        ReduceLine(net, rows_of(s.p_out.at[i], 64), s.out_up.at[i], s.out_down.at[i]) for i in range(2)
+    ]
+    reduce_fc = [
+        ReduceLine(net, lambda k, i=i: s.p_fc.at[i, :, k], s.fc_up.at[i], s.fc_down.at[i])
+        for i in range(2)
+    ]
+
+    def out_view(i, j):
+        return rows_of(o_out, 64)(8 * (j % 2) + 4 * i + j // 2)
+
+    def fc_view(i, j):
+        return o_fc.at[j % 2, i, pl.ds(pl.multiple_of((j // 2) * 64, 64), 64)]
+
+    gather_out = [GatherCtx(net, lambda j, i=i: [out_view(i, j)], 1, TURN_OUT[i]) for i in range(2)]
+    gather_fc = [GatherCtx(net, lambda j, i=i: [fc_view(i, j)], 1, TURN_FC[i]) for i in range(2)]
+    gather_qkv = GatherCtx(net, lambda j: halves(o_qkv.at[j], SHARD, 0), 2, True)
+    gather_part = GatherCtx(net, lambda j: [rows_of(o_proj, 32)(j)], 1)
+
     scale, hat = s.scale_one, s.hat_one
-
-    def norm_rows(i, carry):
-        at = pl.ds(pl.multiple_of(i * 32, 32), 32)
-        hat[at, :], scale[at, :] = normalise(tokens[at, :].astype(F32))
-        return carry
-
-    lax.fori_loop(0, ROWS // 32, norm_rows, 0)
-    pl.semaphore_wait(barrier, len(others))
-
-    mark("send_params")
-    batch_others = [lax.rem(b + i, NB) for i in range(1, NB)]
-    small_slots, pair_slots = net.slots(NB), net.slots(NB * 3)
-    for j in batch_others:
-        net.send(s.small, s.parts.at[b], (j, c), small_slots + b)
-    for j in batch_others:
-        for t in range(3):
-            net.send(
-                cols(wqkv, t * WIDTH + c * PAIR),
-                own(s.wpair, SHARD).at[:, t * PAIR : (t + 1) * PAIR],
-                (j, c),
-                pair_slots + b * 3 + t,
-            )
-
-    mark("norm_one")
-    s.parts[pl.ds(b, 1)] = s.small[...][None]
-    for j in batch_others:
-        net.wait(small_slots + j, s.parts.at[j])
-    gain, bias = row_of(s.parts, 0), row_of(s.parts, 1)
-    n_mine = rows_of(s.n_one, ROWS)(c)
-
-    def gain_rows(i, carry):
-        at = pl.ds(pl.multiple_of(i * 32, 32), 32)
-        n_mine[at, :] = (hat[at, :] * gain + bias).astype(BF)
-        return carry
-
-    lax.fori_loop(0, ROWS // 32, gain_rows, 0)
-
-    mark("gather_one_start")
-    gather_one = GatherCtx(net, lambda j: halves(s.n_one, ROWS, j), 2, True)
-    gather_one.start(halves(s.n_one, ROWS, c))
-    gather_proj = GatherBatch(net, lambda j: [rows_of(s.wproj_all, SHARD)(j)])
-    gather_proj.start([wproj])
-    for p in range(NC):
-        at = p * PAIR
-        row, lane = 2 + (at % 512) // SHARD, at % SHARD
-        s.qv_rows[p : p + 1, :] = s.parts[at // 512, row : row + 1, lane : lane + PAIR]
-        s.qv_rows[8 + p : 9 + p, :] = s.parts[2 + at // 512, row : row + 1, lane : lane + PAIR]
-    mark("gather_one_1")
-    gather_one.stage(1)
-
-    fc_slots, fc_near_slots = net.slots(NB), net.slots(NB)
     half, pair_z = net.z % 2, net.c + 2 - 4 * (net.z % 2)
     half_rows = pl.ds(pl.multiple_of(half * (SHARD // 2), SHARD // 2), SHARD // 2)
-    net.send(cols(wfc, net.sib * WIDTH, WIDTH), own(s.wfc_mine, SHARD), (net.sib, c), fc_slots + b)
-    for j in (net.across, net.diag):
-        net.send(
-            wfc.at[half_rows, pl.ds(pl.multiple_of(j * WIDTH, WIDTH), WIDTH)],
-            own(s.wfc_mine, SHARD).at[half_rows],
-            (j, c),
-            fc_slots + b,
+    other_rows = pl.ds(pl.multiple_of((1 - half) * (SHARD // 2), SHARD // 2), SHARD // 2)
+    side_rows = pl.ds(pl.multiple_of(net.x * (SHARD // 2), SHARD // 2), SHARD // 2)
+    other_side_rows = pl.ds(pl.multiple_of((1 - net.x) * (SHARD // 2), SHARD // 2), SHARD // 2)
+    chip_rows = [
+        pl.ds(pl.multiple_of(first * 256, 256), 256) for first in (b // 2, 1 - b // 2)
+    ]
+    n_mine = rows_of(s.n_one, ROWS)(c)
+    n_two_mine = own(s.n_two, ROWS)
+    g_mine = own(s.g_all, ROWS)
+    n_beside = own(s.n_side, ROWS)
+
+    def enter():
+        v.get_pair = [
+            local(cols(wqkv, t * WIDTH + c * PAIR), own(s.wpair, SHARD).at[:, t * PAIR : (t + 1) * PAIR])
+            for t in range(3)
+        ]
+        v.get_proj = local(wproj, own(s.wproj_all, SHARD))
+        v.get_rest = [
+            local(cols(wfc, b * WIDTH, WIDTH), own(s.wfc_mine, SHARD)),
+            local(wout, s.wout_mine),
+            local(wqkv, own(s.wfull, SHARD)),
+            local(cotangent, g_mine),
+        ]
+        barrier = pltpu.get_barrier_semaphore()
+        others = [(j, c) for j in batch_others]
+        others += [(b, lax.rem(c + i, NC)) for i in range(1, NC)]
+        for device in others:
+            pl.semaphore_signal(barrier, inc=1, device_id=device, device_id_type=MESH)
+        s.small[...] = jnp.zeros_like(s.small)
+        row = 0
+        for vector in vectors:
+            for i in range(vector.shape[0] // SHARD):
+                piece = vector[i * SHARD : (i + 1) * SHARD].astype(F32)
+                s.small[row : row + 1, :] = piece.reshape(1, SHARD)
+                row += 1
+
+        def norm_rows(at):
+            hat[at, :], scale[at, :] = normalise(tokens[at, :].astype(F32))
+
+        loop(ROWS // 32, 32, norm_rows)
+        for copy in v.get_pair:
+            copy.wait()
+        s.parts[pl.ds(b, 1)] = s.small[...][None]
+        pl.semaphore_wait(barrier, len(others))
+
+    def send_small():
+        for j in batch_others:
+            net.send(s.small, s.parts.at[b], (j, c), small_slots + b)
+
+    def pair_start():
+        gather_pair.start([own(s.wpair, SHARD)])
+
+    def g_start():
+        gather_g.start([cotangent])
+
+    def norm_one():
+        for j in batch_others:
+            net.wait(small_slots + j, s.parts.at[j])
+        gain, bias = row_of(s.parts, 0), row_of(s.parts, 1)
+
+        def gain_rows(at):
+            n_mine[at, :] = (hat[at, :] * gain + bias).astype(BF)
+
+        loop(ROWS // 32, 32, gain_rows)
+        gather_one.start(halves(s.n_one, ROWS, c))
+
+    def proj_start():
+        mine = own(s.wproj_all, SHARD)
+        net.send(wproj.at[side_rows], mine.at[side_rows], (net.across, c), proj_slots + b)
+        net.send(wproj, mine, (net.sib, c), proj_slots + b)
+
+    def proj_relay():
+        block = rows_of(s.wproj_all, SHARD)(net.across).at[side_rows]
+        net.wait(proj_slots + net.across, block)
+        net.send(block, block, (b, net.side), proj_side_slot)
+        net.send(block, block, (net.sib, c), proj_near_slots)
+
+    def proj_side():
+        block = rows_of(s.wproj_all, SHARD)(net.across).at[other_side_rows]
+        net.wait(proj_side_slot, block)
+        net.send(block, block, (net.sib, c), proj_near_slots + 1)
+
+    def fc_start():
+        net.send(cols(wfc, net.sib * WIDTH, WIDTH), own(s.wfc_mine, SHARD), (net.sib, c), fc_slots + b)
+        for j in (net.across, net.diag):
+            net.send(
+                wfc.at[half_rows, pl.ds(pl.multiple_of(j * WIDTH, WIDTH), WIDTH)],
+                own(s.wfc_mine, SHARD).at[half_rows],
+                (j, c),
+                fc_slots + b,
+            )
+
+    def fc_relay():
+        for j in (net.across, net.diag):
+            block = rows_of(s.wfc_mine, SHARD)(j).at[half_rows]
+            net.wait(fc_slots + j, block)
+            net.send(block, block, (b, pair_z), fc_near_slots + j)
+
+    def qv_rows():
+        for p in range(NC):
+            at = p * PAIR
+            row, lane = 2 + (at % 512) // SHARD, at % SHARD
+            s.qv_rows[p : p + 1, :] = s.parts[at // 512, row : row + 1, lane : lane + PAIR]
+            s.qv_rows[8 + p : 9 + p, :] = s.parts[2 + at // 512, row : row + 1, lane : lane + PAIR]
+
+    def g_relay():
+        gather_g.relay()
+
+    def gs_give_own():
+        gather_gs.give(b, cotangent)
+
+    def gs_give_across():
+        gather_gs.give(net.across, rows_of(s.g_all, ROWS)(net.across))
+
+    def gs_relay_own():
+        gather_gs.relay(b)
+
+    def gs_relay_across():
+        gather_gs.relay(net.across)
+
+    def mix():
+        mix_bias = jnp.concatenate(
+            [s.qv_rows[pl.ds(c, 1), :], jnp.zeros((1, PAIR), F32), s.qv_rows[pl.ds(8 + c, 1), :]], axis=1
         )
-    mark("gather_one_2")
-    gather_one.stage(2)
-    gather_g = GatherBatch(net, lambda j: [rows_of(s.g_all, ROWS)(j)])
-    gather_g.start([cotangent])
-    mark("gather_one_3")
-    gather_one.stage(3)
-    side_slot = net.slots(1)
-    g_mine = own(s.g_all, ROWS)
-    gather_gs = GatherSide(net, rows_of(s.g_side, ROWS))
-    gather_gs.give(b, cotangent)
-    mark("gather_one_finish")
-    gather_one.finish()
-    mark("wait_pair")
-    for copy in get_pair:
-        copy.wait()
-    for j in batch_others:
-        for t in range(3):
-            net.wait(pair_slots + j * 3 + t, rows_of(s.wpair, SHARD)(j).at[:, t * PAIR : (t + 1) * PAIR])
-    mark("mix")
-    mix_bias = jnp.concatenate(
-        [s.qv_rows[pl.ds(c, 1), :], jnp.zeros((1, PAIR), F32), s.qv_rows[pl.ds(8 + c, 1), :]], axis=1
-    )
-
-    def mix_rows(i, carry):
-        at = pl.ds(pl.multiple_of(i * QB, QB), QB)
-        s.mix[at, :] = (mm(s.n_one[at, :], s.wpair[...]) + mix_bias).astype(BF)
-        return carry
-
-    lax.fori_loop(0, LENGTH // QB, mix_rows, 0)
-
-    mark("attend")
-    swap_att = SwapCtx(
-        net, lambda j: [rows_of(s.att, ROWS)(j)], lambda j: [cols(s.att_own, j * PAIR)], 1
-    )
-
-    def att_ready(qb):
-        swap_att.give(2 * qb)
-        swap_att.give(2 * qb + 1)
-
-    attend(s.mix, s.turned, s.att, s.lse, s.work, s.low_work, att_ready)
-    mark("relays")
-    gather_proj.relay()
-    for j in (net.across, net.diag):
-        block = rows_of(s.wfc_mine, SHARD)(j).at[half_rows]
-        net.wait(fc_slots + j, block)
-        net.send(block, block, (b, pair_z), fc_near_slots + j)
-    get_proj.wait()
-    gather_proj.finish()
-    mark("swap_att_finish")
-    swap_att.finish()
-
-    mark("middle")
-    proj_bias = row_of(s.parts, 4)
-
-    def middle_cols(i, carry):
-        at = pl.ds(pl.multiple_of(i * 256, 256), 256)
-        s.middle[:, at] = mm(s.att_own[...], s.wproj_all[:, at]) + tokens[:, at].astype(F32)
-        return carry
-
-    lax.fori_loop(0, WIDTH // 256, middle_cols, 0)
-    gain_two, bias_two = row_of(s.parts, 5), row_of(s.parts, 6)
-    n_two_mine = own(s.n_two, ROWS)
-
-    def norm_two_rows(i, carry):
-        at = pl.ds(pl.multiple_of(i * 32, 32), 32)
-        middle = s.middle[at, :] + proj_bias
-        s.middle[at, :] = middle
-        norm, width = normalise(middle)
-        s.hat_two[at, :], s.scale_two[at, :] = norm, width
-        n_two_mine[at, :] = (norm * gain_two + bias_two).astype(BF)
-        return carry
-
-    lax.fori_loop(0, ROWS // 32, norm_two_rows, 0)
-
-    mark("gather_two")
-    gather_two = GatherBatch(net, lambda j: halves(s.n_two, ROWS, j), 2)
-    gather_two.start(halves(s.n_two, ROWS, b))
-    n_beside = own(s.n_side, ROWS)
-    gather_g.relay()
-    gather_gs.give(net.across, rows_of(s.g_all, ROWS)(net.across))
-    gather_gs.relay(b)
-    net.send(n_two_mine, n_beside, (b, net.side), side_slot)
-    s.gs[...] = jnp.zeros_like(s.gs)
-    mark("gather_two_relay")
-    gather_two.relay()
-    mark("wait_feed")
-    for copy in (get_fc, get_out, get_g, get_full):
-        copy.wait()
-    gather_g.finish()
-    net.wait(fc_slots + net.sib, rows_of(s.wfc_mine, SHARD)(net.sib))
-    other_rows = pl.ds(pl.multiple_of((1 - half) * (SHARD // 2), SHARD // 2), SHARD // 2)
-    for j in (net.across, net.diag):
-        net.wait(fc_near_slots + j, rows_of(s.wfc_mine, SHARD)(j).at[other_rows])
-    mark("gather_two_finish")
-    gather_two.finish()
-
-    mark("feed")
-    hidden_slots, pre_slots = net.slots(2), net.slots(2)
-
-    def feed_cols(i, carry):
+
+        def mix_rows(at):
+            s.mix[at, :] = (mm(s.n_one[at, :], s.wpair[...]) + mix_bias).astype(BF)
+
+        loop(LENGTH // QB, QB, mix_rows)
+
+    def att():
+        def ready(qb):
+            swap_att.give(2 * qb)
+            swap_att.give(2 * qb + 1)
+
+        attend(s.mix, s.turned, s.att, s.lse, s.work, s.low_work, ready)
+
+    def proj_finish():
+        v.get_proj.wait()
+        net.wait(proj_slots + net.sib, rows_of(s.wproj_all, SHARD)(net.sib))
+        block = rows_of(s.wproj_all, SHARD)(net.diag)
+        net.wait(proj_near_slots, block.at[side_rows])
+        net.wait(proj_near_slots + 1, block.at[other_side_rows])
+
+    def middle():
+        def middle_cols(at):
+            s.middle[:, at] = mm(s.att_own[...], s.wproj_all[:, at]) + tokens[:, at].astype(F32)
+
+        loop(WIDTH // 256, 256, middle_cols)
+        proj_bias, gain_two, bias_two = row_of(s.parts, 4), row_of(s.parts, 5), row_of(s.parts, 6)
+
+        def norm_two_rows(at):
+            middle = s.middle[at, :] + proj_bias
+            s.middle[at, :] = middle
+            norm, width = normalise(middle)
+            s.hat_two[at, :], s.scale_two[at, :] = norm, width
+            n_two_mine[at, :] = (norm * gain_two + bias_two).astype(BF)
+
+        loop(ROWS // 32, 32, norm_two_rows)
+        gather_two.start(halves(s.n_two, ROWS, b))
+
+    def ns_give():
+        net.send(n_two_mine, n_beside, (b, net.side), side_slot)
+
+    def ns_start():
+        net.wait(side_slot, n_beside)
+        gather_ns.start([n_beside])
+
+    def feed_wait():
+        for copy in v.get_rest:
+            copy.wait()
+        gather_g.finish()
+        net.wait(fc_slots + net.sib, rows_of(s.wfc_mine, SHARD)(net.sib))
+        for j in (net.across, net.diag):
+            net.wait(fc_near_slots + j, rows_of(s.wfc_mine, SHARD)(j).at[other_rows])
+        s.gs[...] = jnp.zeros_like(s.gs)
+
+    def feed_cols(r, i):
         n = lax.rem(2 * (1 - net.x) + i, 4)
-        at = pl.ds(pl.multiple_of(n * 256, 256), 256)
-        pre = mm(s.n_two[...], s.wfc_mine[:, at]) + s.small[pl.ds(7 + n, 1), :]
+        rows, at = chip_rows[r], pl.ds(pl.multiple_of(n * 256, 256), 256)
+        pre = mm(s.n_two[rows, :], s.wfc_mine[:, at]) + s.small[pl.ds(7 + n, 1), :]
         value, slope = gelu_pair(pre)
-        s.hidden[:, at] = value.astype(BF)
-        grad = (mm(s.g_all[...], s.wout_mine[at, :], NT) * slope).astype(BF)
-        s.grad_pre[:, at] = grad
-        s.gs[pl.ds(b, 1), pl.ds(7 + n, 1), :] = jnp.sum(grad.astype(F32), 0, keepdims=True)[None]
-        return carry
-
-    for i in range(2):
-        feed_cols(i, 0)
-        source = cols(s.hidden, (2 * (1 - net.x) + i) * 256, 256)
-        net.send(source, s.hidden_side.at[:, i * 256 : (i + 1) * 256], (b, net.side), hidden_slots + i)
-    for i in range(2):
-        source = cols(s.grad_pre, (2 * (1 - net.x) + i) * 256, 256)
-        net.send(source, s.pre_side.at[:, i * 256 : (i + 1) * 256], (b, net.side), pre_slots + i)
-    lax.fori_loop(2, 4, feed_cols, 0)
-
-    mark("p_norm")
-    reduce_norm = ReduceBatch(net, rows_of(s.p_norm, ROWS), s.p_norm_box)
+        s.hidden[rows, at] = value.astype(BF)
+        grad = (mm(s.g_all[rows, :], s.wout_mine[at, :], NT) * slope).astype(BF)
+        s.grad_pre[rows, at] = grad
+        s.gs[pl.ds(b, 1), pl.ds(7 + n, 1), :] += jnp.sum(grad.astype(F32), 0, keepdims=True)[None]
+
+    def tile(ref, r, i):
+        return ref.at[chip_rows[r], pl.ds(pl.multiple_of((2 * (1 - net.x) + i) * 256, 256), 256)]
+
+    def side_tile(ref, r, i):
+        return ref.at[chip_rows[r], i * 256 : (i + 1) * 256]
+
+    def feed_i(r, i):
+        feed_cols(r, i)
+        net.send(tile(s.hidden, r, i), side_tile(s.hidden_side, r, i), (b, net.side), hidden_slots + 2 * r + i)
+
+    def pre_give(r, i):
+        net.send(tile(s.grad_pre, r, i), side_tile(s.pre_side, r, i), (b, net.side), pre_slots + 2 * r + i)
+
+    def feed_rest(r):
+        def step(i, carry):
+            feed_cols(r, i)
+            return carry
+
+        lax.fori_loop(2, 4, step, 0)
 
     def norm_block(j):
         at = pl.ds(pl.multiple_of(j * ROWS, ROWS), ROWS)
         s.p_norm[at, :] = mm(s.grad_pre[at, :], s.wfc_mine[...], NT).astype(BF)
 
-    norm_block(net.diag)
-    reduce_norm.give()
-    norm_block(net.across)
-    reduce_norm.cross()
-    norm_block(net.sib)
-    reduce_norm.keep()
-    norm_block(b)
-
-    mark("sides")
-    gather_ns = GatherBatch(net, lambda j: [rows_of(s.n_side, ROWS)(j)])
-    net.wait(side_slot, n_beside)
-    gather_ns.start([n_beside])
-    gather_gs.relay(net.across)
-    gather_gs.finish()
-
-    def out_views(j):
-        return [rows_of(o_out, 64)(8 * (j % 2) + 4 * i + j // 2) for i in range(2)]
-
-    reduce_out = [
-        ReduceLine(net, rows_of(s.p_out.at[i], 64), s.out_up.at[i], s.out_down.at[i]) for i in range(2)
-    ]
-    gather_out = GatherCtx(net, out_views, 2, True)
+    def norm_diag():
+        norm_block(net.diag)
+        reduce_norm.give()
+
+    def norm_across():
+        norm_block(net.across)
+
+    def norm_sib():
+        norm_block(net.sib)
+        reduce_norm.keep()
+
+    def norm_own():
+        norm_block(b)
+
+    def back_two():
+        gain_two = row_of(s.parts, 5)
+        terms = reduce_norm.finish()
+
+        def back_rows(i, carry):
+            at = pl.ds(pl.multiple_of(i * 32, 32), 32)
+            grad_gain, grad_bias, sum_branch, sum_g = carry
+            grad = terms[0][at, :].astype(F32) + terms[1][at, :].astype(F32) + terms[2][at, :].astype(F32)
+            norm = s.hat_two[at, :]
+            scaled = grad * gain_two
+            inner = scaled - jnp.mean(scaled, -1, keepdims=True)
+            inner = inner - norm * jnp.mean(scaled * norm, -1, keepdims=True)
+            g = g_mine[at, :].astype(F32)
+            total = g + s.scale_two[at, :] * inner
+            s.grad_middle[at, :] = total
+            low = total.astype(BF)
+            s.branch[at, :] = low
+            return (
+                grad_gain + jnp.sum(grad * norm, 0, keepdims=True),
+                grad_bias + jnp.sum(grad, 0, keepdims=True),
+                sum_branch + jnp.sum(low.astype(F32), 0, keepdims=True),
+                sum_g + jnp.sum(g, 0, keepdims=True),
+            )
+
+        sums = lax.fori_loop(0, ROWS // 32, back_rows, (jnp.zeros((1, WIDTH), F32),) * 4)
+        put_row(s.gs, 5, sums[0])
+        put_row(s.gs, 6, sums[1])
+        put_row(s.gs, 4, sums[2])
+        put_row(s.gs, 11, sums[3])
+
+        def att_cols(at):
+            s.g_att[:, at] = mm(s.branch[...], s.wproj_all[at, :], NT).astype(BF)
+
+        loop(4, 256, att_cols)
+        swap_grad.start()
 
     def p_out(i):
         at = slice(i * 256, (i + 1) * 256)
-        net.wait(hidden_slots + i, s.hidden_side.at[:, at])
+        for r in range(2):
+            net.wait(hidden_slots + 2 * r + i, side_tile(s.hidden_side, r, i))
         mine = cols(s.hidden, net.x * 512 + i * 256, 256)
         s.p_out[i] = (
             mm(mine[...], s.g_all[...], TN) + mm(s.hidden_side[:, at], s.g_side[...], TN)
         ).astype(BF)
         reduce_out[i].launch()
 
-    keep = []
-
     def out_done(i):
         part = s.out_block.at[i * 64 : (i + 1) * 64]
         reduce_out[i].finish(part)
-        gather_out.begin(i, part)
-        keep.append(local(part, out_views(c)[i]))
-
-    mark("p_out_0")
-    p_out(0)
-    mark("wait_norm")
-    terms = reduce_norm.finish()
-
-    mark("back_two")
-
-    def back_rows(i, carry):
-        at = pl.ds(pl.multiple_of(i * 32, 32), 32)
-        grad_gain, grad_bias, sum_branch, sum_g = carry
-        grad = terms[0][at, :].astype(F32) + terms[1][at, :].astype(F32) + terms[2][at, :].astype(F32)
-        norm = s.hat_two[at, :]
-        scaled = grad * gain_two
-        inner = scaled - jnp.mean(scaled, -1, keepdims=True)
-        inner = inner - norm * jnp.mean(scaled * norm, -1, keepdims=True)
-        g = g_mine[at, :].astype(F32)
-        total = g + s.scale_two[at, :] * inner
-        s.grad_middle[at, :] = total
-        low = total.astype(BF)
-        s.branch[at, :] = low
-        return (
-            grad_gain + jnp.sum(grad * norm, 0, keepdims=True),
-            grad_bias + jnp.sum(grad, 0, keepdims=True),
-            sum_branch + jnp.sum(low.astype(F32), 0, keepdims=True),
-            sum_g + jnp.sum(g, 0, keepdims=True),
-        )
-
-    sums = lax.fori_loop(0, ROWS // 32, back_rows, (jnp.zeros((1, WIDTH), F32),) * 4)
-    put_row(s.gs, 5, sums[0])
-    put_row(s.gs, 6, sums[1])
-    put_row(s.gs, 4, sums[2])
-    put_row(s.gs, 11, sums[3])
-
-    def att_cols(i, carry):
-        at = pl.ds(pl.multiple_of(i * 256, 256), 256)
-        s.g_att[:, at] = mm(s.branch[...], s.wproj_all[at, :], NT).astype(BF)
-        return carry
-
-    lax.fori_loop(0, 4, att_cols, 0)
-    mark("swap_grad")
-    swap_grad = SwapCtx(
-        net, lambda j: [cols(s.g_att, j * PAIR)], lambda j: [rows_of(s.dout, ROWS)(j)], 1
-    )
-    swap_grad.start()
-
-    mark("p_out_1")
-    p_out(1)
-    mark("out_0_one")
-    reduce_out[0].pass_one()
-    mark("p_proj")
-    reduce_proj = ReduceBatch(net, rows_of(s.p_proj, SHARD), s.p_proj_box)
-
-    def proj_rows(i, carry):
-        at = pl.ds(pl.multiple_of(i * 256, 256), 256)
-        s.p_proj[at, :] = mm(s.att_own[:, at], s.branch[...], TN).astype(BF)
-        return carry
-
-    lax.fori_loop(0, 4, proj_rows, 0)
-    reduce_proj.give()
-    mark("ns_relay")
-    gather_ns.relay()
-    reduce_proj.cross()
-    reduce_proj.keep()
-    mark("out_0_two")
-    reduce_out[0].pass_two()
-    mark("out_1_one")
-    reduce_out[1].pass_one()
-    mark("p_layer")
-    reduce_layer = ReduceBatch(net, rows_of(s.p_layer, ROWS), s.p_layer_box)
-
-    def layer_block(j):
-        at = pl.ds(pl.multiple_of(j * ROWS, ROWS), ROWS)
-        s.p_layer[at, :] = mm(s.hidden[at, :], s.wout_mine[...]).astype(BF)
-
-    layer_block(net.diag)
-    reduce_layer.give()
-    layer_block(net.across)
-    reduce_layer.cross()
-    layer_block(net.sib)
-    reduce_layer.keep()
-    layer_block(b)
-    mark("out_0_done")
-    out_done(0)
-    mark("out_1_two")
-    reduce_out[1].pass_two()
-    mark("swap_grad_finish")
-    swap_grad.finish()
-    mark("ns_finish")
-    gather_ns.finish()
-
-    reduce_fc = [
-        ReduceLine(net, lambda zz, i=i: s.p_fc.at[i, :, zz], s.fc_up.at[i], s.fc_down.at[i])
-        for i in range(2)
-    ]
+        gather_out[i].begin(0, part)
+        v.keep.append(local(part, out_view(i, c)))
 
     def p_fc(i):
         at = slice(i * 256, (i + 1) * 256)
-        net.wait(pre_slots + i, s.pre_side.at[:, at])
+        for r in range(2):
+            net.wait(pre_slots + 2 * r + i, side_tile(s.pre_side, r, i))
         mine = cols(s.grad_pre, net.x * 512 + i * 256, 256)
 
         def fc_rows(k, carry):
@@ -1287,219 +1267,292 @@
         lax.fori_loop(0, 4, fc_rows, 0)
         reduce_fc[i].launch()
 
-    mark("p_fc_0")
-    p_fc(0)
-
-    mark("attend_back")
-    swap_mix = SwapCtx(
-        net,
-        lambda j: [rows_of(s.gmix, ROWS)(j)],
-        lambda j: [s.gmix_own.at[j]],
-        1,
-    )
-    attend_back(
-        s.mix, s.turned, s.dout, s.lse, s.gmix, s.grad_k, s.grad_v,
-        s.work, s.more, s.low_work, s.low_more, lambda qb: None,
-    )
-    mark("out_1_done")
-    out_done(1)
-    mark("fc_0_one")
-    reduce_fc[0].pass_one()
-    mark("p_qkv")
-    reduce_qkv = ReduceBatch(net, rows_of(s.p_qkv, SHARD), s.p_qkv_box)
-
-    def qkv_block(j):
-        at = pl.ds(pl.multiple_of(j * SHARD, SHARD), SHARD)
-        s.p_qkv[at, :] = mm(s.n_one[:, at], s.gmix[...], TN).astype(BF)
-
-    qkv_block(net.diag)
-    reduce_qkv.give()
-    qkv_block(net.across)
-    reduce_qkv.cross()
-    gather_full = GatherBatch(net, lambda j: [rows_of(s.wfull, SHARD)(j)])
-    gather_full.start([wqkv])
-    qkv_block(net.sib)
-    reduce_qkv.keep()
-    qkv_block(b)
-    mark("p_fc_1")
-    p_fc(1)
-    mark("fc_0_two")
-    reduce_fc[0].pass_two()
-    mark("proj_sum")
-    add_into(s.proj_sum, reduce_proj.finish())
-    reduce_part = ReduceCtx(net, rows_of(s.proj_sum, 32), s.proj_beside, s.proj_up, s.proj_down)
-    reduce_part.start()
-    mark("gather_out_1")
-    gather_out.stage(1)
-    mark("fc_1_one")
-    reduce_fc[1].pass_one()
-    swap_mix.give(0)
-    swap_mix.give(1)
-    mark("gqv")
-    s.gqv[...] = jnp.zeros_like(s.gqv)
-    s.gqv[pl.ds(c, 1), :] = jnp.sum(s.gmix[:, :PAIR].astype(F32), 0, keepdims=True)
-    s.gqv[pl.ds(8 + c, 1), :] = jnp.sum(s.gmix[:, 2 * PAIR :].astype(F32), 0, keepdims=True)
-    for p in range(NC):
-        at = p * PAIR
-        row, lane = 2 + (at % 512) // SHARD, at % SHARD
-        s.gs[at // 512, row : row + 1, lane : lane + PAIR] = s.gqv[p : p + 1, :]
-        s.gs[2 + at // 512, row : row + 1, lane : lane + PAIR] = s.gqv[8 + p : 9 + p, :]
-
-    mark("wait_qkv")
-    terms = reduce_qkv.finish()
-    add_into(s.qkv_block, terms)
-    gather_qkv = GatherCtx(net, lambda j: halves(o_qkv.at[j], SHARD, 0), 2, True)
-    gather_qkv.start(halves(s.qkv_block, SHARD, 0))
-    keep.append(local(s.qkv_block, o_qkv.at[c]))
-    swap_slots = net.slots(2 * NB)
-
     def fc_done(i):
         reduce_fc[i].finish(s.fc_sum.at[i])
+        mine = pl.ds(pl.multiple_of(b * 256, 256), 256)
         for j in batch_others:
-            net.send(
-                s.fc_sum.at[i, j], cols(s.fc_block, b * 512 + i * 256, 256), (j, c), swap_slots + 2 * b + i
+            net.send(s.fc_sum.at[i, j], s.fc_block.at[i, :, mine], (j, c), swap_slots + 2 * b + i)
+        s.fc_block[i, :, mine] = s.fc_sum[i, pl.ds(b, 1)][0]
+
+    def fc_swap(i):
+        for j in batch_others:
+            at = pl.ds(pl.multiple_of(j * 256, 256), 256)
+            net.wait(swap_slots + 2 * j + i, s.fc_block.at[i, :, at])
+        gather_fc[i].begin(0, s.fc_block.at[i])
+        v.keep.append(local(s.fc_block.at[i], fc_view(i, c)))
+
+    def p_proj():
+        def proj_rows(at):
+            s.p_proj[at, :] = mm(s.att_own[:, at], s.branch[...], TN).astype(BF)
+
+        loop(4, 256, proj_rows)
+        reduce_proj.give()
+        reduce_proj.keep()
+
+    def proj_done():
+        add_into(s.proj_sum, reduce_proj.finish())
+        reduce_part.start()
+
+    def part_done():
+        reduce_part.line.finish(s.proj_block)
+        gather_part.begin(0, s.proj_block)
+        v.keep.append(local(s.proj_block, rows_of(o_proj, 32)(c)))
+
+    def p_layer():
+        def layer_block(j):
+            at = pl.ds(pl.multiple_of(j * ROWS, ROWS), ROWS)
+            s.p_layer[at, :] = mm(s.hidden[at, :], s.wout_mine[...]).astype(BF)
+
+        layer_block(net.diag)
+        reduce_layer.give()
+        layer_block(net.sib)
+        reduce_layer.keep()
+        layer_block(net.across)
+        layer_block(b)
+
+    def layer_end():
+        layer_bias = row_of(s.parts, 11)
+        terms = reduce_layer.finish()
+
+        def layer_rows(at):
+            total = terms[0][at, :].astype(F32) + terms[1][at, :].astype(F32) + terms[2][at, :].astype(F32)
+            layer_out[at, :] = (s.middle[at, :] + total + layer_bias).astype(BF)
+
+        loop(ROWS // 32, 32, layer_rows)
+
+    def att_back():
+        attend_back(
+            s.mix, s.turned, s.dout, s.lse, s.gmix, s.grad_k, s.grad_v,
+            s.work, s.more, s.low_work, s.low_more,
+        )
+
+    def mix_give(k):
+        swap_mix.give(2 * k)
+        swap_mix.give(2 * k + 1)
+
+    def p_qkv():
+        def qkv_block(j):
+            at = pl.ds(pl.multiple_of(j * SHARD, SHARD), SHARD)
+            s.p_qkv[at, :] = mm(s.n_one[:, at], s.gmix[...], TN).astype(BF)
+
+        qkv_block(net.diag)
+        reduce_qkv.give()
+        qkv_block(net.across)
+        qkv_block(net.sib)
+        reduce_qkv.keep()
+        qkv_block(b)
+
+    def qkv_done():
+        terms = reduce_qkv.finish()
+        add_into(s.qkv_block, terms)
+        gather_qkv.start(halves(s.qkv_block, SHARD, 0))
+        v.keep.append(local(s.qkv_block, o_qkv.at[c]))
+
+    def gqv():
+        s.gqv[...] = jnp.zeros_like(s.gqv)
+        s.gqv[pl.ds(c, 1), :] = jnp.sum(s.gmix[:, :PAIR].astype(F32), 0, keepdims=True)
+        s.gqv[pl.ds(8 + c, 1), :] = jnp.sum(s.gmix[:, 2 * PAIR :].astype(F32), 0, keepdims=True)
+        for p in range(NC):
+            at = p * PAIR
+            row, lane = 2 + (at % 512) // SHARD, at % SHARD
+            s.gs[at // 512, row : row + 1, lane : lane + PAIR] = s.gqv[p : p + 1, :]
+            s.gs[2 + at // 512, row : row + 1, lane : lane + PAIR] = s.gqv[8 + p : 9 + p, :]
+
+    def full_start(i):
+        gather_full[i].start([rows_of(wqkv, SHARD // 2)(i)])
+
+    def grad_in():
+        for gather in gather_full:
+            gather.finish()
+        swap_mix.finish()
+        for j in range(NC):
+            for t in range(3):
+                to, at = t * WIDTH + j * PAIR, t * PAIR
+                s.gmix_all[:, to : to + PAIR] = s.gmix_own[j, :, at : at + PAIR]
+        gain = row_of(s.parts, 0)
+
+        def one_cols(at):
+            s.gn_one[:, at] = mm(s.gmix_all[...], s.wfull[at, :], NT)
+
+        loop(4, 256, one_cols)
+
+        def token_rows(i, carry):
+            at = pl.ds(pl.multiple_of(i * 32, 32), 32)
+            grad_gain, grad_bias = carry
+            grad, norm = s.gn_one[at, :], s.hat_one[at, :]
+            scaled = grad * gain
+            inner = scaled - jnp.mean(scaled, -1, keepdims=True)
+            inner = inner - norm * jnp.mean(scaled * norm, -1, keepdims=True)
+            grad_tokens[at, :] = (s.grad_middle[at, :] + s.scale_one[at, :] * inner).astype(BF)
+            return (
+                grad_gain + jnp.sum(grad * norm, 0, keepdims=True),
+                grad_bias + jnp.sum(grad, 0, keepdims=True),
             )
-        s.fc_block[:, pl.ds(pl.multiple_of(b * 512 + i * 256, 256), 256)] = s.fc_sum[i, pl.ds(b, 1)][0]
-
-    mark("fc_0_done")
+
+        sums = lax.fori_loop(0, ROWS // 32, token_rows, (jnp.zeros((1, WIDTH), F32),) * 2)
+        put_row(s.gs, 0, sums[0])
+        put_row(s.gs, 1, sums[1])
+        for j in batch_others:
+            net.send(s.gs.at[j], s.gs_box.at[b], (j, c), gs_slots + b)
+
+    def gs_sum():
+        total = s.gs[pl.ds(b, 1)][0]
+        for j in batch_others:
+            net.wait(gs_slots + j, s.gs_box.at[j])
+            total = total + s.gs_box[pl.ds(j, 1)][0]
+        s.gs_sum[...] = total
+        for i in range(1, NC):
+            j = lax.rem(c + i, NC)
+            net.send(s.gs_sum, s.gs_far.at[c], (b, j), far_slots + c)
+
+    def far_sum():
+        total = s.gs_sum[...]
+        for i in range(1, NC):
+            j = lax.rem(c - i + NC, NC)
+            net.wait(far_slots + j, s.gs_far.at[j])
+            total = total + s.gs_far[pl.ds(j, 1)][0]
+        grad_small[...] = total
+
+    enter()
+    send_small()
+    norm_one()
+    g_start()
+    pair_start()
+    gather_one.stage(1)
+    gather_one.corner()
+    proj_start()
+    gather_one.pass_on(1)
+    gather_one.stage(2)
+    gather_pair.relay()
+    qv_rows()
+    gather_one.stage(3)
+    proj_relay()
+    gather_pair.finish()
+    fc_start()
+    g_relay()
+    gs_give_own()
+    gather_one.pass_on(2)
+    gather_one.pass_on(3)
+    gather_one.finish()
+    mix()
+    att()
+    fc_relay()
+    gs_give_across()
+    proj_side()
+    proj_finish()
+    swap_att.finish()
+    middle()
+    ns_give()
+    gs_relay_across()
+    gs_relay_own()
+    gather_gs.finish()
+    gather_two.near()
+    feed_wait()
+    feed_i(0,0)
+    gather_two.relay()
+    gather_two.far()
+    feed_i(1,0)
+    feed_i(1,1)
+    feed_i(0,1)
+    feed_rest(1)
+    feed_rest(0)
+    norm_sib()
+    ns_start()
+    norm_across()
+    p_out(0)
+    norm_diag()
+    reduce_norm.cross()
+    pre_give(1,0)
+    reduce_out[0].pass_one()
+    p_out(1)
+    pre_give(0,0)
+    full_start(1)
+    pre_give(1,1)
+    norm_own()
+    back_two()
+    reduce_out[0].pass_two()
+    reduce_out[1].pass_one()
+    pre_give(0,1)
+    gather_ns.relay()
+    gather_ns.finish()
+    out_done(0)
+    p_proj()
+    reduce_proj.cross()
+    reduce_out[1].pass_two()
+    p_fc(0)
+    out_done(1)
+    p_fc(1)
+    swap_grad.finish()
+    gather_out[1].corner()
+    gather_out[0].stage(1)
+    att_back()
+    mix_give(0)
+    mix_give(3)
+    gqv()
+    p_qkv()
+    reduce_qkv.cross()
+    reduce_fc[0].pass_one()
+    proj_done()
+    gather_out[1].stage(1)
+    gather_out[0].stage(2)
+    full_start(0)
+    reduce_fc[1].pass_one()
+    reduce_fc[0].pass_two()
     fc_done(0)
-    swap_mix.give(2)
-    swap_mix.give(3)
-    mark("part_fold")
+    qkv_done()
+    gather_out[1].pass_on(1)
+    gather_full[1].relay()
+    gather_out[0].stage(3)
+    gather_out[1].stage(2)
+    reduce_fc[1].pass_two()
     reduce_part.fold()
-    mark("fc_1_two")
-    reduce_fc[1].pass_two()
-    mark("gather_out_2")
-    gather_out.stage(2)
-    swap_mix.give(4)
-    swap_mix.give(5)
-    mark("part_one")
     reduce_part.line.pass_one()
-    mark("layer_out")
-    layer_bias = row_of(s.parts, 11)
-    layer_terms = reduce_layer.finish()
-
-    def layer_rows(i, carry):
-        at = pl.ds(pl.multiple_of(i * 32, 32), 32)
-        total = [term[at, :].astype(F32) for term in layer_terms]
-        layer_out[at, :] = (s.middle[at, :] + (total[0] + total[1] + total[2]) + layer_bias).astype(BF)
-        return carry
-
-    lax.fori_loop(0, ROWS // 32, layer_rows, 0)
-    mark("fc_1_done")
+    fc_swap(0)
+    mix_give(1)
+    gather_qkv.stage(1)
+    mix_give(2)
+    gather_full[0].relay()
+    reduce_part.line.pass_two()
+    gather_fc[0].stage(1)
+    gather_out[1].pass_on(2)
     fc_done(1)
-    swap_mix.give(6)
-    swap_mix.give(7)
-    mark("part_two")
-    reduce_part.line.pass_two()
-    mark("gather_qkv_1")
-    gather_qkv.stage(1)
-    mark("gather_out_3")
-    gather_out.stage(3)
-    mark("fc_swap")
-    for j in batch_others:
-        for i in range(2):
-            net.wait(swap_slots + 2 * j + i, cols(s.fc_block, j * 512 + i * 256, 256))
-
-    def fc_views(j):
-        block = o_fc.at[j % 2, pl.ds(pl.multiple_of((j // 2) * 64, 64), 64)]
-        return [block.at[0:32], block.at[32:64]]
-
-    gather_fc = GatherCtx(net, fc_views, 2, True)
-    gather_fc.start([s.fc_block.at[0:32], s.fc_block.at[32:64]])
-    keep.append(local(s.fc_block, o_fc.at[net.x, pl.ds(pl.multiple_of(net.z * 64, 64), 64)]))
-    mark("part_finish")
-    reduce_part.line.finish(s.proj_block)
-    gather_part = GatherCtx(net, lambda j: [rows_of(o_proj, 32)(j)], 1)
-    gather_part.start([s.proj_block])
-    keep.append(local(s.proj_block, rows_of(o_proj, 32)(c)))
-    mark("gather_qkv_2")
+    p_layer()
+    fc_swap(1)
+    reduce_layer.cross()
+    gather_out[1].pass_on(3)
     gather_qkv.stage(2)
-    mark("gather_part_1")
+    part_done()
+    gather_fc[0].stage(2)
+    gather_fc[1].corner()
+    gather_fc[1].pass_on(1)
+    gather_fc[1].stage(1)
+    gather_qkv.stage(3)
     gather_part.stage(1)
-    mark("gather_fc_1")
-    gather_fc.stage(1)
-    mark("full_relay")
-    gather_full.relay()
-    mark("gather_qkv_3")
-    gather_qkv.stage(3)
-
-    mark("wait_mix")
-    gather_full.finish()
-    swap_mix.finish()
-    for j in range(NC):
-        for t in range(3):
-            to, at = t * WIDTH + j * PAIR, t * PAIR
-            s.gmix_all[:, to : to + PAIR] = s.gmix_own[j, :, at : at + PAIR]
-    mark("grad_tokens")
-
-    def one_cols(i, carry):
-        at = pl.ds(pl.multiple_of(i * 256, 256), 256)
-        s.gn_one[:, at] = mm(s.gmix_all[...], s.wfull[at, :], NT)
-        return carry
-
-    lax.fori_loop(0, 4, one_cols, 0)
-
-    def token_rows(i, carry):
-        at = pl.ds(pl.multiple_of(i * 32, 32), 32)
-        grad_gain, grad_bias = carry
-        grad, norm = s.gn_one[at, :], s.hat_one[at, :]
-        scaled = grad * gain
-        inner = scaled - jnp.mean(scaled, -1, keepdims=True)
-        inner = inner - norm * jnp.mean(scaled * norm, -1, keepdims=True)
-        grad_tokens[at, :] = (s.grad_middle[at, :] + s.scale_one[at, :] * inner).astype(BF)
-        return (
-            grad_gain + jnp.sum(grad * norm, 0, keepdims=True),
-            grad_bias + jnp.sum(grad, 0, keepdims=True),
-        )
-
-    sums = lax.fori_loop(0, ROWS // 32, token_rows, (jnp.zeros((1, WIDTH), F32),) * 2)
-    put_row(s.gs, 0, sums[0])
-    put_row(s.gs, 1, sums[1])
-    gs_slots, far_slots = net.slots(NB), net.slots(NC)
-    for j in batch_others:
-        net.send(s.gs.at[j], s.gs_box.at[b], (j, c), gs_slots + b)
-
-    mark("gs_sum")
-    total = s.gs[pl.ds(b, 1)][0]
-    for j in batch_others:
-        net.wait(gs_slots + j, s.gs_box.at[j])
-        total = total + s.gs_box[pl.ds(j, 1)][0]
-    s.gs_sum[...] = total
-    for i in range(1, NC):
-        j = lax.rem(c + i, NC)
-        net.send(s.gs_sum, s.gs_far.at[c], (b, j), far_slots + c)
-    mark("gather_part_2")
+    gather_qkv.corner()
+    gather_qkv.pass_on(1)
+    gather_fc[0].stage(3)
+    gather_out[1].stage(3)
+    gather_fc[1].pass_on(2)
+    grad_in()
+    gather_fc[1].stage(2)
+    gather_fc[1].pass_on(3)
     gather_part.stage(2)
-    mark("gather_fc_2")
-    gather_fc.stage(2)
-    mark("gather_part_3")
+    gs_sum()
     gather_part.stage(3)
-    mark("gather_fc_3")
-    gather_fc.stage(3)
-    mark("far_sum")
-    for i in range(1, NC):
-        j = lax.rem(c - i + NC, NC)
-        net.wait(far_slots + j, s.gs_far.at[j])
-        total = total + s.gs_far[pl.ds(j, 1)][0]
-    grad_small[...] = total
-    mark("out_end")
-    gather_out.finish()
-    mark("qkv_end")
-    gather_qkv.finish()
-    mark("part_end")
-    gather_part.finish()
-    mark("fc_end")
-    gather_fc.finish()
-    mark("drain")
-    for copy in keep:
+    gather_qkv.pass_on(2)
+    gather_fc[1].stage(3)
+    layer_end()
+    gather_qkv.pass_on(3)
+    far_sum()
+    for gather in gather_out + gather_fc + [gather_qkv, gather_part]:
+        gather.finish()
+    for copy in v.keep:
         copy.wait()
     net.drain()
-    mark(None)
 
 
 VECTOR_ROWS = (1, 1, 2, 1, 1, 1, 4, 1)
-STEPS = 8
+STEPS = 2
 
 
 def widen_kernel(layer, grad_in, small, w_qkv, w_proj, w_fc, w_out, *outs):
@@ -1514,8 +1567,9 @@
     o_out[...] = w_out[...].astype(F32)
     for j in range(NB):
         for x in range(2):
-            to, at = j * WIDTH + x * 512, j * 512
-            o_fc[:, to : to + 512] = w_fc[x, :, at : at + 512].astype(F32)
+            for i in range(2):
+                to, at = j * WIDTH + x * 512 + i * 256, j * 256
+                o_fc[:, to : to + 256] = w_fc[x, i, :, at : at + 256].astype(F32)
 
     @pl.when(pl.program_id(0) == 0)
     def _():
@@ -1540,7 +1594,7 @@
             shape((SMALL_ROWS, SHARD), F32),
             shape((NC, SHARD, 3 * PAIR), BF),
             shape((SHARD, WIDTH), BF),
-            shape((2, SHARD, FF // 2), BF),
+            shape((2, 2, SHARD, WIDTH), BF),
             shape((FF // NB, WIDTH), BF),
         ),
         in_specs=[vmem] * 10 + [anywhere] * 4,
@@ -1563,7 +1617,7 @@
     def rows(count, width):
         return pl.BlockSpec((count // STEPS, width), lambda i: (i, 0))
 
-    half = pl.BlockSpec((2, SHARD // STEPS, FF // 2), lambda i: (0, i, 0))
+    half = pl.BlockSpec((2, 2, SHARD // STEPS, WIDTH), lambda i: (0, 0, i, 0))
     smalls = [pl.BlockSpec((n * SHARD,), lambda i: (0,)) for n in VECTOR_ROWS]
     layer, grad_in, w_qkv, w_proj, w_fc, w_out, *vectors = pl.pallas_call(
         widen_kernel,

time: 201 us -> 186 us (0.925)
  Pallas kernels: 200 us -> 185 us
    pallas_call x1, Pallas kernels: 191 us -> 178 us  [per_device_fast(): pl.pallas_call(layer_kernel, out_shape=(shape((ROWS, WIDTH), BF), shape((...]
    pallas_call x1, Pallas kernels: 9.37 us -> 7.35 us  [per_device_fast(): pl.pallas_call(widen_kernel, grid=(STEPS,), out_shape=(shape((ROWS, WIDTH...]
where the time goes in v3:
time: 186 us
  Pallas kernels  185 us (99%)
    pallas_call x1, Pallas kernels, per_device_fast(): pl.pallas_call(layer_kernel, out_shape=(shape((ROWS, WIDTH), BF), shape((...  178 us
    pallas_call x1, Pallas kernels, per_device_fast(): pl.pallas_call(widen_kernel, grid=(STEPS,), out_shape=(shape((ROWS, WIDTH...  7.35 us

profile of v3, /device:TPU:0, one launch (start us, length us, event | category | flops | bytes accessed | tf_op | source)
XLA Modules:
  0.0 185.8 jit_solution(8752066185361915190)
XLA Ops:
  0.7 177.7 %shard_map.245 = (bf16[128,1024]{1,0:T(8,128)(2,1)}, bf16[128,1024]{1,0:T(8,128)(2,1)}, f32[16,256]{1,0:T(8,128)}, bf16[8,256,384]{2,1,0:T(8,128)(2,1)}, bf16[25...) custom-call(bf16[128,1024]{1,0:T(8,128)(2,1)} %bitcast.4, ...), custom_call_target="tpu_custom_call" | custom-call | tf_op jit(solution)/shard_map/pallas_call | solution.py:1589
  178.3 7.4 %shard_map.246 = (bf16[128,1024]{1,0:T(8,128)(2,1)}, bf16[128,1024]{1,0:T(8,128)(2,1)}, f32[256,3072]{1,0:T(8,128)}, f32[256,1024]{1,0:T(8,128)}, f32[256,4096]{...) custom-call(bf16[128,1024]{1,0:T(8,128)(2,1)} %get-tuple-element.35., ...), custom_call_target="tpu_custom_call" | custom-call | tf_op jit(solution)/shard_map/pallas_call | solution.py:1622

commit v4 on v3

--- a/solution.py
+++ b/solution.py
@@ -443,23 +443,21 @@
         for i, src in enumerate(srcs):
             self.begin(i, src)
 
-    def stage(self, d):
+    def stage(self, d, sign):
         net, count = self.net, self.count
-        for sign in (-1, 1):
-            zz = net.z + sign * d
-            here = zz >= 0 if sign < 0 else zz <= 3
-            refs = self.views(2 * zz + net.x)
-            onward = both(here, net.z < 3 if sign < 0 else net.z > 0)
-            dsts = self.views(2 * zz + net.x)
-            for i in range(count):
-                slot = self.along + zz * count + i
-                pl.when(here)(lambda slot=slot, ref=refs[i]: net.wait(slot, ref))
-                if d < 3:
-                    net.send(refs[i], dsts[i], (net.b, net.c - 2 * sign), slot, onward)
-                goes = here
-                if self.turn and i == count - 1:
-                    goes = both(here, jnp.logical_and(zz > 0, zz < 3))
-                net.send(refs[i], dsts[i], (net.b, net.side), self.beside + zz * count + i, goes)
+        zz = net.z + sign * d
+        here = zz >= 0 if sign < 0 else zz <= 3
+        refs = self.views(2 * zz + net.x)
+        onward = both(here, net.z < 3 if sign < 0 else net.z > 0)
+        for i in range(count):
+            slot = self.along + zz * count + i
+            pl.when(here)(lambda slot=slot, ref=refs[i]: net.wait(slot, ref))
+            if d < 3:
+                net.send(refs[i], refs[i], (net.b, net.c - 2 * sign), slot, onward)
+            goes = here
+            if self.turn and i == count - 1:
+                goes = both(here, jnp.logical_and(zz > 0, zz < 3))
+            net.send(refs[i], refs[i], (net.b, net.side), self.beside + zz * count + i, goes)
 
     def piece(self, end):
         return self.views(2 * end + 1 - self.net.x)[self.count - 1]
@@ -532,15 +530,13 @@
 
         self.give(k, upward, when)
 
-    def launch(self):
-        for k in (1, 2, 3):
-            self.give(4 - k, True, self.net.z == 0)
-            self.give(k - 1, False, self.net.z == 3)
-
-    def pass_one(self):
-        for k in (0, 1):
-            self.take(3 - k, True, self.net.z == 1)
-            self.take(k, False, self.net.z == 2)
+    def launch(self, k):
+        self.give(3 - k, True, self.net.z == 0)
+        self.give(k, False, self.net.z == 3)
+
+    def pass_one(self, k):
+        self.take(3 - k, True, self.net.z == 1)
+        self.take(k, False, self.net.z == 2)
 
     def pass_two(self):
         self.take(0, False, self.net.z == 1)
@@ -581,7 +577,6 @@
             self.net.wait(self.slots + k, self.beside.at[k])
             mine = self.line.mine(k)
             add_into(mine, [mine, self.beside.at[k]])
-        self.line.launch()
 
 
 class SwapCtx:
@@ -747,13 +742,13 @@
             for kb in range(qb + 1):
                 keys = slice(kb * QB, (kb + 1) * QB)
                 scores = scores_of(mix[keys, PAIR : 2 * PAIR], query, kb == qb)
-                work[h, keys, :] = scores
+                work[keys, :] = scores
                 peak = jnp.max(scores, axis=0, keepdims=True)
                 top = peak if top is None else jnp.maximum(top, peak)
             total = None
             for kb in range(qb + 1):
                 keys = slice(kb * QB, (kb + 1) * QB)
-                grown = jnp.exp(work[h, keys, :] - top)
+                grown = jnp.exp(work[keys, :] - top)
                 part = jnp.sum(grown, axis=0, keepdims=True)
                 total = part if total is None else total + part
                 low_work[h, keys, :] = grown.astype(BF)
@@ -786,12 +781,12 @@
                 grad_probs = mm(mix[keys, 2 * PAIR :], grad, NT)
                 part = jnp.sum(probs * grad_probs, axis=0, keepdims=True)
                 delta = part if delta is None else delta + part
-                work[h, keys, :] = probs
-                more[h, keys, :] = grad_probs
+                work[keys, :] = probs
+                more[keys, :] = grad_probs
                 low_work[h, keys, :] = probs.astype(BF)
             for kb in range(qb + 1):
                 keys = slice(kb * QB, (kb + 1) * QB)
-                low_more[h, keys, :] = (work[h, keys, :] * (more[h, keys, :] - delta)).astype(BF)
+                low_more[h, keys, :] = (work[keys, :] * (more[keys, :] - delta)).astype(BF)
             grad_v[:count, :] += mm(low_work[h, :count, :], grad)
             grad_k[:count, :] += mm(low_more[h, :count, :], query)
             rows = slice(h * HEAD_DIM, (h + 1) * HEAD_DIM)
@@ -813,7 +808,10 @@
     return x * half, slope
 
 
+VECTOR_ROWS = (1, 1, 2, 1, 1, 1, 4, 1)
 SCRATCH = dict(
+    tokens=((ROWS, WIDTH), BF),
+    **{f"v{i}": ((rows * SHARD,), BF) for i, rows in enumerate(VECTOR_ROWS)},
     small=((SMALL_ROWS, SHARD), F32),
     parts=((NB, SMALL_ROWS, SHARD), F32),
     qv_rows=((16, PAIR), F32),
@@ -825,13 +823,14 @@
     g_all=((NB * ROWS, WIDTH), BF),
     hat_one=((ROWS, WIDTH), F32),
     scale_one=((ROWS, 1), F32),
+    hat_all=((LENGTH, WIDTH), BF),
     n_one=((LENGTH, WIDTH), BF),
     mix=((LENGTH, 3 * PAIR), BF),
     turned=((PAIR, LENGTH), BF),
     att=((LENGTH, PAIR), BF),
     lse=((8, QB), F32),
-    work=((2, LENGTH, QB), F32),
-    more=((2, LENGTH, QB), F32),
+    work=((LENGTH, QB), F32),
+    more=((LENGTH, QB), F32),
     low_work=((2, LENGTH, QB), BF),
     low_more=((2, LENGTH, QB), BF),
     att_own=((ROWS, WIDTH), BF),
@@ -884,8 +883,8 @@
     gs_sum=((SMALL_ROWS, SHARD), F32),
     gs_far=((NC, SMALL_ROWS, SHARD), F32),
 )
-TURN_OUT, TURN_FC = (False, True), (False, True)
-SENDS, RECVS, LOCALS = 64, 260, 16
+TURN_OUT, TURN_FC = (False, False), (False, False)
+SENDS, RECVS, LOCALS = 48, 240, 26
 
 
 def layer_kernel(*refs):
@@ -926,12 +925,12 @@
 
     batch_others = [lax.rem(b + i, NB) for i in range(1, NB)]
 
-    small_slots, fc_slots, fc_near_slots = net.slots(NB), net.slots(NB), net.slots(NB)
+    small_slots, fc_slots = net.slots(NB), net.slots(2 * NB)
     hidden_slots, pre_slots, side_slot, swap_slots = net.slots(4), net.slots(4), net.slots(1), net.slots(2 * NB)
     proj_slots, proj_side_slot, proj_near_slots = net.slots(NB), net.slots(1), net.slots(2)
     gs_slots, far_slots = net.slots(NB), net.slots(NC)
     gather_pair = GatherBatch(net, lambda j: [rows_of(s.wpair, SHARD)(j)])
-    gather_one = GatherCtx(net, lambda j: halves(s.n_one, ROWS, j), 2, True)
+    gather_one = GatherCtx(net, lambda j: halves(s.hat_all, ROWS, j), 2, True)
     gather_g = GatherBatch(net, lambda j: [rows_of(s.g_all, ROWS)(j)])
     gather_gs = GatherSide(net, rows_of(s.g_side, ROWS))
     gather_ns = GatherBatch(net, lambda j: [rows_of(s.n_side, ROWS)(j)])
@@ -973,21 +972,26 @@
     gather_part = GatherCtx(net, lambda j: [rows_of(o_proj, 32)(j)], 1)
 
     scale, hat = s.scale_one, s.hat_one
-    half, pair_z = net.z % 2, net.c + 2 - 4 * (net.z % 2)
-    half_rows = pl.ds(pl.multiple_of(half * (SHARD // 2), SHARD // 2), SHARD // 2)
-    other_rows = pl.ds(pl.multiple_of((1 - half) * (SHARD // 2), SHARD // 2), SHARD // 2)
     side_rows = pl.ds(pl.multiple_of(net.x * (SHARD // 2), SHARD // 2), SHARD // 2)
     other_side_rows = pl.ds(pl.multiple_of((1 - net.x) * (SHARD // 2), SHARD // 2), SHARD // 2)
     chip_rows = [
         pl.ds(pl.multiple_of(first * 256, 256), 256) for first in (b // 2, 1 - b // 2)
     ]
-    n_mine = rows_of(s.n_one, ROWS)(c)
+    hat_mine = rows_of(s.hat_all, ROWS)(c)
     n_two_mine = own(s.n_two, ROWS)
     g_mine = own(s.g_all, ROWS)
     n_beside = own(s.n_side, ROWS)
 
     def enter():
-        v.get_pair = [
+        barrier = pltpu.get_barrier_semaphore()
+        others = [(j, c) for j in batch_others]
+        others += [(b, lax.rem(c + i, NC)) for i in range(1, NC)]
+        for device in others:
+            pl.semaphore_signal(barrier, inc=1, device_id=device, device_id_type=MESH)
+        get_tokens = local(tokens, s.tokens)
+        own_vectors = [getattr(s, f"v{i}") for i in range(len(vectors))]
+        get_vectors = [local(one, two) for one, two in zip(vectors, own_vectors)]
+        get_pair = [
             local(cols(wqkv, t * WIDTH + c * PAIR), own(s.wpair, SHARD).at[:, t * PAIR : (t + 1) * PAIR])
             for t in range(3)
         ]
@@ -998,24 +1002,23 @@
             local(wqkv, own(s.wfull, SHARD)),
             local(cotangent, g_mine),
         ]
-        barrier = pltpu.get_barrier_semaphore()
-        others = [(j, c) for j in batch_others]
-        others += [(b, lax.rem(c + i, NC)) for i in range(1, NC)]
-        for device in others:
-            pl.semaphore_signal(barrier, inc=1, device_id=device, device_id_type=MESH)
         s.small[...] = jnp.zeros_like(s.small)
+        for copy in get_vectors:
+            copy.wait()
         row = 0
-        for vector in vectors:
+        for vector in own_vectors:
             for i in range(vector.shape[0] // SHARD):
                 piece = vector[i * SHARD : (i + 1) * SHARD].astype(F32)
                 s.small[row : row + 1, :] = piece.reshape(1, SHARD)
                 row += 1
 
         def norm_rows(at):
-            hat[at, :], scale[at, :] = normalise(tokens[at, :].astype(F32))
-
+            hat[at, :], scale[at, :] = normalise(s.tokens[at, :].astype(F32))
+            hat_mine[at, :] = hat[at, :].astype(BF)
+
+        get_tokens.wait()
         loop(ROWS // 32, 32, norm_rows)
-        for copy in v.get_pair:
+        for copy in get_pair:
             copy.wait()
         s.parts[pl.ds(b, 1)] = s.small[...][None]
         pl.semaphore_wait(barrier, len(others))
@@ -1030,16 +1033,13 @@
     def g_start():
         gather_g.start([cotangent])
 
-    def norm_one():
+    def one_start():
+        gather_one.start(halves(s.hat_all, ROWS, c))
+
+    def small_wait():
         for j in batch_others:
             net.wait(small_slots + j, s.parts.at[j])
-        gain, bias = row_of(s.parts, 0), row_of(s.parts, 1)
-
-        def gain_rows(at):
-            n_mine[at, :] = (hat[at, :] * gain + bias).astype(BF)
-
-        loop(ROWS // 32, 32, gain_rows)
-        gather_one.start(halves(s.n_one, ROWS, c))
+        v.gain, v.bias = row_of(s.parts, 0), row_of(s.parts, 1)
 
     def proj_start():
         mine = own(s.wproj_all, SHARD)
@@ -1057,21 +1057,11 @@
         net.wait(proj_side_slot, block)
         net.send(block, block, (net.sib, c), proj_near_slots + 1)
 
-    def fc_start():
-        net.send(cols(wfc, net.sib * WIDTH, WIDTH), own(s.wfc_mine, SHARD), (net.sib, c), fc_slots + b)
-        for j in (net.across, net.diag):
-            net.send(
-                wfc.at[half_rows, pl.ds(pl.multiple_of(j * WIDTH, WIDTH), WIDTH)],
-                own(s.wfc_mine, SHARD).at[half_rows],
-                (j, c),
-                fc_slots + b,
-            )
-
-    def fc_relay():
-        for j in (net.across, net.diag):
-            block = rows_of(s.wfc_mine, SHARD)(j).at[half_rows]
-            net.wait(fc_slots + j, block)
-            net.send(block, block, (b, pair_z), fc_near_slots + j)
+    def fc_start(i):
+        at = slice(i * (SHARD // 2), (i + 1) * (SHARD // 2))
+        for j in (net.across, net.diag, net.sib):
+            cut = wfc.at[at, pl.ds(pl.multiple_of(j * WIDTH, WIDTH), WIDTH)]
+            net.send(cut, own(s.wfc_mine, SHARD).at[at], (j, c), fc_slots + 2 * b + i)
 
     def qv_rows():
         for p in range(NC):
@@ -1095,15 +1085,29 @@
     def gs_relay_across():
         gather_gs.relay(net.across)
 
-    def mix():
+    def mix_block(j):
+        rows = pl.ds(pl.multiple_of(j * ROWS, ROWS), ROWS)
         mix_bias = jnp.concatenate(
             [s.qv_rows[pl.ds(c, 1), :], jnp.zeros((1, PAIR), F32), s.qv_rows[pl.ds(8 + c, 1), :]], axis=1
         )
-
-        def mix_rows(at):
-            s.mix[at, :] = (mm(s.n_one[at, :], s.wpair[...]) + mix_bias).astype(BF)
-
-        loop(LENGTH // QB, QB, mix_rows)
+        s.n_one[rows, :] = (s.hat_all[rows, :].astype(F32) * v.gain + v.bias).astype(BF)
+        s.mix[rows, :] = (mm(s.n_one[rows, :], s.wpair[...]) + mix_bias).astype(BF)
+
+    def mix_at(d):
+        if d == 0:
+            mix_block(c)
+        for zz in (net.z - d, net.z + d)[: 2 * d]:
+
+            @pl.when(jnp.logical_and(zz >= 0, zz <= 3))
+            def _():
+                mix_block(2 * zz + net.x)
+
+    def mix_side():
+        def step(zz, carry):
+            mix_block(2 * zz + 1 - net.x)
+            return carry
+
+        lax.fori_loop(0, 4, step, 0)
 
     def att():
         def ready(qb):
@@ -1121,7 +1125,7 @@
 
     def middle():
         def middle_cols(at):
-            s.middle[:, at] = mm(s.att_own[...], s.wproj_all[:, at]) + tokens[:, at].astype(F32)
+            s.middle[:, at] = mm(s.att_own[...], s.wproj_all[:, at]) + s.tokens[:, at].astype(F32)
 
         loop(WIDTH // 256, 256, middle_cols)
         proj_bias, gain_two, bias_two = row_of(s.parts, 4), row_of(s.parts, 5), row_of(s.parts, 6)
@@ -1147,9 +1151,9 @@
         for copy in v.get_rest:
             copy.wait()
         gather_g.finish()
-        net.wait(fc_slots + net.sib, rows_of(s.wfc_mine, SHARD)(net.sib))
-        for j in (net.across, net.diag):
-            net.wait(fc_near_slots + j, rows_of(s.wfc_mine, SHARD)(j).at[other_rows])
+        for j in batch_others:
+            for i, block in enumerate(halves(s.wfc_mine, SHARD, j)):
+                net.wait(fc_slots + 2 * j + i, block)
         s.gs[...] = jnp.zeros_like(s.gs)
 
     def feed_cols(r, i):
@@ -1244,7 +1248,6 @@
         s.p_out[i] = (
             mm(mine[...], s.g_all[...], TN) + mm(s.hidden_side[:, at], s.g_side[...], TN)
         ).astype(BF)
-        reduce_out[i].launch()
 
     def out_done(i):
         part = s.out_block.at[i * 64 : (i + 1) * 64]
@@ -1265,7 +1268,6 @@
             return carry
 
         lax.fori_loop(0, 4, fc_rows, 0)
-        reduce_fc[i].launch()
 
     def fc_done(i):
         reduce_fc[i].finish(s.fc_sum.at[i])
@@ -1369,7 +1371,7 @@
             for t in range(3):
                 to, at = t * WIDTH + j * PAIR, t * PAIR
                 s.gmix_all[:, to : to + PAIR] = s.gmix_own[j, :, at : at + PAIR]
-        gain = row_of(s.parts, 0)
+        gain = v.gain
 
         def one_cols(at):
             s.gn_one[:, at] = mm(s.gmix_all[...], s.wfull[at, :], NT)
@@ -1414,134 +1416,172 @@
         grad_small[...] = total
 
     enter()
+    one_start()
     send_small()
-    norm_one()
+    pair_start()
+    small_wait()
     g_start()
-    pair_start()
-    gather_one.stage(1)
+    proj_start()
+    gather_one.stage(1,-1)
+    gather_one.stage(1,1)
     gather_one.corner()
-    proj_start()
+    gather_pair.relay()
+    gather_one.stage(2,-1)
     gather_one.pass_on(1)
-    gather_one.stage(2)
-    gather_pair.relay()
     qv_rows()
-    gather_one.stage(3)
+    gather_one.stage(2,1)
+    gather_one.pass_on(2)
+    fc_start(0)
+    gather_one.stage(3,1)
+    gather_one.stage(3,-1)
     proj_relay()
     gather_pair.finish()
-    fc_start()
+    mix_at(0)
+    gs_give_own()
     g_relay()
-    gs_give_own()
-    gather_one.pass_on(2)
+    mix_at(1)
+    mix_at(2)
     gather_one.pass_on(3)
+    mix_at(3)
     gather_one.finish()
-    mix()
+    mix_side()
+    fc_start(1)
     att()
-    fc_relay()
-    gs_give_across()
     proj_side()
     proj_finish()
+    gs_give_across()
     swap_att.finish()
     middle()
     ns_give()
+    gs_relay_own()
     gs_relay_across()
-    gs_relay_own()
     gather_gs.finish()
+    feed_wait()
     gather_two.near()
-    feed_wait()
     feed_i(0,0)
     gather_two.relay()
     gather_two.far()
     feed_i(1,0)
     feed_i(1,1)
     feed_i(0,1)
+    pre_give(0,0)
+    pre_give(0,1)
+    ns_start()
     feed_rest(1)
+    norm_diag()
     feed_rest(0)
+    p_out(0)
+    reduce_out[0].launch(0)
+    pre_give(1,0)
+    norm_across()
+    reduce_norm.cross()
+    reduce_out[0].pass_one(0)
+    pre_give(1,1)
+    reduce_out[0].launch(1)
     norm_sib()
-    ns_start()
-    norm_across()
-    p_out(0)
-    norm_diag()
-    reduce_norm.cross()
-    pre_give(1,0)
-    reduce_out[0].pass_one()
     p_out(1)
-    pre_give(0,0)
-    full_start(1)
-    pre_give(1,1)
+    reduce_out[1].launch(0)
+    reduce_out[0].pass_one(1)
     norm_own()
+    gather_ns.relay()
+    reduce_out[0].pass_two()
+    reduce_out[1].pass_one(0)
+    reduce_out[1].launch(1)
+    reduce_out[0].launch(2)
     back_two()
-    reduce_out[0].pass_two()
-    reduce_out[1].pass_one()
-    pre_give(0,1)
-    gather_ns.relay()
+    p_proj()
+    reduce_out[1].launch(2)
+    reduce_out[1].pass_one(1)
+    reduce_out[1].pass_two()
+    reduce_proj.cross()
     gather_ns.finish()
+    p_fc(0)
+    reduce_fc[0].launch(0)
     out_done(0)
-    p_proj()
-    reduce_proj.cross()
-    reduce_out[1].pass_two()
-    p_fc(0)
     out_done(1)
     p_fc(1)
+    reduce_fc[0].pass_one(0)
+    p_layer()
+    full_start(0)
+    gather_out[0].stage(1,-1)
+    gather_out[0].stage(1,1)
+    reduce_fc[0].launch(1)
+    gather_out[1].stage(1,1)
+    proj_done()
+    gather_out[1].stage(1,-1)
+    reduce_fc[0].pass_one(1)
+    reduce_fc[0].pass_two()
     swap_grad.finish()
-    gather_out[1].corner()
-    gather_out[0].stage(1)
     att_back()
+    mix_give(3)
     mix_give(0)
-    mix_give(3)
-    gqv()
     p_qkv()
     reduce_qkv.cross()
-    reduce_fc[0].pass_one()
-    proj_done()
-    gather_out[1].stage(1)
-    gather_out[0].stage(2)
-    full_start(0)
-    reduce_fc[1].pass_one()
-    reduce_fc[0].pass_two()
+    reduce_part.fold()
+    reduce_part.line.launch(1)
+    reduce_fc[0].launch(2)
+    gather_out[0].stage(2,1)
+    reduce_part.line.launch(0)
+    gather_out[0].stage(2,-1)
+    reduce_fc[1].launch(0)
+    reduce_part.line.pass_one(0)
+    reduce_part.line.pass_one(1)
+    gqv()
+    gather_full[0].relay()
+    reduce_fc[1].launch(1)
     fc_done(0)
+    gather_out[1].stage(2,1)
+    gather_out[1].stage(2,-1)
+    reduce_part.line.launch(2)
+    reduce_fc[1].pass_one(0)
+    reduce_part.line.pass_two()
+    reduce_fc[1].launch(2)
+    full_start(1)
     qkv_done()
-    gather_out[1].pass_on(1)
+    mix_give(2)
+    reduce_fc[1].pass_one(1)
+    reduce_fc[1].pass_two()
+    gather_out[0].stage(3,-1)
+    gather_out[0].stage(3,1)
+    gather_out[1].stage(3,-1)
+    gather_out[1].stage(3,1)
+    mix_give(1)
+    fc_swap(0)
+    gather_qkv.stage(1,-1)
+    part_done()
+    gather_qkv.stage(1,1)
+    fc_done(1)
+    fc_swap(1)
+    gather_part.stage(1,1)
+    gather_qkv.corner()
+    gather_fc[0].stage(1,1)
+    reduce_layer.cross()
+    gather_qkv.stage(2,-1)
     gather_full[1].relay()
-    gather_out[0].stage(3)
-    gather_out[1].stage(2)
-    reduce_fc[1].pass_two()
-    reduce_part.fold()
-    reduce_part.line.pass_one()
-    fc_swap(0)
-    mix_give(1)
-    gather_qkv.stage(1)
-    mix_give(2)
-    gather_full[0].relay()
-    reduce_part.line.pass_two()
-    gather_fc[0].stage(1)
-    gather_out[1].pass_on(2)
-    fc_done(1)
-    p_layer()
-    fc_swap(1)
-    reduce_layer.cross()
-    gather_out[1].pass_on(3)
-    gather_qkv.stage(2)
-    part_done()
-    gather_fc[0].stage(2)
-    gather_fc[1].corner()
-    gather_fc[1].pass_on(1)
-    gather_fc[1].stage(1)
-    gather_qkv.stage(3)
-    gather_part.stage(1)
-    gather_qkv.corner()
+    gather_fc[0].stage(1,-1)
+    gather_part.stage(1,-1)
+    gather_fc[1].stage(1,1)
+    gather_qkv.stage(3,-1)
+    gather_part.stage(2,1)
+    gather_fc[0].stage(2,1)
+    gather_fc[1].stage(1,-1)
+    gather_qkv.stage(2,1)
+    gather_fc[1].stage(2,1)
+    gather_part.stage(2,-1)
+    layer_end()
+    gather_fc[0].stage(2,-1)
+    gather_fc[1].stage(2,-1)
     gather_qkv.pass_on(1)
-    gather_fc[0].stage(3)
-    gather_out[1].stage(3)
-    gather_fc[1].pass_on(2)
     grad_in()
-    gather_fc[1].stage(2)
-    gather_fc[1].pass_on(3)
-    gather_part.stage(2)
+    gather_qkv.pass_on(2)
+    gather_qkv.stage(3,1)
+    gather_fc[0].stage(3,-1)
+    gather_fc[1].stage(3,-1)
+    gather_fc[0].stage(3,1)
     gs_sum()
-    gather_part.stage(3)
-    gather_qkv.pass_on(2)
-    gather_fc[1].stage(3)
-    layer_end()
+    gather_fc[1].stage(3,1)
+    gather_part.stage(3,1)
+    gather_part.stage(3,-1)
     gather_qkv.pass_on(3)
     far_sum()
     for gather in gather_out + gather_fc + [gather_qkv, gather_part]:
@@ -1551,33 +1591,45 @@
     net.drain()
 
 
-VECTOR_ROWS = (1, 1, 2, 1, 1, 1, 4, 1)
-STEPS = 2
-
-
-def widen_kernel(layer, grad_in, small, w_qkv, w_proj, w_fc, w_out, *outs):
-    o_layer, o_grad_in, o_qkv, o_proj, o_fc, o_out = outs[:6]
-    o_layer[...] = layer[...]
-    o_grad_in[...] = grad_in[...]
-    for j in range(NC):
-        for t in range(3):
-            to, at = t * WIDTH + j * PAIR, t * PAIR
-            o_qkv[:, to : to + PAIR] = w_qkv[j, :, at : at + PAIR].astype(F32)
-    o_proj[...] = w_proj[...].astype(F32)
-    o_out[...] = w_out[...].astype(F32)
-    for j in range(NB):
-        for x in range(2):
-            for i in range(2):
-                to, at = j * WIDTH + x * 512 + i * 256, j * 256
-                o_fc[:, to : to + 256] = w_fc[x, i, :, at : at + 256].astype(F32)
-
-    @pl.when(pl.program_id(0) == 0)
-    def _():
-        row = 0
-        for out in outs[6:]:
-            for i in range(out.shape[0] // SHARD):
-                out[i * SHARD : (i + 1) * SHARD] = small[row, :]
-                row += 1
+PARTS = 4
+
+
+def widen_kernel(layer, grad_in, small, w_qkv, w_proj, w_fc, w_out, *refs):
+    o_layer, o_grad_in, o_qkv, o_proj, o_fc, o_out = refs[:6]
+    vectors, (qkv, proj, fc, out, sems) = refs[6:14], refs[14:]
+    leaving = []
+
+    def leave(src, dst):
+        copy = pltpu.make_async_copy(src, dst, sems.at[len(leaving)])
+        copy.start()
+        leaving.append(copy)
+
+    for k in range(PARTS):
+        wide, at = slice(k * 256, (k + 1) * 256), slice(k * 64, (k + 1) * 64)
+        out[wide, :] = w_out[wide, :].astype(F32)
+        leave(out.at[wide], o_out.at[wide])
+        for j in range(NB):
+            for x in range(2):
+                for i in range(2):
+                    to = j * WIDTH + x * 512 + i * 256
+                    fc[at, to : to + 256] = w_fc[x, i, at, j * 256 : (j + 1) * 256].astype(F32)
+        leave(fc.at[at], o_fc.at[at])
+        for j in range(NC):
+            for t in range(3):
+                to = t * WIDTH + j * PAIR
+                qkv[at, to : to + PAIR] = w_qkv[j, at, t * PAIR : (t + 1) * PAIR].astype(F32)
+        leave(qkv.at[at], o_qkv.at[at])
+        proj[at, :] = w_proj[at, :].astype(F32)
+        leave(proj.at[at], o_proj.at[at])
+    leave(layer, o_layer)
+    leave(grad_in, o_grad_in)
+    row = 0
+    for vector in vectors:
+        for i in range(vector.shape[0] // SHARD):
+            vector[i * SHARD : (i + 1) * SHARD] = small[row, :]
+            row += 1
+    for copy in leaving:
+        copy.wait()
 
 
 def per_device_fast(
@@ -1589,16 +1641,16 @@
     layer, grad_in, grad_small, w_qkv, w_proj, w_fc, w_out = pl.pallas_call(
         layer_kernel,
         out_shape=(
-            shape((ROWS, WIDTH), BF),
-            shape((ROWS, WIDTH), BF),
-            shape((SMALL_ROWS, SHARD), F32),
-            shape((NC, SHARD, 3 * PAIR), BF),
-            shape((SHARD, WIDTH), BF),
-            shape((2, 2, SHARD, WIDTH), BF),
-            shape((FF // NB, WIDTH), BF),
+            pltpu.VMEM((ROWS, WIDTH), BF),
+            pltpu.VMEM((ROWS, WIDTH), BF),
+            pltpu.VMEM((SMALL_ROWS, SHARD), F32),
+            pltpu.VMEM((NC, SHARD, 3 * PAIR), BF),
+            pltpu.VMEM((SHARD, WIDTH), BF),
+            pltpu.VMEM((2, 2, SHARD, WIDTH), BF),
+            pltpu.VMEM((FF // NB, WIDTH), BF),
         ),
-        in_specs=[vmem] * 10 + [anywhere] * 4,
-        out_specs=(vmem, vmem, vmem, anywhere, anywhere, anywhere, anywhere),
+        in_specs=[anywhere] * 14,
+        out_specs=(vmem,) * 7,
         scratch_shapes=[pltpu.VMEM(*item) for item in SCRATCH.values()]
         + [
             pltpu.SemaphoreType.DMA((SENDS,)),
@@ -1606,22 +1658,15 @@
             pltpu.SemaphoreType.DMA((LOCALS,)),
         ],
         compiler_params=pltpu.CompilerParams(
-            collective_id=0, has_side_effects=True, vmem_limit_bytes=VMEM_BYTES
+            collective_id=0, has_side_effects=True, vmem_limit_bytes=LAYER_VMEM
         ),
     )(
         tokens.reshape(ROWS, WIDTH), cotangent.reshape(ROWS, WIDTH),
         ln1_gain, ln1_bias, qv_bias, proj_bias, ln2_gain, ln2_bias, fc_bias, out_bias,
         qkv_weight, proj_weight, fc_weight, out_weight,
     )
-
-    def rows(count, width):
-        return pl.BlockSpec((count // STEPS, width), lambda i: (i, 0))
-
-    half = pl.BlockSpec((2, 2, SHARD // STEPS, WIDTH), lambda i: (0, 0, i, 0))
-    smalls = [pl.BlockSpec((n * SHARD,), lambda i: (0,)) for n in VECTOR_ROWS]
     layer, grad_in, w_qkv, w_proj, w_fc, w_out, *vectors = pl.pallas_call(
         widen_kernel,
-        grid=(STEPS,),
         out_shape=(
             shape((ROWS, WIDTH), BF),
             shape((ROWS, WIDTH), BF),
@@ -1631,25 +1676,16 @@
             shape((FF // NB, WIDTH), F32),
             *[shape((n * SHARD,), F32) for n in VECTOR_ROWS],
         ),
-        in_specs=[
-            rows(ROWS, WIDTH),
-            rows(ROWS, WIDTH),
-            pl.BlockSpec((SMALL_ROWS, SHARD), lambda i: (0, 0)),
-            pl.BlockSpec((NC, SHARD // STEPS, 3 * PAIR), lambda i: (0, i, 0)),
-            rows(SHARD, WIDTH),
-            half,
-            rows(FF // NB, WIDTH),
+        in_specs=[vmem] * 7,
+        out_specs=(anywhere,) * 6 + (vmem,) * len(VECTOR_ROWS),
+        scratch_shapes=[
+            pltpu.VMEM((SHARD, 3 * WIDTH), F32),
+            pltpu.VMEM((SHARD, WIDTH), F32),
+            pltpu.VMEM((SHARD, FF), F32),
+            pltpu.VMEM((FF // NB, WIDTH), F32),
+            pltpu.SemaphoreType.DMA((4 * PARTS + 2,)),
         ],
-        out_specs=(
-            rows(ROWS, WIDTH),
-            rows(ROWS, WIDTH),
-            rows(SHARD, 3 * WIDTH),
-            rows(SHARD, WIDTH),
-            rows(SHARD, FF),
-            rows(FF // NB, WIDTH),
-            *smalls,
-        ),
-        compiler_params=pltpu.CompilerParams(vmem_limit_bytes=VMEM_BYTES),
+        compiler_params=pltpu.CompilerParams(vmem_limit_bytes=WIDEN_VMEM),
     )(layer, grad_in, grad_small, w_qkv, w_proj, w_fc, w_out)
     return (
         layer.reshape(tokens.shape),
@@ -1669,7 +1705,7 @@
     )
 
 
-VMEM_BYTES = 62 * 1024 * 1024
+LAYER_VMEM, WIDEN_VMEM = 55 * 1024 * 1024, 20 * 1024 * 1024
 
 
 def solution(mesh):

time: 186 us -> 175 us (0.941)
  Pallas kernels: 185 us -> 174 us
    pallas_call x2, Pallas kernels: 185 us -> 174 us  [the longest x1 168 us: per_device_fast(): pl.pallas_call(layer_kernel, out_shape=(pltpu.VMEM((ROWS, WIDTH), BF), pl...]
where the time goes in v4:
time: 175 us
  Pallas kernels  174 us (99%)
    pallas_call x1, Pallas kernels, per_device_fast(): pl.pallas_call(layer_kernel, out_shape=(pltpu.VMEM((ROWS, WIDTH), BF), pl...  168 us
    pallas_call x1, Pallas kernels, per_device_fast(): pl.pallas_call(widen_kernel, out_shape=(shape((ROWS, WIDTH), BF), shape((...  5.54 us

profile of v4, /device:TPU:0, one launch (start us, length us, event | category | flops | bytes accessed | tf_op | source)
XLA Modules:
  0.0 174.7 jit_solution(14092589047236174737)
XLA Ops:
  0.7 168.3 %shard_map.245 = (bf16[128,1024]{1,0:T(8,128)(2,1)S(1)}, bf16[128,1024]{1,0:T(8,128)(2,1)S(1)}, f32[16,256]{1,0:T(8,128)S(1)}, bf16[8,256,384]{2,1,0:T(8,128)(2,...) custom-call(bf16[128,1024]{1,0:T(8,128)(2,1)} %bitcast.4, ...), custom_call_target="tpu_custom_call" | custom-call | tf_op jit(solution)/shard_map/pallas_call | solution.py:1641
  168.9 5.5 %shard_map.246 = (bf16[128,1024]{1,0:T(8,128)(2,1)}, bf16[128,1024]{1,0:T(8,128)(2,1)}, f32[256,3072]{1,0:T(8,128)}, f32[256,1024]{1,0:T(8,128)}, f32[256,4096]{...) custom-call(bf16[128,1024]{1,0:T(8,128)(2,1)S(1)} %get-tuple-element, ...), custom_call_target="tpu_custom_call" | custom-call | tf_op jit(solution)/shard_map/pallas_call | solution.py:1668

commit v5 on v4

--- a/solution.py
+++ b/solution.py
@@ -427,15 +427,21 @@
 
 
 class GatherCtx:
-    def __init__(self, net, views, count, turn=False):
-        self.net, self.views, self.count, self.turn = net, views, count, turn
-        self.along, self.beside = net.slots(4 * count), net.slots(4 * count)
-        self.turned = net.slots(2) if turn else None
+    def __init__(self, net, views, others, count, turn=False):
+        self.net, self.views, self.others, self.count, self.turn = net, views, others, count, turn
+        self.along, self.beside = net.slots(4 * count), net.slots(1)
+        self.turned = net.slots(4) if turn else None
 
     def begin(self, i, src):
         net, count = self.net, self.count
         dst, at = self.views(net.c)[i], net.z * count + i
-        net.send(src, dst, (net.b, net.side), self.beside + at)
+        if self.turn and i == count - 1:
+            end = jnp.logical_or(net.z == 0, net.z == 3)
+            net.send(src, dst, (net.b, net.side), self.turned + 2, net.z == 0)
+            net.send(src, dst, (net.b, net.side), self.turned + 3, net.z == 3)
+            net.send(src, dst, (net.b, net.side), self.beside, jnp.logical_not(end))
+        else:
+            net.send(src, dst, (net.b, net.side), self.beside)
         net.send(src, dst, (net.b, net.c + 2), self.along + at, net.z < 3)
         net.send(src, dst, (net.b, net.c - 2), self.along + at, net.z > 0)
 
@@ -457,15 +463,15 @@
             goes = here
             if self.turn and i == count - 1:
                 goes = both(here, jnp.logical_and(zz > 0, zz < 3))
-            net.send(refs[i], refs[i], (net.b, net.side), self.beside + zz * count + i, goes)
+            net.send(refs[i], refs[i], (net.b, net.side), self.beside, goes)
 
     def piece(self, end):
         return self.views(2 * end + 1 - self.net.x)[self.count - 1]
 
     def corner(self):
-        net, count = self.net, self.count
+        net = self.net
         for end, step in ((0, 2), (3, -2)):
-            ref, slot = self.piece(end), self.beside + end * count + count - 1
+            ref, slot = self.piece(end), self.turned + 2 + (end > 0)
             pl.when(net.z == end)(lambda slot=slot, ref=ref: net.wait(slot, ref))
             net.send(ref, ref, (net.b, net.c + step), self.turned + (end > 0), net.z == end)
 
@@ -479,12 +485,7 @@
                 net.send(ref, ref, (net.b, net.c + step), slot, here)
 
     def finish(self):
-        net, count = self.net, self.count
-        for zz in range(4):
-            refs = self.views(2 * zz + 1 - net.x)
-            for i in range(count):
-                if not (self.turn and i == count - 1 and zz in (0, 3)):
-                    net.wait(self.beside + zz * count + i, refs[i])
+        self.net.wait(self.beside, self.others)
 
 
 def chunks(ref):
@@ -580,52 +581,24 @@
 
 
 class SwapCtx:
-    def __init__(self, net, src, dst, count):
-        self.net, self.src, self.dst, self.count = net, src, dst, count
-        self.base = net.slots(NC * count)
+    def __init__(self, net, src, dst, others):
+        self.net, self.src, self.dst, self.others = net, src, dst, others
+        self.slot = net.slots(1)
 
     def give(self, j):
-        net, count = self.net, self.count
-        srcs, dsts = self.src(j), self.dst(net.c)
-        for i in range(count):
-            net.send(srcs[i], dsts[i], (net.b, j), self.base + net.c * count + i, net.c != j)
+        net, src, dst = self.net, self.src(j), self.dst(self.net.c)
+        net.send(src, dst, (net.b, j), self.slot, net.c != j)
 
         @pl.when(net.c == j)
         def _():
-            for one, two in zip(srcs, dsts):
-                two[...] = one[...]
+            dst[...] = src[...]
 
     def start(self):
         for j in range(NC):
             self.give(j)
 
     def finish(self):
-        net, count = self.net, self.count
-        for step in range(1, NC):
-            j = lax.rem(net.c - step + NC, NC)
-            dsts = self.dst(j)
-            for i in range(count):
-                net.wait(self.base + j * count + i, dsts[i])
-
-
-class GatherSide:
-    def __init__(self, net, views):
-        self.net, self.views = net, views
-        self.far, self.near = net.slots(NB), net.slots(NB)
-
-    def give(self, j, src):
-        net = self.net
-        net.send(src, self.views(j), (net.b, net.side), self.far + j)
-
-    def relay(self, j):
-        net, ref = self.net, self.views(j)
-        net.wait(self.far + j, ref)
-        net.send(ref, ref, (net.sib, net.c), self.near + j)
-
-    def finish(self):
-        net = self.net
-        for j in (net.sib, net.diag):
-            net.wait(self.near + j, self.views(j))
+        self.net.wait(self.slot, self.others)
 
 
 class GatherBatch:
@@ -883,8 +856,7 @@
     gs_sum=((SMALL_ROWS, SHARD), F32),
     gs_far=((NC, SMALL_ROWS, SHARD), F32),
 )
-TURN_OUT, TURN_FC = (False, False), (False, False)
-SENDS, RECVS, LOCALS = 48, 240, 26
+SENDS, RECVS, LOCALS = 40, 176, 26
 
 
 def layer_kernel(*refs):
@@ -925,27 +897,27 @@
 
     batch_others = [lax.rem(b + i, NB) for i in range(1, NB)]
 
-    small_slots, fc_slots = net.slots(NB), net.slots(2 * NB)
-    hidden_slots, pre_slots, side_slot, swap_slots = net.slots(4), net.slots(4), net.slots(1), net.slots(2 * NB)
+    small_slot, fc_slots, fc_side_slots = net.slots(1), net.slots(2 * NB), net.slots(NB)
+    hidden_slots, pre_slots, side_slot, swap_slots = net.slots(4), net.slots(4), net.slots(2), net.slots(2)
     proj_slots, proj_side_slot, proj_near_slots = net.slots(NB), net.slots(1), net.slots(2)
-    gs_slots, far_slots = net.slots(NB), net.slots(NC)
+    gs_slot, far_slot = net.slots(1), net.slots(1)
     gather_pair = GatherBatch(net, lambda j: [rows_of(s.wpair, SHARD)(j)])
-    gather_one = GatherCtx(net, lambda j: halves(s.hat_all, ROWS, j), 2, True)
+    gather_one = GatherCtx(net, lambda j: halves(s.hat_all, ROWS, j), s.hat_all.at[: 3 * ROWS], 2, True)
     gather_g = GatherBatch(net, lambda j: [rows_of(s.g_all, ROWS)(j)])
-    gather_gs = GatherSide(net, rows_of(s.g_side, ROWS))
+    gather_gs = GatherBatch(net, lambda j: [rows_of(s.g_side, ROWS)(j)])
     gather_ns = GatherBatch(net, lambda j: [rows_of(s.n_side, ROWS)(j)])
     gather_two = GatherBatch(net, lambda j: halves(s.n_two, ROWS, j), 2)
     gather_full = [
         GatherBatch(net, lambda j, i=i: [rows_of(s.wfull, SHARD // 2)(2 * j + i)]) for i in range(2)
     ]
     swap_att = SwapCtx(
-        net, lambda j: [rows_of(s.att, ROWS)(j)], lambda j: [cols(s.att_own, j * PAIR)], 1
+        net, rows_of(s.att, ROWS), lambda j: cols(s.att_own, j * PAIR), s.att_own.at[:, : 7 * PAIR]
     )
     swap_grad = SwapCtx(
-        net, lambda j: [cols(s.g_att, j * PAIR)], lambda j: [rows_of(s.dout, ROWS)(j)], 1
+        net, lambda j: cols(s.g_att, j * PAIR), rows_of(s.dout, ROWS), s.dout.at[: 7 * ROWS]
     )
     swap_mix = SwapCtx(
-        net, lambda j: [rows_of(s.gmix, ROWS)(j)], lambda j: [s.gmix_own.at[j]], 1
+        net, rows_of(s.gmix, ROWS), lambda j: s.gmix_own.at[j], s.gmix_own.at[:7]
     )
     reduce_norm = ReduceBatch(net, rows_of(s.p_norm, ROWS), s.p_norm_box)
     reduce_layer = ReduceBatch(net, rows_of(s.p_layer, ROWS), s.p_layer_box)
@@ -966,14 +938,18 @@
     def fc_view(i, j):
         return o_fc.at[j % 2, i, pl.ds(pl.multiple_of((j // 2) * 64, 64), 64)]
 
-    gather_out = [GatherCtx(net, lambda j, i=i: [out_view(i, j)], 1, TURN_OUT[i]) for i in range(2)]
-    gather_fc = [GatherCtx(net, lambda j, i=i: [fc_view(i, j)], 1, TURN_FC[i]) for i in range(2)]
-    gather_qkv = GatherCtx(net, lambda j: halves(o_qkv.at[j], SHARD, 0), 2, True)
-    gather_part = GatherCtx(net, lambda j: [rows_of(o_proj, 32)(j)], 1)
+    gather_out = [GatherCtx(net, lambda j, i=i: [out_view(i, j)], o_out.at[:256], 1) for i in range(2)]
+    gather_fc = [GatherCtx(net, lambda j, i=i: [fc_view(i, j)], o_fc.at[0, 0], 1) for i in range(2)]
+    gather_qkv = GatherCtx(net, lambda j: halves(o_qkv.at[j], SHARD, 0), o_qkv.at[:3], 2, True)
+    gather_part = GatherCtx(net, lambda j: [rows_of(o_proj, 32)(j)], o_proj.at[:128], 1)
 
     scale, hat = s.scale_one, s.hat_one
-    side_rows = pl.ds(pl.multiple_of(net.x * (SHARD // 2), SHARD // 2), SHARD // 2)
-    other_side_rows = pl.ds(pl.multiple_of((1 - net.x) * (SHARD // 2), SHARD // 2), SHARD // 2)
+    half, pair_z = net.z % 2, (b, c + 2 - 4 * (net.z % 2))
+    fc_rows = [
+        pl.ds(pl.multiple_of(SHARD // 2 + x * (SHARD // 4), SHARD // 4), SHARD // 4) for x in (half, 1 - half)
+    ]
+    side_rows = pl.ds(pl.multiple_of(half * (SHARD // 2), SHARD // 2), SHARD // 2)
+    other_side_rows = pl.ds(pl.multiple_of((1 - half) * (SHARD // 2), SHARD // 2), SHARD // 2)
     chip_rows = [
         pl.ds(pl.multiple_of(first * 256, 256), 256) for first in (b // 2, 1 - b // 2)
     ]
@@ -1025,7 +1001,7 @@
 
     def send_small():
         for j in batch_others:
-            net.send(s.small, s.parts.at[b], (j, c), small_slots + b)
+            net.send(s.small, s.parts.at[b], (j, c), small_slot)
 
     def pair_start():
         gather_pair.start([own(s.wpair, SHARD)])
@@ -1037,8 +1013,7 @@
         gather_one.start(halves(s.hat_all, ROWS, c))
 
     def small_wait():
-        for j in batch_others:
-            net.wait(small_slots + j, s.parts.at[j])
+        net.wait(small_slot, s.parts.at[: NB - 1])
         v.gain, v.bias = row_of(s.parts, 0), row_of(s.parts, 1)
 
     def proj_start():
@@ -1049,7 +1024,7 @@
     def proj_relay():
         block = rows_of(s.wproj_all, SHARD)(net.across).at[side_rows]
         net.wait(proj_slots + net.across, block)
-        net.send(block, block, (b, net.side), proj_side_slot)
+        net.send(block, block, pair_z, proj_side_slot)
         net.send(block, block, (net.sib, c), proj_near_slots)
 
     def proj_side():
@@ -1058,10 +1033,18 @@
         net.send(block, block, (net.sib, c), proj_near_slots + 1)
 
     def fc_start(i):
-        at = slice(i * (SHARD // 2), (i + 1) * (SHARD // 2))
-        for j in (net.across, net.diag, net.sib):
+        at = [slice(0, SHARD // 2), fc_rows[0]][i]
+        for j in (net.across, net.diag):
             cut = wfc.at[at, pl.ds(pl.multiple_of(j * WIDTH, WIDTH), WIDTH)]
             net.send(cut, own(s.wfc_mine, SHARD).at[at], (j, c), fc_slots + 2 * b + i)
+        if i == 0:
+            net.send(cols(wfc, net.sib * WIDTH, WIDTH), own(s.wfc_mine, SHARD), (net.sib, c), fc_slots + 2 * b)
+
+    def fc_relay():
+        for j in (net.across, net.diag):
+            block = rows_of(s.wfc_mine, SHARD)(j).at[fc_rows[0]]
+            net.wait(fc_slots + 2 * j + 1, block)
+            net.send(block, block, pair_z, fc_side_slots + j)
 
     def qv_rows():
         for p in range(NC):
@@ -1073,17 +1056,12 @@
     def g_relay():
         gather_g.relay()
 
-    def gs_give_own():
-        gather_gs.give(b, cotangent)
-
-    def gs_give_across():
-        gather_gs.give(net.across, rows_of(s.g_all, ROWS)(net.across))
-
-    def gs_relay_own():
-        gather_gs.relay(b)
-
-    def gs_relay_across():
-        gather_gs.relay(net.across)
+    def gs_give():
+        net.send(cotangent, own(s.g_side, ROWS), (b, net.side), side_slot + 1)
+
+    def gs_start():
+        net.wait(side_slot + 1, own(s.g_side, ROWS))
+        gather_gs.start([own(s.g_side, ROWS)])
 
     def mix_block(j):
         rows = pl.ds(pl.multiple_of(j * ROWS, ROWS), ROWS)
@@ -1151,9 +1129,11 @@
         for copy in v.get_rest:
             copy.wait()
         gather_g.finish()
-        for j in batch_others:
-            for i, block in enumerate(halves(s.wfc_mine, SHARD, j)):
-                net.wait(fc_slots + 2 * j + i, block)
+        net.wait(fc_slots + 2 * net.sib, rows_of(s.wfc_mine, SHARD)(net.sib))
+        for j in (net.across, net.diag):
+            block = rows_of(s.wfc_mine, SHARD)(j)
+            net.wait(fc_slots + 2 * j, block.at[0 : SHARD // 2])
+            net.wait(fc_side_slots + j, block.at[fc_rows[1]])
         s.gs[...] = jnp.zeros_like(s.gs)
 
     def feed_cols(r, i):
@@ -1273,13 +1253,11 @@
         reduce_fc[i].finish(s.fc_sum.at[i])
         mine = pl.ds(pl.multiple_of(b * 256, 256), 256)
         for j in batch_others:
-            net.send(s.fc_sum.at[i, j], s.fc_block.at[i, :, mine], (j, c), swap_slots + 2 * b + i)
+            net.send(s.fc_sum.at[i, j], s.fc_block.at[i, :, mine], (j, c), swap_slots + i)
         s.fc_block[i, :, mine] = s.fc_sum[i, pl.ds(b, 1)][0]
 
     def fc_swap(i):
-        for j in batch_others:
-            at = pl.ds(pl.multiple_of(j * 256, 256), 256)
-            net.wait(swap_slots + 2 * j + i, s.fc_block.at[i, :, at])
+        net.wait(swap_slots + i, s.fc_block.at[i, :, : (NB - 1) * 256])
         gather_fc[i].begin(0, s.fc_block.at[i])
         v.keep.append(local(s.fc_block.at[i], fc_view(i, c)))
 
@@ -1395,23 +1373,23 @@
         put_row(s.gs, 0, sums[0])
         put_row(s.gs, 1, sums[1])
         for j in batch_others:
-            net.send(s.gs.at[j], s.gs_box.at[b], (j, c), gs_slots + b)
+            net.send(s.gs.at[j], s.gs_box.at[b], (j, c), gs_slot)
 
     def gs_sum():
         total = s.gs[pl.ds(b, 1)][0]
+        net.wait(gs_slot, s.gs_box.at[: NB - 1])
         for j in batch_others:
-            net.wait(gs_slots + j, s.gs_box.at[j])
             total = total + s.gs_box[pl.ds(j, 1)][0]
         s.gs_sum[...] = total
         for i in range(1, NC):
             j = lax.rem(c + i, NC)
-            net.send(s.gs_sum, s.gs_far.at[c], (b, j), far_slots + c)
+            net.send(s.gs_sum, s.gs_far.at[c], (b, j), far_slot)
 
     def far_sum():
         total = s.gs_sum[...]
+        net.wait(far_slot, s.gs_far.at[: NC - 1])
         for i in range(1, NC):
             j = lax.rem(c - i + NC, NC)
-            net.wait(far_slots + j, s.gs_far.at[j])
             total = total + s.gs_far[pl.ds(j, 1)][0]
         grad_small[...] = total
 
@@ -1420,170 +1398,170 @@
     send_small()
     pair_start()
     small_wait()
-    g_start()
+    gather_one.stage(1,-1)
+    gather_one.corner()
     proj_start()
-    gather_one.stage(1,-1)
     gather_one.stage(1,1)
-    gather_one.corner()
+    fc_start(1)
     gather_pair.relay()
+    gather_pair.finish()
+    qv_rows()
     gather_one.stage(2,-1)
     gather_one.pass_on(1)
-    qv_rows()
     gather_one.stage(2,1)
+    gather_one.stage(3,-1)
+    mix_at(0)
+    mix_at(1)
+    g_start()
+    mix_at(2)
     gather_one.pass_on(2)
+    gather_one.stage(3,1)
+    proj_relay()
+    gs_give()
+    mix_at(3)
     fc_start(0)
-    gather_one.stage(3,1)
-    gather_one.stage(3,-1)
-    proj_relay()
-    gather_pair.finish()
-    mix_at(0)
-    gs_give_own()
-    g_relay()
-    mix_at(1)
-    mix_at(2)
     gather_one.pass_on(3)
-    mix_at(3)
     gather_one.finish()
     mix_side()
-    fc_start(1)
     att()
     proj_side()
     proj_finish()
-    gs_give_across()
     swap_att.finish()
+    fc_relay()
     middle()
+    gs_start()
     ns_give()
-    gs_relay_own()
-    gs_relay_across()
-    gather_gs.finish()
+    g_relay()
     feed_wait()
     gather_two.near()
     feed_i(0,0)
     gather_two.relay()
+    ns_start()
     gather_two.far()
     feed_i(1,0)
     feed_i(1,1)
-    feed_i(0,1)
-    pre_give(0,0)
-    pre_give(0,1)
-    ns_start()
     feed_rest(1)
     norm_diag()
+    feed_i(0,1)
+    pre_give(0,1)
+    gather_gs.relay()
     feed_rest(0)
+    gather_gs.finish()
     p_out(0)
     reduce_out[0].launch(0)
-    pre_give(1,0)
     norm_across()
+    reduce_out[0].launch(1)
     reduce_norm.cross()
-    reduce_out[0].pass_one(0)
-    pre_give(1,1)
-    reduce_out[0].launch(1)
-    norm_sib()
+    gather_ns.relay()
+    norm_own()
     p_out(1)
     reduce_out[1].launch(0)
+    pre_give(1,1)
+    pre_give(0,0)
+    reduce_out[0].pass_one(0)
+    reduce_out[0].launch(2)
+    pre_give(1,0)
+    norm_sib()
     reduce_out[0].pass_one(1)
-    norm_own()
-    gather_ns.relay()
+    reduce_out[1].launch(1)
+    back_two()
+    p_proj()
     reduce_out[0].pass_two()
     reduce_out[1].pass_one(0)
-    reduce_out[1].launch(1)
-    reduce_out[0].launch(2)
-    back_two()
-    p_proj()
-    reduce_out[1].launch(2)
+    reduce_proj.cross()
+    out_done(0)
     reduce_out[1].pass_one(1)
-    reduce_out[1].pass_two()
-    reduce_proj.cross()
     gather_ns.finish()
     p_fc(0)
     reduce_fc[0].launch(0)
-    out_done(0)
+    full_start(1)
+    reduce_out[1].pass_two()
+    reduce_out[1].launch(2)
+    gather_out[0].stage(1,1)
+    gather_out[0].stage(1,-1)
+    p_fc(1)
+    reduce_fc[0].launch(1)
+    reduce_fc[0].pass_one(0)
     out_done(1)
-    p_fc(1)
-    reduce_fc[0].pass_one(0)
-    p_layer()
-    full_start(0)
-    gather_out[0].stage(1,-1)
-    gather_out[0].stage(1,1)
-    reduce_fc[0].launch(1)
-    gather_out[1].stage(1,1)
+    reduce_fc[1].launch(0)
+    swap_grad.finish()
+    gather_out[0].stage(2,1)
     proj_done()
-    gather_out[1].stage(1,-1)
+    reduce_fc[0].launch(2)
+    gather_out[0].stage(2,-1)
     reduce_fc[0].pass_one(1)
     reduce_fc[0].pass_two()
-    swap_grad.finish()
     att_back()
+    gather_out[0].stage(3,1)
+    gather_out[1].stage(1,-1)
+    gather_out[0].stage(3,-1)
+    reduce_fc[1].launch(1)
+    gather_out[1].stage(1,1)
     mix_give(3)
     mix_give(0)
     p_qkv()
+    fc_done(0)
     reduce_qkv.cross()
     reduce_part.fold()
     reduce_part.line.launch(1)
-    reduce_fc[0].launch(2)
-    gather_out[0].stage(2,1)
+    reduce_fc[1].pass_one(0)
     reduce_part.line.launch(0)
-    gather_out[0].stage(2,-1)
-    reduce_fc[1].launch(0)
+    gqv()
+    gather_out[1].stage(2,1)
+    full_start(0)
+    gather_out[1].stage(2,-1)
+    fc_swap(0)
+    gather_full[1].relay()
+    reduce_fc[1].launch(2)
     reduce_part.line.pass_one(0)
-    reduce_part.line.pass_one(1)
-    gqv()
-    gather_full[0].relay()
-    reduce_fc[1].launch(1)
-    fc_done(0)
-    gather_out[1].stage(2,1)
-    gather_out[1].stage(2,-1)
-    reduce_part.line.launch(2)
-    reduce_fc[1].pass_one(0)
-    reduce_part.line.pass_two()
-    reduce_fc[1].launch(2)
-    full_start(1)
     qkv_done()
-    mix_give(2)
     reduce_fc[1].pass_one(1)
     reduce_fc[1].pass_two()
-    gather_out[0].stage(3,-1)
-    gather_out[0].stage(3,1)
+    gather_fc[0].stage(1,1)
     gather_out[1].stage(3,-1)
+    p_layer()
+    gather_fc[0].stage(1,-1)
+    mix_give(1)
+    reduce_part.line.pass_one(1)
+    reduce_part.line.pass_two()
+    gather_qkv.stage(1,1)
     gather_out[1].stage(3,1)
-    mix_give(1)
-    fc_swap(0)
     gather_qkv.stage(1,-1)
+    fc_done(1)
+    gather_qkv.corner()
+    reduce_part.line.launch(2)
+    mix_give(2)
+    gather_fc[0].stage(2,-1)
+    fc_swap(1)
     part_done()
-    gather_qkv.stage(1,1)
-    fc_done(1)
-    fc_swap(1)
+    gather_qkv.stage(2,-1)
+    gather_full[0].relay()
+    gather_fc[0].stage(3,-1)
+    gather_fc[0].stage(2,1)
+    gather_qkv.stage(2,1)
+    gather_fc[1].stage(1,1)
+    gather_fc[1].stage(1,-1)
+    grad_in()
+    gather_fc[0].stage(3,1)
+    gather_qkv.stage(3,1)
     gather_part.stage(1,1)
-    gather_qkv.corner()
-    gather_fc[0].stage(1,1)
+    gather_qkv.stage(3,-1)
     reduce_layer.cross()
-    gather_qkv.stage(2,-1)
-    gather_full[1].relay()
-    gather_fc[0].stage(1,-1)
     gather_part.stage(1,-1)
-    gather_fc[1].stage(1,1)
-    gather_qkv.stage(3,-1)
-    gather_part.stage(2,1)
-    gather_fc[0].stage(2,1)
-    gather_fc[1].stage(1,-1)
-    gather_qkv.stage(2,1)
+    gather_fc[1].stage(2,-1)
+    gather_qkv.pass_on(1)
     gather_fc[1].stage(2,1)
     gather_part.stage(2,-1)
-    layer_end()
-    gather_fc[0].stage(2,-1)
-    gather_fc[1].stage(2,-1)
-    gather_qkv.pass_on(1)
-    grad_in()
-    gather_qkv.pass_on(2)
-    gather_qkv.stage(3,1)
-    gather_fc[0].stage(3,-1)
+    gs_sum()
+    gather_part.stage(2,1)
+    gather_fc[1].stage(3,1)
     gather_fc[1].stage(3,-1)
-    gather_fc[0].stage(3,1)
-    gs_sum()
-    gather_fc[1].stage(3,1)
     gather_part.stage(3,1)
     gather_part.stage(3,-1)
+    gather_qkv.pass_on(2)
+    far_sum()
     gather_qkv.pass_on(3)
-    far_sum()
+    layer_end()
     for gather in gather_out + gather_fc + [gather_qkv, gather_part]:
         gather.finish()
     for copy in v.keep:
@@ -1596,7 +1574,7 @@
 
 def widen_kernel(layer, grad_in, small, w_qkv, w_proj, w_fc, w_out, *refs):
     o_layer, o_grad_in, o_qkv, o_proj, o_fc, o_out = refs[:6]
-    vectors, (qkv, proj, fc, out, sems) = refs[6:14], refs[14:]
+    vectors, rows, (qkv, proj, fc, out, sems) = refs[6:14], refs[14:22], refs[22:]
     leaving = []
 
     def leave(src, dst):
@@ -1604,6 +1582,14 @@
         copy.start()
         leaving.append(copy)
 
+    row = 0
+    for vector, here in zip(vectors, rows):
+        for i in range(vector.shape[0] // SHARD):
+            here[i * SHARD : (i + 1) * SHARD] = small[row, :]
+            row += 1
+        leave(here, vector)
+    leave(layer, o_layer)
+    leave(grad_in, o_grad_in)
     for k in range(PARTS):
         wide, at = slice(k * 256, (k + 1) * 256), slice(k * 64, (k + 1) * 64)
         out[wide, :] = w_out[wide, :].astype(F32)
@@ -1621,13 +1607,6 @@
         leave(qkv.at[at], o_qkv.at[at])
         proj[at, :] = w_proj[at, :].astype(F32)
         leave(proj.at[at], o_proj.at[at])
-    leave(layer, o_layer)
-    leave(grad_in, o_grad_in)
-    row = 0
-    for vector in vectors:
-        for i in range(vector.shape[0] // SHARD):
-            vector[i * SHARD : (i + 1) * SHARD] = small[row, :]
-            row += 1
     for copy in leaving:
         copy.wait()
 
@@ -1677,13 +1656,14 @@
             *[shape((n * SHARD,), F32) for n in VECTOR_ROWS],
         ),
         in_specs=[vmem] * 7,
-        out_specs=(anywhere,) * 6 + (vmem,) * len(VECTOR_ROWS),
+        out_specs=(anywhere,) * (6 + len(VECTOR_ROWS)),
         scratch_shapes=[
+            *[pltpu.VMEM((n * SHARD,), F32) for n in VECTOR_ROWS],
             pltpu.VMEM((SHARD, 3 * WIDTH), F32),
             pltpu.VMEM((SHARD, WIDTH), F32),
             pltpu.VMEM((SHARD, FF), F32),
             pltpu.VMEM((FF // NB, WIDTH), F32),
-            pltpu.SemaphoreType.DMA((4 * PARTS + 2,)),
+            pltpu.SemaphoreType.DMA((4 * PARTS + 2 + len(VECTOR_ROWS),)),
         ],
         compiler_params=pltpu.CompilerParams(vmem_limit_bytes=WIDEN_VMEM),
     )(layer, grad_in, grad_small, w_qkv, w_proj, w_fc, w_out)

time: 175 us -> 172 us (0.983)
  Pallas kernels: 174 us -> 171 us
    pallas_call x1, Pallas kernels: 168 us -> 166 us  [per_device_fast(): pl.pallas_call(layer_kernel, out_shape=(pltpu.VMEM((ROWS, WIDTH), BF), pl...]
where the time goes in v5:
time: 172 us; the launch traced here: 171 us
  Pallas kernels  171 us (99%)
    pallas_call x1, Pallas kernels, per_device_fast(): pl.pallas_call(layer_kernel, out_shape=(pltpu.VMEM((ROWS, WIDTH), BF), pl...  166 us
    pallas_call x1, Pallas kernels, per_device_fast(): pl.pallas_call(widen_kernel, out_shape=(shape((ROWS, WIDTH), BF), shape((...  4.97 us

profile of v5, /device:TPU:0, one launch (start us, length us, event | category | flops | bytes accessed | tf_op | source)
XLA Modules:
  0.0 171.4 jit_solution(12354353156223748419)
XLA Ops:
  0.7 165.6 %shard_map.245 = (bf16[128,1024]{1,0:T(8,128)(2,1)S(1)}, bf16[128,1024]{1,0:T(8,128)(2,1)S(1)}, f32[16,256]{1,0:T(8,128)S(1)}, bf16[8,256,384]{2,1,0:T(8,128)(2,...) custom-call(bf16[128,1024]{1,0:T(8,128)(2,1)} %bitcast.4, ...), custom_call_target="tpu_custom_call" | custom-call | tf_op jit(solution)/shard_map/pallas_call | solution.py:1620
  166.3 5.0 %shard_map.246 = (bf16[128,1024]{1,0:T(8,128)(2,1)}, bf16[128,1024]{1,0:T(8,128)(2,1)}, f32[256,3072]{1,0:T(8,128)}, f32[256,1024]{1,0:T(8,128)}, f32[256,4096]{...) custom-call(bf16[128,1024]{1,0:T(8,128)(2,1)S(1)} %get-tuple-element, ...), custom_call_target="tpu_custom_call" | custom-call | tf_op jit(solution)/shard_map/pallas_call | solution.py:1647

commit v6 on v5

--- a/solution.py
+++ b/solution.py
@@ -856,7 +856,7 @@
     gs_sum=((SMALL_ROWS, SHARD), F32),
     gs_far=((NC, SMALL_ROWS, SHARD), F32),
 )
-SENDS, RECVS, LOCALS = 40, 176, 26
+SENDS, RECVS, LOCALS = 40, 180, 26
 
 
 def layer_kernel(*refs):
@@ -939,7 +939,7 @@
         return o_fc.at[j % 2, i, pl.ds(pl.multiple_of((j // 2) * 64, 64), 64)]
 
     gather_out = [GatherCtx(net, lambda j, i=i: [out_view(i, j)], o_out.at[:256], 1) for i in range(2)]
-    gather_fc = [GatherCtx(net, lambda j, i=i: [fc_view(i, j)], o_fc.at[0, 0], 1) for i in range(2)]
+    gather_fc = [GatherCtx(net, lambda j, i=i: [fc_view(i, j)], o_fc.at[0, 0, : 256 - 128 * i], 1, i == 1) for i in range(2)]
     gather_qkv = GatherCtx(net, lambda j: halves(o_qkv.at[j], SHARD, 0), o_qkv.at[:3], 2, True)
     gather_part = GatherCtx(net, lambda j: [rows_of(o_proj, 32)(j)], o_proj.at[:128], 1)
 
@@ -1395,173 +1395,177 @@
 
     enter()
     one_start()
-    send_small()
+    proj_start()
     pair_start()
-    small_wait()
+    g_start()
     gather_one.stage(1,-1)
     gather_one.corner()
-    proj_start()
     gather_one.stage(1,1)
-    fc_start(1)
+    gather_one.stage(2,-1)
+    gather_one.pass_on(1)
+    send_small()
     gather_pair.relay()
+    gather_one.stage(2,1)
+    gather_one.pass_on(2)
+    proj_relay()
+    gather_one.stage(3,-1)
+    small_wait()
+    gather_one.stage(3,1)
+    gs_give()
     gather_pair.finish()
     qv_rows()
-    gather_one.stage(2,-1)
-    gather_one.pass_on(1)
-    gather_one.stage(2,1)
-    gather_one.stage(3,-1)
+    fc_start(1)
+    fc_start(0)
     mix_at(0)
     mix_at(1)
-    g_start()
     mix_at(2)
-    gather_one.pass_on(2)
-    gather_one.stage(3,1)
-    proj_relay()
-    gs_give()
     mix_at(3)
-    fc_start(0)
     gather_one.pass_on(3)
     gather_one.finish()
     mix_side()
     att()
     proj_side()
+    g_relay()
     proj_finish()
     swap_att.finish()
     fc_relay()
     middle()
+    ns_give()
+    gather_two.near()
     gs_start()
-    ns_give()
-    g_relay()
     feed_wait()
-    gather_two.near()
     feed_i(0,0)
     gather_two.relay()
-    ns_start()
     gather_two.far()
     feed_i(1,0)
+    feed_i(0,1)
     feed_i(1,1)
+    ns_start()
+    pre_give(1,1)
     feed_rest(1)
-    norm_diag()
-    feed_i(0,1)
-    pre_give(0,1)
     gather_gs.relay()
+    pre_give(1,0)
     feed_rest(0)
     gather_gs.finish()
     p_out(0)
     reduce_out[0].launch(0)
+    reduce_out[0].launch(1)
+    norm_diag()
+    norm_sib()
     norm_across()
-    reduce_out[0].launch(1)
     reduce_norm.cross()
+    reduce_out[0].pass_one(0)
+    pre_give(0,0)
+    reduce_out[0].pass_one(1)
+    p_out(1)
+    reduce_out[1].launch(0)
+    reduce_out[0].launch(2)
+    reduce_out[1].launch(1)
     gather_ns.relay()
     norm_own()
-    p_out(1)
-    reduce_out[1].launch(0)
-    pre_give(1,1)
-    pre_give(0,0)
-    reduce_out[0].pass_one(0)
-    reduce_out[0].launch(2)
-    pre_give(1,0)
-    norm_sib()
-    reduce_out[0].pass_one(1)
-    reduce_out[1].launch(1)
+    reduce_out[1].pass_one(0)
+    reduce_out[0].pass_two()
+    pre_give(0,1)
     back_two()
     p_proj()
-    reduce_out[0].pass_two()
-    reduce_out[1].pass_one(0)
+    out_done(0)
+    gather_ns.finish()
     reduce_proj.cross()
-    out_done(0)
-    reduce_out[1].pass_one(1)
-    gather_ns.finish()
+    reduce_out[1].launch(2)
     p_fc(0)
     reduce_fc[0].launch(0)
+    reduce_out[1].pass_one(1)
+    reduce_out[1].pass_two()
+    gather_out[0].stage(1,1)
+    p_fc(1)
+    reduce_fc[1].launch(0)
+    reduce_fc[0].launch(1)
     full_start(1)
-    reduce_out[1].pass_two()
-    reduce_out[1].launch(2)
-    gather_out[0].stage(1,1)
     gather_out[0].stage(1,-1)
-    p_fc(1)
-    reduce_fc[0].launch(1)
-    reduce_fc[0].pass_one(0)
+    reduce_fc[1].launch(1)
     out_done(1)
-    reduce_fc[1].launch(0)
+    reduce_fc[1].launch(2)
     swap_grad.finish()
     gather_out[0].stage(2,1)
+    reduce_fc[0].pass_one(0)
+    att_back()
+    mix_give(3)
+    mix_give(0)
     proj_done()
-    reduce_fc[0].launch(2)
-    gather_out[0].stage(2,-1)
+    reduce_fc[1].pass_one(0)
+    gather_out[1].stage(1,-1)
     reduce_fc[0].pass_one(1)
     reduce_fc[0].pass_two()
-    att_back()
+    reduce_fc[1].pass_one(1)
+    p_qkv()
+    reduce_fc[1].pass_two()
+    gather_out[0].stage(2,-1)
+    reduce_qkv.cross()
+    gather_out[1].stage(1,1)
+    reduce_fc[0].launch(2)
+    reduce_part.fold()
+    reduce_part.line.launch(0)
+    reduce_part.line.launch(1)
+    gather_out[1].stage(2,-1)
     gather_out[0].stage(3,1)
-    gather_out[1].stage(1,-1)
+    reduce_part.line.pass_one(0)
+    fc_done(0)
+    reduce_part.line.launch(2)
+    qkv_done()
+    reduce_part.line.pass_one(1)
+    fc_done(1)
+    reduce_part.line.pass_two()
     gather_out[0].stage(3,-1)
-    reduce_fc[1].launch(1)
-    gather_out[1].stage(1,1)
-    mix_give(3)
-    mix_give(0)
-    p_qkv()
-    fc_done(0)
-    reduce_qkv.cross()
-    reduce_part.fold()
-    reduce_part.line.launch(1)
-    reduce_fc[1].pass_one(0)
-    reduce_part.line.launch(0)
+    fc_swap(0)
+    fc_swap(1)
+    full_start(0)
+    gather_qkv.stage(1,-1)
+    gather_out[1].stage(2,1)
+    gather_fc[0].stage(1,1)
+    gather_full[1].relay()
+    part_done()
+    mix_give(1)
+    gather_fc[1].stage(1,1)
+    gather_fc[1].corner()
+    gather_qkv.stage(1,1)
+    gather_part.stage(1,1)
+    mix_give(2)
+    gather_fc[0].stage(1,-1)
+    gather_qkv.stage(2,-1)
+    gather_out[1].stage(3,1)
+    gather_fc[1].stage(1,-1)
+    p_layer()
+    gather_full[0].relay()
     gqv()
-    gather_out[1].stage(2,1)
-    full_start(0)
-    gather_out[1].stage(2,-1)
-    fc_swap(0)
-    gather_full[1].relay()
-    reduce_fc[1].launch(2)
-    reduce_part.line.pass_one(0)
-    qkv_done()
-    reduce_fc[1].pass_one(1)
-    reduce_fc[1].pass_two()
-    gather_fc[0].stage(1,1)
+    gather_fc[0].stage(2,1)
+    gather_fc[0].stage(2,-1)
+    gather_qkv.corner()
+    reduce_layer.cross()
     gather_out[1].stage(3,-1)
-    p_layer()
-    gather_fc[0].stage(1,-1)
-    mix_give(1)
-    reduce_part.line.pass_one(1)
-    reduce_part.line.pass_two()
-    gather_qkv.stage(1,1)
-    gather_out[1].stage(3,1)
-    gather_qkv.stage(1,-1)
-    fc_done(1)
-    gather_qkv.corner()
-    reduce_part.line.launch(2)
-    mix_give(2)
-    gather_fc[0].stage(2,-1)
-    fc_swap(1)
-    part_done()
-    gather_qkv.stage(2,-1)
-    gather_full[0].relay()
-    gather_fc[0].stage(3,-1)
-    gather_fc[0].stage(2,1)
-    gather_qkv.stage(2,1)
-    gather_fc[1].stage(1,1)
-    gather_fc[1].stage(1,-1)
-    grad_in()
-    gather_fc[0].stage(3,1)
-    gather_qkv.stage(3,1)
-    gather_part.stage(1,1)
     gather_qkv.stage(3,-1)
-    reduce_layer.cross()
+    gather_fc[1].stage(2,1)
     gather_part.stage(1,-1)
     gather_fc[1].stage(2,-1)
+    gather_fc[1].pass_on(1)
+    grad_in()
+    gather_qkv.stage(2,1)
+    gather_part.stage(2,1)
+    gather_fc[0].stage(3,1)
+    gather_part.stage(2,-1)
     gather_qkv.pass_on(1)
-    gather_fc[1].stage(2,1)
-    gather_part.stage(2,-1)
+    gather_fc[1].pass_on(2)
+    gather_fc[0].stage(3,-1)
+    layer_end()
     gs_sum()
-    gather_part.stage(2,1)
+    gather_qkv.pass_on(2)
+    gather_part.stage(3,-1)
+    gather_qkv.stage(3,1)
+    gather_part.stage(3,1)
+    gather_fc[1].stage(3,-1)
+    far_sum()
+    gather_fc[1].pass_on(3)
     gather_fc[1].stage(3,1)
-    gather_fc[1].stage(3,-1)
-    gather_part.stage(3,1)
-    gather_part.stage(3,-1)
-    gather_qkv.pass_on(2)
-    far_sum()
     gather_qkv.pass_on(3)
-    layer_end()
     for gather in gather_out + gather_fc + [gather_qkv, gather_part]:
         gather.finish()
     for copy in v.keep:

time: 172 us -> 169 us (0.983)
  Pallas kernels: 171 us -> 167 us
    pallas_call x1, Pallas kernels: 166 us -> 162 us  [per_device_fast(): pl.pallas_call(layer_kernel, out_shape=(pltpu.VMEM((ROWS, WIDTH), BF), pl...]
where the time goes in v6:
time: 169 us; the launch traced here: 168 us
  Pallas kernels  167 us (99%)
    pallas_call x1, Pallas kernels, per_device_fast(): pl.pallas_call(layer_kernel, out_shape=(pltpu.VMEM((ROWS, WIDTH), BF), pl...  162 us
    pallas_call x1, Pallas kernels, per_device_fast(): pl.pallas_call(widen_kernel, out_shape=(shape((ROWS, WIDTH), BF), shape((...  4.97 us

profile of v6, /device:TPU:0, one launch (start us, length us, event | category | flops | bytes accessed | tf_op | source)
XLA Modules:
  0.0 168.2 jit_solution(13306648796057364291)
XLA Ops:
  0.7 162.4 %shard_map.245 = (bf16[128,1024]{1,0:T(8,128)(2,1)S(1)}, bf16[128,1024]{1,0:T(8,128)(2,1)S(1)}, f32[16,256]{1,0:T(8,128)S(1)}, bf16[8,256,384]{2,1,0:T(8,128)(2,...) custom-call(bf16[128,1024]{1,0:T(8,128)(2,1)} %bitcast.4, ...), custom_call_target="tpu_custom_call" | custom-call | tf_op jit(solution)/shard_map/pallas_call | solution.py:1624
  163.0 5.0 %shard_map.246 = (bf16[128,1024]{1,0:T(8,128)(2,1)}, bf16[128,1024]{1,0:T(8,128)(2,1)}, f32[256,3072]{1,0:T(8,128)}, f32[256,1024]{1,0:T(8,128)}, f32[256,4096]{...) custom-call(bf16[128,1024]{1,0:T(8,128)(2,1)S(1)} %get-tuple-element, ...), custom_call_target="tpu_custom_call" | custom-call | tf_op jit(solution)/shard_map/pallas_call | solution.py:1651

commit v7 on v6

--- a/solution.py
+++ b/solution.py
@@ -695,8 +695,11 @@
 QB = 256
 
 
+log2_e = 1.4426950408889634
+
+
 def scores_of(keys, query, masked):
-    scores = mm(keys, query, NT) * 0.125
+    scores = mm(keys, query, NT) * (0.125 * log2_e)
     if masked:
         key_pos = lax.broadcasted_iota(jnp.int32, scores.shape, 0)
         query_pos = lax.broadcasted_iota(jnp.int32, scores.shape, 1)
@@ -721,7 +724,7 @@
             total = None
             for kb in range(qb + 1):
                 keys = slice(kb * QB, (kb + 1) * QB)
-                grown = jnp.exp(work[keys, :] - top)
+                grown = jnp.exp2(work[keys, :] - top)
                 part = jnp.sum(grown, axis=0, keepdims=True)
                 total = part if total is None else total + part
                 low_work[h, keys, :] = grown.astype(BF)
@@ -729,7 +732,7 @@
             lanes = slice(h * HEAD_DIM, (h + 1) * HEAD_DIM)
             out = mm(value_t[lanes, :count], low_work[h, :count, :])
             outs.append(out / total)
-            lse[h * 4 + qb : h * 4 + qb + 1, :] = top + jnp.log(total)
+            lse[h * 4 + qb : h * 4 + qb + 1, :] = top + jnp.log2(total)
         att[here, :] = jnp.concatenate(outs, axis=0).T.astype(BF)
         ready(qb)
 
@@ -750,7 +753,7 @@
             delta = None
             for kb in range(qb + 1):
                 keys = slice(kb * QB, (kb + 1) * QB)
-                probs = jnp.exp(scores_of(mix[keys, PAIR : 2 * PAIR], query, kb == qb) - level)
+                probs = jnp.exp2(scores_of(mix[keys, PAIR : 2 * PAIR], query, kb == qb) - level)
                 grad_probs = mm(mix[keys, 2 * PAIR :], grad, NT)
                 part = jnp.sum(probs * grad_probs, axis=0, keepdims=True)
                 delta = part if delta is None else delta + part

time: 169 us -> 170 us (level)
  no operation moved by 1% of the time
where the time goes in v7:
time: 170 us; the launch traced here: 168 us
  Pallas kernels  168 us (99%)
    pallas_call x1, Pallas kernels, per_device_fast(): pl.pallas_call(layer_kernel, out_shape=(pltpu.VMEM((ROWS, WIDTH), BF), pl...  163 us
    pallas_call x1, Pallas kernels, per_device_fast(): pl.pallas_call(widen_kernel, out_shape=(shape((ROWS, WIDTH), BF), shape((...  4.97 us

profile of v7, /device:TPU:0, one launch (start us, length us, event | category | flops | bytes accessed | tf_op | source)
XLA Modules:
  0.0 168.5 jit_solution(2133291341572655638)
XLA Ops:
  0.7 162.6 %shard_map.245 = (bf16[128,1024]{1,0:T(8,128)(2,1)S(1)}, bf16[128,1024]{1,0:T(8,128)(2,1)S(1)}, f32[16,256]{1,0:T(8,128)S(1)}, bf16[8,256,384]{2,1,0:T(8,128)(2,...) custom-call(bf16[128,1024]{1,0:T(8,128)(2,1)} %bitcast.4, ...), custom_call_target="tpu_custom_call" | custom-call | tf_op jit(solution)/shard_map/pallas_call | solution.py:1627
  163.3 5.0 %shard_map.246 = (bf16[128,1024]{1,0:T(8,128)(2,1)}, bf16[128,1024]{1,0:T(8,128)(2,1)}, f32[256,3072]{1,0:T(8,128)}, f32[256,1024]{1,0:T(8,128)}, f32[256,4096]{...) custom-call(bf16[128,1024]{1,0:T(8,128)(2,1)S(1)} %get-tuple-element, ...), custom_call_target="tpu_custom_call" | custom-call | tf_op jit(solution)/shard_map/pallas_call | solution.py:1654
